TPU v7x, 256 devices: a whole 4x4x8 slice. The times are simulated.
256 devices in a mesh: row: 32 (over z_lo, x, y), col: 8 (over z_hi, core).
Axes of the slice: x: 4, y: 4, z: 8 (z_hi: 4, z_lo: 2; z = z_hi * 2 + z_lo), core: 2. Of those that a mesh axis runs over, the one named last changes fastest.
Arguments:
- grad_out: bfloat16 [64, 512, 2048], P(None, 'row', 'col'), may hold values from -6 to 6
- row_feat: bfloat16 [512, 64], P('row'), may hold values from -6 to 6
- col_feat: bfloat16 [2048, 64], P('col'), may hold values from -6 to 6
- conv_one: bfloat16 [3, 3, 64, 64], replicated, may hold values from -0.25 to 0.25
- bias_one: float32 [64], replicated, may hold values from -3 to 3
- conv_two: bfloat16 [3, 3, 64, 64], replicated, may hold values from -0.25 to 0.25
Outputs:
- row_grad: float32 [512, 64], P('row')
- col_grad: float32 [2048, 64], P('col')
- grad_conv_one: float32 [3, 3, 64, 64], replicated
- grad_bias: float32 [64], replicated
- grad_conv_two: float32 [3, 3, 64, 64], replicated
All inputs are finite; a program needn't handle non-finite values.
Results may differ from a plain program's by a relative error of at most 0.0065.
Values may be sent and summed in bfloat16 or wider, within the bound.
No kernel may reach another device: no remote copies, remote signals or barrier semaphores. Data moves between devices by JAX's collectives and lax.ppermute only.
A program may use at most 128 MiB of HBM per device.

v0:
```python
import math

import jax
import jax.numpy as jnp
from jax import lax
from jax.sharding import PartitionSpec as P


def extended(block, sides, width):
    for axis, dim in sides:
        count = lax.axis_size(axis)
        forward = [(i, i + 1) for i in range(count - 1)]
        backward = [(target, source) for source, target in forward]
        low = lax.ppermute(
            lax.slice_in_dim(block, block.shape[dim] - width, None, axis=dim), axis, forward
        )
        high = lax.ppermute(lax.slice_in_dim(block, 0, width, axis=dim), axis, backward)
        block = jnp.concatenate([low, block, high], axis=dim)
    return block


def conv_valid(kernel, field):
    result = lax.conv_general_dilated(
        field[None],
        kernel,
        (1, 1),
        "VALID",
        rhs_dilation=(8, 8),
        dimension_numbers=("NCHW", "HWOI", "NCHW"),
        preferred_element_type=jnp.float32,
    )
    return result[0]


def flipped(kernel):
    return jnp.transpose(kernel[::-1, ::-1], (0, 1, 3, 2))


def tap_grads(upper, field, base_r, base_c, rows, cols):
    taps = []
    for tap_r in range(3):
        line = []
        for tap_c in range(3):
            top = base_r + 8 * (tap_r - 1)
            left = base_c + 8 * (tap_c - 1)
            piece = field[:, top : top + rows, left : left + cols]
            line.append(
                lax.dot_general(
                    upper, piece, (((1, 2), (1, 2)), ((), ())), preferred_element_type=jnp.float32
                )
            )
        taps.append(jnp.stack(line))
    return jnp.stack(taps)


def slope(pre):
    sig = jax.nn.sigmoid(pre)
    return sig * (1.0 + pre * (1.0 - sig))


def inside_mask(row_first, col_first, margin, tile_rows, tile_cols, total_rows, total_cols):
    global_rows = row_first + jnp.arange(tile_rows + 2 * margin, dtype=jnp.int32) - margin
    global_cols = col_first + jnp.arange(tile_cols + 2 * margin, dtype=jnp.int32) - margin
    return ((global_rows >= 0) & (global_rows < total_rows))[:, None] & (
        (global_cols >= 0) & (global_cols < total_cols)
    )[None, :]


def shards(grad_out, row_feat, col_feat, conv_one, bias_one, conv_two):
    chans, tile_rows, tile_cols = grad_out.shape
    total_rows = tile_rows * lax.axis_size("row")
    total_cols = tile_cols * lax.axis_size("col")
    row_first = lax.axis_index("row") * tile_rows
    col_first = lax.axis_index("col") * tile_cols
    row_ext = extended(row_feat, (("row", 0),), 16)
    col_ext = extended(col_feat, (("col", 0),), 16)
    outer = inside_mask(row_first, col_first, 16, tile_rows, tile_cols, total_rows, total_cols)
    summed = row_ext.T.astype(jnp.float32)[:, :, None] + col_ext.T.astype(jnp.float32)[:, None, :]
    field = jnp.where(outer[None], summed, 0.0).astype(jnp.bfloat16)
    pre = conv_valid(conv_one, field) + bias_one[:, None, None]
    inside = inside_mask(row_first, col_first, 8, tile_rows, tile_cols, total_rows, total_cols)
    act = jnp.where(inside[None], jax.nn.silu(pre), 0.0).astype(jnp.bfloat16)
    grad_ext = extended(grad_out, (("row", 1), ("col", 2)), 16)
    back = conv_valid(flipped(conv_two), grad_ext)
    inner = jnp.where(inside[None], back * slope(pre), 0.0).astype(jnp.bfloat16)
    spread = conv_valid(flipped(conv_one), inner)
    inner_tile = inner[:, 8 : 8 + tile_rows, 8 : 8 + tile_cols]
    grad_in = grad_out.astype(jnp.float32) + spread
    row_part = jnp.sum(grad_in, axis=2).T
    col_part = jnp.sum(grad_in, axis=1).T
    grad_one = tap_grads(inner_tile, field, 16, 16, tile_rows, tile_cols)
    grad_two = tap_grads(grad_out, act, 8, 8, tile_rows, tile_cols)
    bias_part = jnp.sum(inner_tile.astype(jnp.float32), axis=(1, 2))
    row_grad = lax.psum(row_part, "col") / math.sqrt(total_cols)
    col_grad = lax.psum(col_part, "row") / math.sqrt(total_rows)
    sum_one, sum_bias, sum_two = lax.psum((grad_one, bias_part, grad_two), ("row", "col"))
    whole = math.sqrt(total_rows * total_cols)
    return (row_grad, col_grad, sum_one / whole, sum_bias / whole, sum_two / whole)


def solution(mesh):
    in_specs = (P(None, "row", "col"), P("row", None), P("col", None), P(), P(), P())
    out_specs = (P("row", None), P("col", None), P(), P(), P())
    return jax.shard_map(shards, mesh=mesh, in_specs=in_specs, out_specs=out_specs, check_vma=False)
```

profile of v0, /device:TPU:1, one launch (start us, length us, event | category | flops | bytes accessed | tf_op | source)
XLA Modules:
  0.0 769.2 jit_solution(11806747635135335982)
XLA Ops:
  7.2 4.2 collective-permute-start.4
  13.5 5.7 collective-permute-start.6
  19.3 1.9 collective-permute-start.7
  21.2 5.1 collective-permute-start
  26.5 3.6 copy.67
  33.4 2.7 select_convert_fusion
  36.1 2.3 copy.77
  39.3 5.9 broadcast_select_fusion
  45.2 2.7 copy.84
  47.9 2.6 slice.105
  50.5 6.2 copy.124
  56.7 3.2 select_convert_fusion.2
  63.5 2.3 select_convert_fusion.1
  66.5 3.8 add_divide_fusion
  70.3 3.5 copy.69
  73.8 3.6 copy.71
  78.7 4.8 collective-permute-start.2
  83.5 1.9 collective-permute-start.3
  86.2 5.2 collective-permute-done.3
  91.4 5.1 pad_maximum_fusion
  96.5 2.3 copy.73
  99.4 6.2 multiply_multiply_fusion
  105.5 2.7 copy.82
  108.3 2.5 slice.104
  110.8 6.1 copy.123
  116.9 3.8 convert_reduce_fusion
  124.1 86.2 %psum.38 = f32[64]{0:T(128)S(1)} all-reduce(f32[64]{0:T(128)S(1)} %get-tuple-element.14), channel_id=1, replica_groups=mesh['row'=32,'col'=8] {'row','col'}, use_global_device_ids=true, to_apply=%region_6.7 | all-reduce | flops 64 | bytes 512 | tf_op jit(solution)/shard_map/psum | solution.py:96
  211.6 2.2 fusion.17
  215.7 2.0 fusion.33
  220.4 14.5 %psum.35 = f32[16,64]{1,0:T(8,128)S(1)} all-reduce(f32[16,64]{1,0:T(8,128)S(1)} %bitcast.166), channel_id=1, replica_groups=mesh['row'=32,'col'=8] {'col'}, use_global_device_ids=true, to_apply=%region_1.2 | all-reduce | flops 1024 | bytes 8192 | tf_op jit(solution)/shard_map/psum | solution.py:94
  236.3 250.7 %all-reduce.4.cloned.1.call-done = f32[256,64]{1,0:T(8,128)} async-done(((f32[256,64]{1,0:T(8,128)}), f32[256,64]{1,0:T(8,128)}) %all-reduce.4.cloned.1.call-update) | async-done | bytes 65552 | tf_op jit(solution)/shard_map/psum | solution.py:95
  488.6 270.1 %all-reduce.6.cloned.1.call-done = (f32[3,3,64,64]{3,2,1,0:T(8,128)}, f32[3,3,64,64]{3,2,1,0:T(8,128)}) async-done(((f32[3,3,64,64]{3,2,1,0:T(8,128)}, f32[3,3,64,64]{3,2,1,0:T(8,128)}), (f32[3,3,64,64]{3,2,1,0:T(8,128)}, f32[3,3,64,64]{3,2,1,0:T(8,128)})) %all-reduce.6.cloned.1.call-update) | async-done | bytes 294928 | tf_op jit(solution)/shard_map/psum | solution.py:96
  (101 shorter events, 28.7 us)
Async XLA Ops:
  7.2 92.2 %copy-start = (bf16[3,3,64,64]{3,2,1,0:T(8,128)(2,1)S(1)}, bf16[3,3,64,64]{3,2,1,0:T(8,128)(2,1)}, u32[]{:S(2)}) copy-start(bf16[3,3,64,64]{3,2,1,0:T(8,128)(2,1)} %param.11) | copy-start | bytes 221188
  7.2 479.8 %all-reduce.4.cloned.1.call-start = ((), (), s32[]{:S(2)}) async-start(), calls=%async_computation | async-start | bytes 262144 | tf_op jit(solution)/shard_map/psum | solution.py:95
  7.2 25.5 %collective-permute-start.4 = (bf16[16,64]{1,0:T(8,128)(2,1)}, bf16[16,64]{1,0:T(8,128)(2,1)S(1)}, u32[]{:S(2)}, u32[]{:S(2)}) collective-permute-start(bf16[16,64]{1,0:T(8,128)(2,1)} %param.7), channel_id=1, source_target_pairs={{0,8},{8,16},{16,24},{24,32},{32,40},{40,48},{48,56},{56,64},{64,7... | collective-permute-start | bytes 6152 | tf_op jit(solution)/shard_map/ppermute | solution.py:14
  11.4 21.3 %collective-permute-start.5 = (bf16[16,64]{1,0:T(8,128)(2,1)}, bf16[16,64]{1,0:T(8,128)(2,1)S(1)}, u32[]{:S(2)}, u32[]{:S(2)}) collective-permute-start(bf16[16,64]{1,0:T(8,128)(2,1)} %param.7), channel_id=1, source_target_pairs={{8,0},{16,8},{24,16},{32,24},{40,32},{48,40},{56,48},{64,56},{72,6... | collective-permute-start | bytes 6152 | tf_op jit(solution)/shard_map/ppermute | solution.py:17
  13.5 16.9 %collective-permute-start.6 = (bf16[16,64]{0,1:T(8,128)(2,1)S(1)}, bf16[16,64]{0,1:T(8,128)(2,1)S(1)}, u32[]{:S(2)}, u32[]{:S(2)}) collective-permute-start(bf16[16,64]{0,1:T(8,128)(2,1)S(1)} %get-tuple-element.22), channel_id=1, source_target_pairs={{0,1},{1,2},{2,3},{3,4},{4,5},{5,6},{6,7},{8,9},{9,10},{10,11},{11... | collective-permute-start | bytes 6152 | tf_op jit(solution)/shard_map/ppermute | solution.py:14
  19.3 12.5 %collective-permute-start.7 = (bf16[16,64]{0,1:T(8,128)(2,1)S(1)}, bf16[16,64]{0,1:T(8,128)(2,1)S(1)}, u32[]{:S(2)}, u32[]{:S(2)}) collective-permute-start(bf16[16,64]{0,1:T(8,128)(2,1)S(1)} %get-tuple-element.23), channel_id=1, source_target_pairs={{1,0},{2,1},{3,2},{4,3},{5,4},{6,5},{7,6},{9,8},{10,9},{11,10},{12... | collective-permute-start | bytes 6152 | tf_op jit(solution)/shard_map/ppermute | solution.py:17
  21.2 49.1 %collective-permute-start = (bf16[64,16,256]{2,1,0:T(8,128)(2,1)}, bf16[64,16,256]{2,1,0:T(8,128)(2,1)}, u32[]{:S(2)}, u32[]{:S(2)}) collective-permute-start(bf16[64,16,256]{2,1,0:T(8,128)(2,1)} %param.6), channel_id=1, source_target_pairs={{0,8},{8,16},{16,24},{24,32},{32,40},{40,48},{48,56},{56,64},{64,7... | collective-permute-start | bytes 1572872 | tf_op jit(solution)/shard_map/ppermute | solution.py:14
  30.4 43.4 %collective-permute-start.1 = (bf16[64,16,256]{2,1,0:T(8,128)(2,1)}, bf16[64,16,256]{2,1,0:T(8,128)(2,1)}, u32[]{:S(2)}, u32[]{:S(2)}) collective-permute-start(bf16[64,16,256]{2,1,0:T(8,128)(2,1)} %param.6), channel_id=1, source_target_pairs={{8,0},{16,8},{24,16},{32,24},{40,32},{48,40},{56,48},{64,56},{72,6... | collective-permute-start | bytes 1572872 | tf_op jit(solution)/shard_map/ppermute | solution.py:17
  38.4 0.9 copy-start.12
  38.4 0.9 copy-start.15
  45.2 2.8 copy-start.6
  50.5 6.2 copy-start.11
  56.7 3.2 copy-start.9
  77.4 8.0 %copy-start.10 = (f32[1,3,64,64]{3,2,1,0:T(8,128)S(1)}, f32[1,3,64,64]{3,2,1,0:T(8,128)}, u32[]{:S(2)}) copy-start(f32[1,3,64,64]{3,2,1,0:T(8,128)} %get-tuple-element.29) | copy-start | bytes 147460
  77.4 14.0 %copy-start.2 = (bf16[64,16,256]{0,1,2:T(8,128)(2,1)S(1)}, bf16[64,16,256]{0,1,2:T(8,128)(2,1)}, u32[]{:S(2)}) copy-start(bf16[64,16,256]{0,1,2:T(8,128)(2,1)} %copy.67) | copy-start | bytes 1572868
  77.4 14.0 %copy-start.4 = (bf16[64,16,256]{0,1,2:T(8,128)(2,1)S(1)}, bf16[64,16,256]{0,1,2:T(8,128)(2,1)}, u32[]{:S(2)}) copy-start(bf16[64,16,256]{0,1,2:T(8,128)(2,1)} %copy.69) | copy-start | bytes 1572868
  77.4 14.0 %copy-start.5 = (bf16[64,16,256]{0,1,2:T(8,128)(2,1)S(1)}, bf16[64,16,256]{0,1,2:T(8,128)(2,1)}, u32[]{:S(2)}) copy-start(bf16[64,16,256]{0,1,2:T(8,128)(2,1)} %copy.71) | copy-start | bytes 1572868
  78.7 7.5 collective-permute-start.2
  83.5 7.9 %collective-permute-start.3 = (bf16[64,48,16]{0,1,2:T(8,128)(2,1)S(1)}, bf16[64,48,16]{0,1,2:T(8,128)(2,1)S(1)}, u32[]{:S(2)}, u32[]{:S(2)}) collective-permute-start(bf16[64,48,16]{0,1,2:T(8,128)(2,1)S(1)} %get-tuple-element.21), channel_id=1, source_target_pairs={{1,0},{2,1},{3,2},{4,3},{5,4},{6,5},{7,6},{9,8},{10,9},{11,10},{12... | collective-permute-start | bytes 294920 | tf_op jit(solution)/shard_map/ppermute | solution.py:17
  91.4 7.9 %slice-start = ((s8[4718592]{0:T(1024)(128)(4,1)}), s8[4194304]{0:T(1024)(128)(4,1)S(1)}, s32[]{:S(2)}) async-start(s8[4718592]{0:T(1024)(128)(4,1)} %bitcast.163), calls=%async_computation.2 | async-start | bytes 8388608
  96.5 2.8 slice-start.1
  116.9 3.8 copy-start.7
  121.8 88.9 %copy-start.8 = (bf16[32,8,36,64]{3,1,2,0:T(8,128)(2,1)S(1)}, bf16[32,8,36,64]{3,1,2,0:T(8,128)(2,1)}, u32[]{:S(2)}) copy-start(bf16[32,8,36,64]{3,1,2,0:T(8,128)(2,1)} %get-tuple-element.24) | copy-start | bytes 3538948
  213.9 1.8 copy-start.13
  213.9 1.8 copy-start.14
  217.7 1.2 copy-start.3
  218.5 543.7 %copy-start.1 = (bf16[3,3,64,64]{3,2,1,0:T(8,128)(2,1)S(1)}, bf16[3,3,64,64]{3,2,1,0:T(8,128)(2,1)}, u32[]{:S(2)}) copy-start(bf16[3,3,64,64]{3,2,1,0:T(8,128)(2,1)} %param.11) | copy-start | bytes 221188
  220.4 538.3 %all-reduce.6.cloned.1.call-start = ((), (), s32[]{:S(2)}) async-start(), calls=%async_computation.1 | async-start | bytes 1179648 | tf_op jit(solution)/shard_map/psum | solution.py:96
Sparse Core Ops, SparseCore 0:
  220.5 266.4 all-reduce.3
  494.1 264.5 all-reduce.5
where the time goes:
time: 772 us; the launch traced here: 769 us
  waiting for transfers between devices  526 us (68%)
  blocking collectives  101 us (13%)
  local copies, waits for them, and re-layouts  45.4 us (6%)
  other arithmetic  35.1 us (5%)
  starting transfers between devices  26.3 us (3%)
  matrix products  20.9 us (3%)
  between operations  14.8 us (2%)
    psum x1, waiting for transfers between devices, shards(): lax.psum((grad_one, bias_part, grad_two), ('row', 'col'))  270 us
    psum x1, waiting for transfers between devices, shards(): col_grad = lax.psum(col_part, 'row') / math.sqrt(total_rows)  251 us
    psum x1, blocking collectives, shards(): lax.psum((grad_one, bias_part, grad_two), ('row', 'col'))  86.2 us
    ppermute x4, starting transfers between devices, extended(): lax.ppermute(lax.slice_in_dim(block, block.shape[dim] - width, None, axis...  19.8 us
    conv_general_dilated x11, local copies, waits for them, and re-layouts, conv_valid(): lax.conv_general_dilated(field[None], kernel, (1, 1), 'VALID', rhs_dilati...  18.6 us
    unnamed x40, local copies, waits for them, and re-layouts  17.6 us
  transfers between devices with their start and end apart: 10, of which 3 were waited for; matrix products, arithmetic and copies ran while one was open for 7% of the time, Pallas kernels for 0%

commit v1 on v0

v1 whole, which is shorter than its diff:
```python
import math

import jax
import jax.numpy as jnp
from jax import lax
from jax.experimental import pallas as pl
from jax.experimental.pallas import tpu as pltpu
from jax.sharding import PartitionSpec as P

F32, BF16 = jnp.float32, jnp.bfloat16
NN = (((1,), (0,)), ((), ()))
NT = (((1,), (1,)), ((), ()))
TN = (((0,), (0,)), ((), ()))
CH = 64
LANES = 128


def dot(x, y, dims):
    return lax.dot_general(x, y, dims, preferred_element_type=F32)


def dot_exact(x, y, dims):
    return lax.dot_general(
        x.astype(F32), y.astype(F32), dims, precision=lax.Precision.HIGHEST, preferred_element_type=F32
    )


def chunk_rows(n_row):
    weights, chans = 9 * CH // n_row, CH // n_row
    return weights, chans, weights + 3 * chans


def pack_kernel(grad_ref, row_ref, col_ref, out_ref, rows_scr):
    rows_scr[...] = grad_ref[:, :, :LANES].astype(F32).reshape(CH * 16, LANES)
    lane = lax.broadcasted_iota(jnp.int32, (CH, LANES), 1)
    for half in range(2):
        packed = jnp.zeros((CH, LANES), F32)
        for k in range(8):
            strip = rows_scr[pl.ds(half * 8 + k, CH, stride=16), :]
            if k:
                strip = pltpu.roll(strip, 16 * k, 1)
            packed = jnp.where((lane >= 16 * k) & (lane < 16 * k + 16), strip, packed)
        out_ref[half * CH : (half + 1) * CH, :] = packed.astype(BF16)
    out_ref[2 * CH :, :] = jnp.concatenate(
        [row_ref[...].astype(F32), col_ref[:16, :].astype(F32)], axis=1
    ).astype(BF16)


def main_kernel(
    n_row, n_col, grad_ref, next_ref, right_ref, diag_ref, row_ref, col_ref, w2_ref, k1c_ref, k1ct_ref, k1f_ref,
    bias_ref, out_ref, own_ref, rows_scr, x_scr, act_scr, inner_scr, ind_scr, back_scr, pre_scr, w_scr,
):
    cols = grad_ref.shape[2]
    seam = jnp.where(lax.axis_index("row") == n_row - 1, 0.0, 1.0).astype(F32)
    last_col = lax.axis_index("col") == n_col - 1

    def lane_of(shape):
        return lax.broadcasted_iota(jnp.int32, shape, 1) % cols

    def valid(lane, tap):
        if tap == 1:
            return jnp.ones(lane.shape, jnp.bool_)
        if tap == 0:
            crossing = lane >= cols - 8
        else:
            crossing = (lane >= cols - 16) & (lane < cols - 8)
        return jnp.logical_not(crossing & last_col)

    lane = lane_of((CH, cols))
    keep_low, keep_high = valid(lane, 0), valid(lane, 2)
    col_sum = jnp.zeros((CH, cols), F32)
    for side, (tile_ref, strip_ref) in enumerate(((grad_ref, right_ref), (next_ref, diag_ref))):
        for piece in range(cols // LANES):
            wide = tile_ref[:, :, LANES * piece : LANES * (piece + 1)]
            rows_scr[piece] = wide.astype(F32).reshape(CH * 16, LANES)
        for half in range(2):
            strip = strip_ref[half * CH : (half + 1) * CH, :].astype(F32)
            blk = 2 * side + half
            for k in range(8):
                line = jnp.concatenate(
                    [rows_scr[p, pl.ds(half * 8 + k, CH, stride=16), :] for p in range(cols // LANES)], axis=1
                )
                if side == 0:
                    col_sum = col_sum + line
                edge = pltpu.roll(strip, LANES - 16 * k, 1) if k else strip
                wide = jnp.concatenate([line, edge], axis=1)
                shift_one = pltpu.roll(wide, cols + LANES - 8, 1)[:, :cols]
                shift_two = pltpu.roll(wide, cols + LANES - 16, 1)[:, :cols]
                rows, span = slice(blk * CH, (blk + 1) * CH), slice(k * cols, (k + 1) * cols)
                x_scr[2, rows, span] = jnp.where(keep_low, line, 0.0).astype(BF16)
                x_scr[1, rows, span] = shift_one.astype(BF16)
                x_scr[0, rows, span] = jnp.where(keep_high, shift_two, 0.0).astype(BF16)

    row_ext = jnp.concatenate([row_ref[...], diag_ref[2 * CH :, :CH]], axis=0).astype(F32)
    col_ext = jnp.concatenate([col_ref[...], diag_ref[2 * CH :, CH:]], axis=0).astype(F32)
    blocks = [row_ext[8 * k : 8 * k + 8, :] for k in range(4)]
    row_cat = jnp.concatenate(
        [
            jnp.concatenate([blocks[0], blocks[1], blocks[2] * seam], axis=1),
            jnp.concatenate([blocks[1] * seam, blocks[2], blocks[3]], axis=1),
        ],
        axis=0,
    )
    place = lax.broadcasted_iota(jnp.int32, (cols, CH), 0)
    col_cat = jnp.concatenate(
        [jnp.where(valid(place, tap), col_ext[8 * tap : 8 * tap + cols, :], 0.0) for tap in range(3)], axis=1
    ).astype(BF16)
    col_terms = dot(k1c_ref[...], col_cat, NT)
    low, mid, high = (col_terms[CH * a : CH * (a + 1)] for a in range(3))
    bias = bias_ref[...]
    col_part = jnp.concatenate([low + mid + seam * high + bias, seam * low + mid + high + bias], axis=0)
    row_terms = dot(k1f_ref[...], row_cat.astype(BF16), NT)
    row_part = jnp.concatenate(
        [
            jnp.concatenate([row_terms[CH * b : CH * (b + 1), 8 * rb : 8 * rb + 8] for b in range(3)], axis=1)
            for rb in range(2)
        ],
        axis=0,
    )

    ind_lane = lax.broadcasted_iota(jnp.int32, (8, 8 * cols), 1)
    ind_row = lax.broadcasted_iota(jnp.int32, (8, 8 * cols), 0)
    for tap in range(3):
        hit = (ind_lane // cols == ind_row) & valid(ind_lane % cols, tap)
        ind_scr[8 * tap : 8 * tap + 8, :] = jnp.where(hit, 1.0, 0.0)
    indicator = ind_scr[...]
    pre_scr[...] = dot_exact(row_part, indicator, NN)
    x_all = x_scr[...].reshape(3 * 4 * CH, 8 * cols)
    back_scr[...] = dot(w2_ref[...], x_all, NN)

    inner_sum = jnp.zeros((2 * CH, cols), F32)
    for k in range(8):
        span = slice(k * cols, (k + 1) * cols)
        pre = pre_scr[:, span] + col_part
        sig = 1.0 / (1.0 + jnp.exp(-pre))
        act_scr[:, span] = (pre * sig).astype(BF16)
        inner = (back_scr[:, span] * (sig * (1.0 + pre * (1.0 - sig)))).astype(BF16)
        inner_scr[:, span] = inner
        inner_sum = inner_sum + inner.astype(F32)

    full = dot(x_all, act_scr[...], NT)
    both = jnp.concatenate([inner_scr[...], x_scr[1, : 2 * CH, :]], axis=0)
    sums = dot(indicator.astype(BF16), both, NT)
    row_sums = jnp.concatenate(
        [
            jnp.concatenate([sums[8 * b : 8 * b + 8, CH * rb : CH * (rb + 1)] for b in range(3)], axis=1)
            for rb in range(2)
        ],
        axis=0,
    )
    grad_rows = sums[8:16, 2 * CH :]
    spread_row = dot_exact(row_sums, k1f_ref[...], NN)

    def part(rb, a):
        return spread_row[8 * rb : 8 * rb + 8, CH * a : CH * (a + 1)]

    own_ref[...] = grad_rows + jnp.concatenate([part(0, 0), part(0, 1) + seam * part(1, 0)], axis=1)
    beyond = jnp.concatenate([seam * part(0, 2) + part(1, 1), part(1, 2)], axis=1)
    first, second = inner_sum[:CH], inner_sum[CH:]
    col_sums = jnp.concatenate([first + seam * second, first + second, seam * first + second], axis=0)
    spread_col = dot_exact(k1ct_ref[...], col_sums, NN)
    nothing = jnp.zeros((CH, LANES), F32)
    total = jnp.concatenate([col_sum, nothing], axis=1)
    for tap in range(3):
        piece = jnp.where(valid(lane, tap), spread_col[CH * tap : CH * (tap + 1)], 0.0)
        piece = jnp.concatenate([piece, nothing], axis=1)
        total = total + (pltpu.roll(piece, 8 * tap, 1) if tap else piece)
    one_row = dot_exact(row_sums, row_cat, TN)
    one_col = dot_exact(col_sums, col_cat, NN)
    gap = jnp.zeros((32, cols), F32)
    bias_row = dot_exact(jnp.ones((8, cols), F32), jnp.concatenate([gap, first + second, gap], axis=0), NT)
    for a in range(3):
        for b in range(3):
            one = one_row[CH * b : CH * (b + 1), CH * a : CH * (a + 1)]
            one = one + one_col[CH * a : CH * (a + 1), CH * b : CH * (b + 1)]
            at = [CH * (4 * b + rb + 2 - a) for rb in range(2)]
            zero, unit = full[at[0] : at[0] + CH, :CH], full[at[1] : at[1] + CH, CH:]
            if a == 0:
                zero = zero * seam
            if a == 2:
                unit = unit * seam
            w_scr[CH * (3 * a + b) : CH * (3 * a + b + 1), :] = jnp.concatenate([one, zero + unit], axis=1)

    weights, chans, sums_end = chunk_rows(n_row)
    tail = total[:, cols:] + bias_row[:1, :]
    for j in range(n_row):
        out_ref[j, :weights, :] = w_scr[weights * j : weights * (j + 1), :]
        mine = slice(chans * j, chans * (j + 1))
        out_ref[j, weights : weights + chans, :] = total[mine, :LANES]
        out_ref[j, weights + chans : weights + 2 * chans, :] = total[mine, LANES:cols]
        out_ref[j, weights + 2 * chans : sums_end, :] = tail[mine]
        out_ref[j, sums_end:, :] = beyond


def row_sum_kernel(n_row, n_col, got_ref, own_ref, out_ref):
    sums_end = chunk_rows(n_row)[2]
    before = lax.rem(lax.axis_index("row") + n_row - 1, n_row)
    total = got_ref[0, :sums_end, :]
    for j in range(1, n_row):
        total = total + got_ref[j, :sums_end, :]
    rows = own_ref[...] + got_ref[before, sums_end:, :]
    for k in range(n_col):
        out_ref[k, :sums_end, :] = total
        out_ref[k, sums_end:, :] = rows


def col_sum_kernel(n_row, n_col, cols, got_ref, row_ref, bias_ref, out_ref):
    weights, chans, sums_end = chunk_rows(n_row)
    me = lax.axis_index("col")
    before = lax.rem(me + n_col - 1, n_col)
    whole = math.sqrt(16 * n_row * cols * n_col)
    total = got_ref[0]
    for k in range(1, n_col):
        total = total + got_ref[k]
    rows = total[sums_end:, :] * (1.0 / math.sqrt(cols * n_col))
    row_ref[0:8, :] = rows[:, :CH]
    row_ref[8:16, :] = rows[:, CH:]
    bias_ref[...] = total[sums_end - 1 : sums_end, 32 : 32 + CH] * (1.0 / whole)
    scale = 1.0 / math.sqrt(16 * n_row)
    edge = got_ref[before, weights + 2 * chans : sums_end, :]
    edge = jnp.where(lax.broadcasted_iota(jnp.int32, edge.shape, 1) < 16, edge, 0.0)
    low = (got_ref[me, weights : weights + chans, :] + edge) * scale
    high = got_ref[me, weights + chans : weights + 2 * chans, :] * scale
    share = total[:weights, :] * (1.0 / whole)
    for j in range(n_row):
        out_ref[j, :weights, :] = share
        out_ref[j, weights : weights + chans, :] = low
        out_ref[j, weights + chans : weights + 2 * chans, :] = high
        if weights + 2 * chans < out_ref.shape[1]:
            out_ref[j, weights + 2 * chans :, :] = jnp.zeros((out_ref.shape[1] - weights - 2 * chans, LANES), F32)


def spread_kernel(n_row, got_ref, col_ref, one_ref, two_ref, col_scr):
    weights, chans, _ = chunk_rows(n_row)
    for j in range(n_row):
        share = got_ref[j, :weights, :]
        one_ref[weights * j : weights * (j + 1), :] = share[:, :CH]
        two_ref[weights * j : weights * (j + 1), :] = share[:, CH:]
        col_scr[chans * j : chans * (j + 1), :LANES] = got_ref[j, weights : weights + chans, :]
        col_scr[chans * j : chans * (j + 1), LANES:] = got_ref[j, weights + chans : weights + 2 * chans, :]
    col_ref[...] = col_scr[...].T


PARAMS = pltpu.CompilerParams(vmem_limit_bytes=48 * 1024 * 1024)


def sds(shape, dtype=F32):
    return jax.ShapeDtypeStruct(shape, dtype)


def shards(n_row, n_col, grad_out, row_feat, col_feat, conv_one, bias_one, conv_two):
    cols = grad_out.shape[2]
    weights, chans, sums_end = chunk_rows(n_row)
    nxt = lax.ppermute(grad_out, "row", [(k, (k - 1) % n_row) for k in range(n_row)])
    strip = pl.pallas_call(
        pack_kernel,
        out_shape=sds((2 * CH + 16, LANES), BF16),
        scratch_shapes=[pltpu.VMEM((CH * 16, LANES), F32)],
        compiler_params=PARAMS,
    )(grad_out, row_feat, col_feat)
    right = lax.ppermute(strip, "col", [(k, (k - 1) % n_col) for k in range(n_col)])
    pairs = [
        (r * n_col + c, (r - 1) % n_row * n_col + (c - 1) % n_col) for r in range(n_row) for c in range(n_col)
    ]
    diag = lax.ppermute(strip, ("row", "col"), pairs)

    is_last = lax.axis_index("row") == n_row - 1
    turned = jnp.transpose(conv_two[::-1], (3, 1, 0, 2))
    zero = jnp.where(is_last, turned.at[:, :, 2].set(0), turned)
    unit = jnp.where(is_last, turned.at[:, :, 0].set(0), turned)
    gap = ((0, 0), (0, 0))
    w2 = jnp.concatenate(
        [jnp.pad(zero, gap + ((0, 1), (0, 0))), jnp.pad(unit, gap + ((1, 0), (0, 0)))], axis=0
    ).reshape(2 * CH, 12 * CH)
    k1c = jnp.transpose(conv_one, (0, 2, 1, 3)).reshape(3 * CH, 3 * CH)
    k1f = jnp.transpose(conv_one, (1, 2, 0, 3)).reshape(3 * CH, 3 * CH)

    chunks, own = pl.pallas_call(
        lambda *refs: main_kernel(n_row, n_col, *refs),
        out_shape=(sds((n_row, sums_end + 8, LANES)), sds((8, LANES))),
        scratch_shapes=[
            pltpu.VMEM((cols // LANES, CH * 16, LANES), F32),
            pltpu.VMEM((3, 4 * CH, 8 * cols), BF16),
            pltpu.VMEM((2 * CH, 8 * cols), BF16),
            pltpu.VMEM((2 * CH, 8 * cols), BF16),
            pltpu.VMEM((24, 8 * cols), F32),
            pltpu.VMEM((2 * CH, 8 * cols), F32),
            pltpu.VMEM((2 * CH, 8 * cols), F32),
            pltpu.VMEM((9 * CH, LANES), F32),
        ],
        compiler_params=PARAMS,
    )(grad_out, nxt, right, diag, row_feat, col_feat, w2, k1c, k1c.T, k1f, bias_one[:, None])
    got = lax.all_to_all(chunks, "row", 0, 0)
    copies = pl.pallas_call(
        lambda *refs: row_sum_kernel(n_row, n_col, *refs),
        out_shape=sds((n_col, sums_end + 8, LANES)),
        compiler_params=PARAMS,
    )(got, own)
    got = lax.all_to_all(copies, "col", 0, 0)
    end = -(-(weights + 2 * chans) // 8) * 8
    row_grad, bias_grad, copies = pl.pallas_call(
        lambda *refs: col_sum_kernel(n_row, n_col, cols, *refs),
        out_shape=(sds((16, CH)), sds((1, CH)), sds((n_row, end, LANES))),
        compiler_params=PARAMS,
    )(got)
    got = lax.all_to_all(copies, "row", 0, 0)
    col_grad, one, two = pl.pallas_call(
        lambda *refs: spread_kernel(n_row, *refs),
        out_shape=(sds((cols, CH)), sds((9 * CH, CH)), sds((9 * CH, CH))),
        scratch_shapes=[pltpu.VMEM((CH, cols), F32)],
        compiler_params=PARAMS,
    )(got)
    shape = conv_one.shape
    return row_grad, col_grad, one.reshape(shape), bias_grad[0], two.reshape(shape)


def solution(mesh):
    in_specs = (P(None, "row", "col"), P("row", None), P("col", None), P(), P(), P())
    out_specs = (P("row", None), P("col", None), P(), P(), P())
    n_row, n_col = mesh.shape["row"], mesh.shape["col"]
    return jax.shard_map(
        lambda *args: shards(n_row, n_col, *args), mesh=mesh, in_specs=in_specs, out_specs=out_specs, check_vma=False
    )
```

time: 772 us -> 80.7 us (0.10)
  waiting for transfers between devices: 526 us -> 8.1 us
  blocking collectives: 101 us -> 44.8 us
  local copies, waits for them, and re-layouts: 45.4 us -> 3.97 us
  other arithmetic: 35.1 us -> 0.17 us
  matrix products: 20.9 us -> 0 us
  between operations: 14.8 us -> 0.75 us
  starting transfers between devices: 26.3 us -> 12.9 us
  Pallas kernels: 0 us -> 9.04 us
    psum x2 -> x0, waiting for transfers between devices: 521 us -> none  [the longest x1 270 us: shards(): lax.psum((grad_one, bias_part, grad_two), ('row', 'col'))]
    psum x2 -> x0, blocking collectives: 101 us -> none  [the longest x1 86.2 us: shards(): lax.psum((grad_one, bias_part, grad_two), ('row', 'col'))]
    all_to_all x0 -> x3, blocking collectives: none -> 44.8 us  [the longest x1 17.4 us: shards(): got = lax.all_to_all(chunks, 'row', 0, 0)]
    conv_general_dilated x11 -> x0, local copies, waits for them, and re-layouts: 18.6 us -> none  [conv_valid(): lax.conv_general_dilated(field[None], kernel, (1, 1), 'VALID', rhs_dilati...]
    unnamed x40 -> x12, local copies, waits for them, and re-layouts: 17.6 us -> 3.03 us
    conv_general_dilated x3 -> x0, matrix products: 14.1 us -> none  [conv_valid(): lax.conv_general_dilated(field[None], kernel, (1, 1), 'VALID', rhs_dilati...]
    ppermute x8 -> x3, starting transfers between devices: 26.2 us -> 12.9 us  [the longest x1 7.75 us: shards(): diag = lax.ppermute(strip, ('row', 'col'), pairs)]
    convert_element_type x6 -> x0, other arithmetic: 12 us -> none  [the longest x2 4.98 us: shards(): field = jnp.where(outer[None], summed, 0.0).astype(jnp.bfloat16)]
  transfers between devices with their start and end apart: 10 -> 3, of which waited for: 3 -> 1; matrix products, arithmetic and copies ran while one was open for 7% -> 1% of each run, Pallas kernels for 0% -> 0%
where the time goes in v1:
time: 80.7 us; the launch traced here: 79.7 us
  blocking collectives  44.8 us (56%)
  starting transfers between devices  12.9 us (16%)
  Pallas kernels  9.04 us (11%)
  waiting for transfers between devices  8.1 us (10%)
  local copies, waits for them, and re-layouts  3.97 us (5%)
    all_to_all x1, blocking collectives, shards(): got = lax.all_to_all(chunks, 'row', 0, 0)  17.4 us
    all_to_all x1, blocking collectives, shards(): got = lax.all_to_all(copies, 'col', 0, 0)  15.1 us
    all_to_all x1, blocking collectives, shards(): got = lax.all_to_all(copies, 'row', 0, 0)  12.3 us
    ppermute x1, waiting for transfers between devices, shards(): lax.ppermute(grad_out, 'row', [(k, (k - 1) % n_row) for k in range(n_row)])  8.09 us
    ppermute x1, starting transfers between devices, shards(): diag = lax.ppermute(strip, ('row', 'col'), pairs)  7.75 us
    pallas_call x1, Pallas kernels, shards(): pl.pallas_call(lambda *refs: main_kernel(n_row, n_col, *refs), out_shape=...  6.09 us
    ppermute x1, starting transfers between devices, shards(): lax.ppermute(strip, 'col', [(k, (k - 1) % n_col) for k in range(n_col)])  3.77 us
    unnamed x12, local copies, waits for them, and re-layouts  3.03 us
  transfers between devices with their start and end apart: 3, of which 1 were waited for; matrix products, arithmetic and copies ran while one was open for 1% of the time, Pallas kernels for 0%

profile of v1, /device:TPU:1, one launch (start us, length us, event | category | flops | bytes accessed | tf_op | source)
XLA Modules:
  0.0 79.7 jit_solution(1744011107455886625)
XLA Ops:
  0.6 0.0 copy-start
  0.6 0.9 %copy.19.col_ref.refs_5_ = bf16[256,64]{1,0:T(8,128)(2,1)S(1)} copy(bf16[256,64]{0,1:T(8,128)(2,1)} %param.12) | data formatting | bytes 65536 | tf_op args[2]
  1.5 0.0 copy-done
  1.5 0.0 copy-start.2
  1.5 1.3 %shard_map.101 = bf16[144,128]{1,0:T(8,128)(2,1)S(1)} custom-call(bf16[64,16,256]{2,1,0:T(8,128)(2,1)} %refs_0_.1, bf16[16,64]{1,0:T(8,128)(2,1)S(1)} %copy-done, bf16[256,64]{1,0:T(8,128)(2,1)S(1)} %copy.19.col_ref.refs_5_), custom_call_target="tpu_custom_call" | custom-call | tf_op jit(solution)/shard_map/pallas_call | solution.py:255
  2.9 7.7 %collective-permute-start.2 = (bf16[144,128]{1,0:T(8,128)(2,1)S(1)}, bf16[144,128]{1,0:T(8,128)(2,1)S(1)}, u32[]{:S(2)}, u32[]{:S(2)}) collective-permute-start(bf16[144,128]{1,0:T(8,128)(2,1)S(1)} %shard_map.101), channel_id=1, source_target_pairs={{0,255},{1,248},{2,249},{3,250},{4,251},{5,252},{6,253},{7,254},{8... | collective-permute-start | bytes 110600 | tf_op jit(solution)/shard_map/ppermute | solution.py:265
  10.6 3.8 %collective-permute-start.1 = (bf16[144,128]{1,0:T(8,128)(2,1)S(1)}, bf16[144,128]{1,0:T(8,128)(2,1)S(1)}, u32[]{:S(2)}, u32[]{:S(2)}) collective-permute-start(bf16[144,128]{1,0:T(8,128)(2,1)S(1)} %shard_map.101), channel_id=1, source_target_pairs={{0,7},{1,0},{2,1},{3,2},{4,3},{5,4},{6,5},{7,6},{8,15},{9,8},{10,9... | collective-permute-start | bytes 110600 | tf_op jit(solution)/shard_map/ppermute | solution.py:261
  14.4 1.4 %collective-permute-start = (bf16[64,16,256]{2,1,0:T(8,128)(2,1)}, bf16[64,16,256]{2,1,0:T(8,128)(2,1)S(1)}, u32[]{:S(2)}, u32[]{:S(2)}) collective-permute-start(bf16[64,16,256]{2,1,0:T(8,128)(2,1)} %refs_0_.1), channel_id=1, source_target_pairs={{0,248},{8,0},{16,8},{24,16},{32,24},{40,32},{48,40},{56,48},{64,5... | collective-permute-start | bytes 1572872 | tf_op jit(solution)/shard_map/ppermute | solution.py:254
  15.7 0.0 copy-done.2
  15.9 0.1 fusion.2
  16.0 0.0 copy-start.3
  16.0 0.6 copy-done.3
  16.6 0.1 copy.28.refs_10_
  16.7 0.0 copy-start.1
  16.7 0.1 copy.27.refs_6_
  16.9 0.8 copy-done.1
  17.7 0.1 copy.23
  17.8 0.2 reshape.88.refs_7_
  17.9 0.1 copy.24
  18.1 0.1 copy.25
  18.2 0.2 reshape.89.refs_9_
  18.4 0.0 collective-permute-done.2.refs_3_
  18.4 0.0 collective-permute-done.1.refs_2_
  18.4 8.1 %collective-permute-done.refs_1_ = bf16[64,16,256]{2,1,0:T(8,128)(2,1)S(1)} collective-permute-done((bf16[64,16,256]{2,1,0:T(8,128)(2,1)}, bf16[64,16,256]{2,1,0:T(8,128)(2,1)S(1)}, u32[]{:S(2)}, u32[]{:S(2)}) %collective-permute-start) | collective-permute-done | bytes 524320 | tf_op jit(solution)/shard_map/ppermute | solution.py:254
  26.5 6.1 %shard_map.102 = (f32[32,32,128]{2,1,0:T(8,128)S(1)}, f32[8,128]{1,0:T(8,128)S(1)}) custom-call(bf16[64,16,256]{2,1,0:T(8,128)(2,1)} %refs_0_.1, bf16[64,16,256]{2,1,0:T(8,128)(2,1)S(1)} %collective-permute-done.refs_1_, bf16[144,128]{1,0:T(8,128)(2,1)S(1)} %collective-permute-done.1.refs_2_, bf16[144,128]{1,0:T(8,128)(2,1)S(1)} %collective-permute-done.2.refs_3_, ...), custom_call_target="tpu_custom_call" | custom-call | tf_op jit(solution)/shard_map/pallas_call | solution.py:278
  32.6 17.4 %all_to_all.15.refs_0_ = f32[32,32,128]{2,1,0:T(8,128)S(1)} all-to-all(f32[32,32,128]{2,1,0:T(8,128)S(1)} %get-tuple-element.37), channel_id=1, replica_groups=mesh['row'=32,'col'=8] {'row'}, dimensions={0} | all-to-all | bytes 1048576 | tf_op jit(solution)/shard_map/all_to_all | solution.py:293
  50.0 15.1 %all_to_all.16.refs_0_ = f32[8,32,128]{2,1,0:T(8,128)S(1)} all-to-all(f32[8,32,128]{2,1,0:T(8,128)S(1)} %shard_map.103), channel_id=1, replica_groups=mesh['row'=32,'col'=8] {'col'}, dimensions={0} | all-to-all | bytes 262144 | tf_op jit(solution)/shard_map/all_to_all | solution.py:299
  65.1 0.7 shard_map.104
  65.7 12.3 %all_to_all.17.refs_0_ = f32[32,24,128]{2,1,0:T(8,128)S(1)} all-to-all(f32[32,24,128]{2,1,0:T(8,128)S(1)} %get-tuple-element.40), channel_id=1, replica_groups=mesh['row'=32,'col'=8] {'row'}, dimensions={0} | all-to-all | bytes 786432 | tf_op jit(solution)/shard_map/all_to_all | solution.py:306
  78.1 0.9 %shard_map.105 = (f32[256,64]{1,0:T(8,128)S(1)}, f32[576,64]{1,0:T(8,128)}, f32[576,64]{1,0:T(8,128)}) custom-call(f32[32,24,128]{2,1,0:T(8,128)S(1)} %all_to_all.17.refs_0_), custom_call_target="tpu_custom_call" | custom-call | tf_op jit(solution)/shard_map/pallas_call | solution.py:307
  79.0 0.7 copy.29
  (6 shorter events, 0.1 us)
Async XLA Ops:
  0.6 0.9 %copy-start = (bf16[16,64]{1,0:T(8,128)(2,1)S(1)}, bf16[16,64]{1,0:T(8,128)(2,1)}, u32[]{:S(2)}) copy-start(bf16[16,64]{1,0:T(8,128)(2,1)} %refs_4_.1) | copy-start | bytes 6148
  1.5 14.2 %copy-start.2 = (bf16[3,3,64,64]{3,2,1,0:T(8,128)(2,1)S(1)}, bf16[3,3,64,64]{3,2,1,0:T(8,128)(2,1)}, u32[]{:S(2)}) copy-start(bf16[3,3,64,64]{3,2,1,0:T(8,128)(2,1)} %param.15) | copy-start | bytes 221188
  2.9 15.5 %collective-permute-start.2 = (bf16[144,128]{1,0:T(8,128)(2,1)S(1)}, bf16[144,128]{1,0:T(8,128)(2,1)S(1)}, u32[]{:S(2)}, u32[]{:S(2)}) collective-permute-start(bf16[144,128]{1,0:T(8,128)(2,1)S(1)} %shard_map.101), channel_id=1, source_target_pairs={{0,255},{1,248},{2,249},{3,250},{4,251},{5,252},{6,253},{7,254},{8... | collective-permute-start | bytes 110600 | tf_op jit(solution)/shard_map/ppermute | solution.py:265
  10.6 7.8 %collective-permute-start.1 = (bf16[144,128]{1,0:T(8,128)(2,1)S(1)}, bf16[144,128]{1,0:T(8,128)(2,1)S(1)}, u32[]{:S(2)}, u32[]{:S(2)}) collective-permute-start(bf16[144,128]{1,0:T(8,128)(2,1)S(1)} %shard_map.101), channel_id=1, source_target_pairs={{0,7},{1,0},{2,1},{3,2},{4,3},{5,4},{6,5},{7,6},{8,15},{9,8},{10,9... | collective-permute-start | bytes 110600 | tf_op jit(solution)/shard_map/ppermute | solution.py:261
  14.4 12.1 %collective-permute-start = (bf16[64,16,256]{2,1,0:T(8,128)(2,1)}, bf16[64,16,256]{2,1,0:T(8,128)(2,1)S(1)}, u32[]{:S(2)}, u32[]{:S(2)}) collective-permute-start(bf16[64,16,256]{2,1,0:T(8,128)(2,1)} %refs_0_.1), channel_id=1, source_target_pairs={{0,248},{8,0},{16,8},{24,16},{32,24},{40,32},{48,40},{56,48},{64,5... | collective-permute-start | bytes 1572872 | tf_op jit(solution)/shard_map/ppermute | solution.py:254
  16.0 0.7 copy-start.3
  16.7 0.9 %copy-start.1 = (bf16[3,3,64,64]{3,2,1,0:T(8,128)(2,1)S(1)}, bf16[3,3,64,64]{3,2,1,0:T(8,128)(2,1)}, u32[]{:S(2)}) copy-start(bf16[3,3,64,64]{3,2,1,0:T(8,128)(2,1)} %param.13) | copy-start | bytes 221188

commit v2 on v1

v2 whole, which is shorter than its diff:
```python
import math

import jax
import jax.numpy as jnp
from jax import lax
from jax.experimental import pallas as pl
from jax.experimental.pallas import tpu as pltpu
from jax.sharding import PartitionSpec as P

F32, BF16 = jnp.float32, jnp.bfloat16
NN = (((1,), (0,)), ((), ()))
NT = (((1,), (1,)), ((), ()))
TN = (((0,), (0,)), ((), ()))
CH = 64
LANES = 128


def dot(x, y, dims):
    return lax.dot_general(x, y, dims, preferred_element_type=F32)


def dot_exact(x, y, dims):
    return lax.dot_general(
        x.astype(F32), y.astype(F32), dims, precision=lax.Precision.HIGHEST, preferred_element_type=F32
    )


def chunk_rows(n_row):
    weights, chans = 9 * CH // n_row, CH // n_row
    return weights, chans, weights + 3 * chans


def dot_split(x, y, dims):
    high = x.astype(BF16)
    low = (x - high.astype(F32)).astype(BF16)
    y = y.astype(BF16)
    return dot(high, y, dims) + dot(low, y, dims)


def pack_kernel(row_ref, col_ref, out_ref):
    rows = row_ref[...].astype(F32)
    out_ref[:16, :] = jnp.concatenate([rows, jnp.zeros_like(rows)], axis=1).astype(BF16)
    cols = col_ref.shape[1]
    lane = lax.broadcasted_iota(jnp.int32, (CH, LANES), 1)
    first, last = col_ref[:, :LANES].astype(F32), col_ref[:, cols - LANES :].astype(F32)
    out_ref[16:, :] = jnp.where(lane < LANES // 2, first, last).astype(BF16)


def off_edge(axis, index):
    return jnp.where(lax.axis_index(axis) == index, 0.0, 1.0).astype(F32)


def indicator(cols, n_col):
    lane = lax.broadcasted_iota(jnp.int32, (8, cols), 1)
    row = lax.broadcasted_iota(jnp.int32, (8, cols), 0)
    me = lax.axis_index("col")
    off_map = ((lane < 8) & (me == 0), lane < 0, (lane >= cols - 8) & (me == n_col - 1))
    edge_lane = lax.broadcasted_iota(jnp.int32, (8, LANES), 1)
    edge_row = lax.broadcasted_iota(jnp.int32, (8, LANES), 0)
    edge = jnp.where(edge_lane // 16 == edge_row, 1.0, 0.0)
    taps = []
    for tap in range(3):
        on_map = jnp.logical_not(off_map[tap])
        main = [jnp.where(on_map & (row == k), 1.0, 0.0) for k in range(8)]
        taps.append(jnp.concatenate(main + [edge], axis=1))
    return jnp.concatenate(taps, axis=0).astype(BF16)


def own_kernel(n_col, grad_ref, w2_ref, x_ref, back_ref, grad_rows_ref, grad_cols_ref, ind_ref, rows_scr):
    cols = grad_ref.shape[2]
    lane = lax.broadcasted_iota(jnp.int32, (CH, cols), 1)
    edge_lane = lax.broadcasted_iota(jnp.int32, (CH, LANES), 1)
    for piece in range(cols // LANES):
        wide = grad_ref[:, :, LANES * piece : LANES * (piece + 1)]
        rows_scr[piece] = wide.astype(F32).reshape(CH * 16, LANES)
    col_sum = jnp.zeros((CH, cols), F32)
    for half in range(2):
        rows = slice(half * CH, (half + 1) * CH)
        left = right = jnp.zeros((CH, LANES), F32)
        for k in range(8):
            pieces = [rows_scr[p, pl.ds(half * 8 + k, CH, stride=16), :] for p in range(cols // LANES)]
            line = jnp.concatenate(pieces, axis=1)
            col_sum = col_sum + line
            span = slice(k * cols, (k + 1) * cols)
            x_ref[1, rows, span] = line.astype(BF16)
            x_ref[0, rows, span] = jnp.where(lane < cols - 8, pltpu.roll(line, cols - 8, 1), 0.0).astype(BF16)
            x_ref[2, rows, span] = jnp.where(lane >= 8, pltpu.roll(line, 8, 1), 0.0).astype(BF16)
            first = pltpu.roll(pieces[0], 16 * k, 1) if k else pieces[0]
            last = pltpu.roll(pieces[-1], 16 * k + 16, 1) if k < 7 else pieces[-1]
            here = edge_lane // 16 == k
            left = jnp.where(here & (edge_lane % 16 < 8), first, left)
            right = jnp.where(here & (edge_lane % 16 >= 8), last, right)
        x_ref[0, rows, 8 * cols :] = left.astype(BF16)
        x_ref[1, rows, 8 * cols :] = jnp.zeros((CH, LANES), BF16)
        x_ref[2, rows, 8 * cols :] = right.astype(BF16)
    grad_cols_ref[...] = col_sum
    hits = indicator(cols, n_col)
    ind_ref[...] = hits
    row = lax.broadcasted_iota(jnp.int32, (8, 8 * cols), 0)
    span = lax.broadcasted_iota(jnp.int32, (8, 8 * cols), 1) // cols
    grad_rows_ref[...] = dot(jnp.where(row == span, 1.0, 0.0).astype(BF16), x_ref[1, :, : 8 * cols], NT)
    x_all = x_ref[...].reshape(6 * CH, x_ref.shape[2])
    back_ref[...] = dot(w2_ref[...], x_all, NN)


def main_kernel(
    n_row, n_col, prev_ref, next_ref, row_ref, col_ref, k1c_ref, k1ct_ref, k1f_ref, bias_ref,
    x_ref, back_ref, grad_rows_ref, grad_cols_ref, ind_ref,
    out_ref, own_ref, pre_scr, act_scr, inner_scr, w_scr, chunk_scr,
):
    cols = col_ref.shape[1]
    top, bottom = off_edge("row", 0), off_edge("row", n_row - 1)
    left, right = off_edge("col", 0), off_edge("col", n_col - 1)
    edge_lane = lax.broadcasted_iota(jnp.int32, (CH, LANES), 1)
    row_ext = jnp.concatenate(
        [top * prev_ref[:16, :CH].astype(F32), row_ref[...].astype(F32), bottom * next_ref[:16, :CH].astype(F32)],
        axis=0,
    )
    row_cat = jnp.concatenate([row_ext[8 * a : 8 * a + 32] for a in range(3)], axis=1).astype(BF16)
    col_ext = jnp.concatenate(
        [left * prev_ref[16:, :].astype(F32), col_ref[...].astype(F32), right * next_ref[16:, :].astype(F32)], axis=1
    )
    taps = []
    for tap in range(3):
        moved = pltpu.roll(col_ext, (8 * (1 - tap)) % (cols + 2 * LANES), 1) if tap != 1 else col_ext
        low, high = pltpu.roll(moved[:, :LANES], 8, 1), pltpu.roll(moved[:, LANES + cols :], 8, 1)
        edge = jnp.where(edge_lane < 8, low, jnp.where(edge_lane < 16, high, 0.0))
        for width in (16, 32, 64):
            edge = edge + pltpu.roll(edge, width, 1)
        taps.append(jnp.concatenate([moved[:, LANES : LANES + cols], edge], axis=1))
    col_cat = jnp.concatenate(taps, axis=0).astype(BF16)
    terms = dot(k1c_ref[...], col_cat, NN)
    low, mid, high = (terms[CH * a : CH * (a + 1)] for a in range(3))
    mid = mid + bias_ref[...]
    col_part = [low + mid + high, top * low + mid + high, low + mid + bottom * high, low + mid + high]
    row_terms = dot(k1f_ref[...], row_cat, NT)
    row_part = jnp.concatenate(
        [
            jnp.concatenate([row_terms[CH * b : CH * (b + 1), 8 * eb : 8 * eb + 8] for b in range(3)], axis=1)
            for eb in range(4)
        ],
        axis=0,
    )
    hits = ind_ref[...]
    pre_scr[...] = dot_split(row_part, hits, NN)
    on_map = jnp.where(edge_lane % 16 < 8, left, right)
    sums_of = []
    for eb in range(4):
        rows = slice(CH * eb, CH * (eb + 1))
        total = jnp.zeros((CH, cols), F32)
        for k in range(9):
            span = slice(k * cols, (k + 1) * cols) if k < 8 else slice(8 * cols, 8 * cols + LANES)
            pre = pre_scr[rows, span] + (col_part[eb][:, :cols] if k < 8 else col_part[eb][:, cols:])
            sig = 1.0 / (1.0 + jnp.exp(-pre))
            held = sig
            if eb == 0:
                held = held * top
            if eb == 3:
                held = held * bottom
            if k == 8:
                held = held * on_map
            act_scr[rows, span] = (pre * held).astype(BF16)
            inner = (back_ref[rows, span] * (held * (1.0 + pre * (1.0 - sig)))).astype(BF16)
            inner_scr[rows, span] = inner
            if k < 8:
                total = total + inner.astype(F32)
            else:
                total = jnp.concatenate([total, inner.astype(F32)], axis=1)
        sums_of.append(total)

    full = dot(x_ref[...].reshape(6 * CH, x_ref.shape[2]), act_scr[...], NT)
    sums = dot(hits, inner_scr[...], NT)
    row_sums = jnp.concatenate(
        [
            jnp.concatenate([sums[8 * b : 8 * b + 8, CH * eb : CH * (eb + 1)] for b in range(3)], axis=1)
            for eb in range(4)
        ],
        axis=0,
    )
    spread_row = dot_split(row_sums, k1f_ref[...], NN)

    def part(eb, a):
        return spread_row[8 * eb : 8 * eb + 8, CH * a : CH * (a + 1)]

    reached = [sum(part(eb, pb - eb) for eb in range(4) if 0 <= pb - eb <= 2) for pb in range(6)]
    above, mine, below = (jnp.concatenate(reached[2 * k : 2 * k + 2], axis=1) for k in range(3))
    own_ref[...] = grad_rows_ref[...] + mine
    whole = sums_of[0] + sums_of[1] + sums_of[2] + sums_of[3]
    col_sums = jnp.concatenate(
        [whole - (1.0 - top) * sums_of[1], whole, whole - (1.0 - bottom) * sums_of[2]], axis=0
    )
    high = col_sums.astype(BF16)
    rest = (col_sums - high.astype(F32)).astype(BF16)
    k1ct = k1ct_ref[...]
    spread_col = dot(k1ct, high, NN) + dot(k1ct, rest, NN)
    nothing = jnp.zeros((CH, LANES), F32)
    total = jnp.concatenate([nothing, grad_cols_ref[...], nothing], axis=1)
    for tap in range(3):
        piece = spread_col[CH * tap : CH * (tap + 1)]
        edge = piece[:, cols:]
        for width in (16, 32, 64):
            edge = edge + pltpu.roll(edge, width, 1)
        low = jnp.where(edge_lane >= LANES - 8, pltpu.roll(edge, LANES - 8, 1), 0.0)
        high_edge = jnp.where(edge_lane < 8, pltpu.roll(edge, LANES - 8, 1), 0.0)
        piece = jnp.concatenate([low, piece[:, :cols], high_edge], axis=1)
        total = total + (pltpu.roll(piece, (8 * (tap - 1)) % (cols + 2 * LANES), 1) if tap != 1 else piece)
    one_row = dot_split(row_sums, row_cat, TN)
    one_col = dot(high, col_cat, NT) + dot(rest, col_cat, NT)
    gap = jnp.zeros((32, cols + LANES), F32)
    bias_row = dot_exact(jnp.ones((8, cols + LANES), F32), jnp.concatenate([gap, whole, gap], axis=0), NT)
    for a in range(3):
        for b in range(3):
            one = one_row[CH * b : CH * (b + 1), CH * a : CH * (a + 1)]
            one = one + one_col[CH * a : CH * (a + 1), CH * b : CH * (b + 1)]
            two = [
                full[CH * (2 * b + gb) : CH * (2 * b + gb + 1), CH * (a + gb) : CH * (a + gb + 1)] for gb in range(2)
            ]
            w_scr[CH * (3 * a + b) : CH * (3 * a + b + 1), :] = jnp.concatenate([one, two[0] + two[1]], axis=1)

    weights, chans, sums_end = chunk_rows(n_row)
    tail = total[:, :LANES] + total[:, cols + LANES :] + bias_row[:1, :]
    before = lax.axis_index("row") - 1
    for j in range(n_row):
        chunk_scr[j, :weights, :] = w_scr[weights * j : weights * (j + 1), :]
        share = slice(chans * j, chans * (j + 1))
        chunk_scr[j, weights : weights + chans, :] = total[share, LANES : 2 * LANES]
        chunk_scr[j, weights + chans : weights + 2 * chans, :] = total[share, cols : cols + LANES]
        chunk_scr[j, weights + 2 * chans : sums_end, :] = tail[share]
        chunk_scr[j, sums_end:, :] = jnp.where(before == j, above, below)
    out_ref[...] = chunk_scr[...].astype(BF16)


def row_sum_kernel(n_row, n_col, got_ref, own_ref, out_ref):
    sums_end = chunk_rows(n_row)[2]
    me = lax.axis_index("row")
    total = got_ref[0].astype(F32)
    for j in range(1, n_row):
        total = total + got_ref[j].astype(F32)
    total = total[:sums_end]
    before = got_ref[jnp.maximum(me - 1, 0)].astype(F32)[sums_end:]
    after = got_ref[jnp.minimum(me + 1, n_row - 1)].astype(F32)[sums_end:]
    rows = own_ref[...] + off_edge("row", 0) * before + off_edge("row", n_row - 1) * after
    for k in range(n_col):
        out_ref[k, :sums_end, :] = total
        out_ref[k, sums_end:, :] = rows


def col_sum_kernel(n_row, n_col, cols, got_ref, row_ref, bias_ref, out_ref):
    weights, chans, sums_end = chunk_rows(n_row)
    me = lax.axis_index("col")
    whole = math.sqrt(16 * n_row * cols * n_col)
    total = got_ref[0]
    for k in range(1, n_col):
        total = total + got_ref[k]
    rows = total[sums_end:, :] * (1.0 / math.sqrt(cols * n_col))
    row_ref[0:8, :] = rows[:, :CH]
    row_ref[8:16, :] = rows[:, CH:]
    bias_ref[...] = total[sums_end - 1 : sums_end, 32 : 32 + CH] * (1.0 / whole)
    scale = 1.0 / math.sqrt(16 * n_row)
    before = got_ref[jnp.maximum(me - 1, 0), weights + 2 * chans : sums_end, :] * off_edge("col", 0)
    after = got_ref[jnp.minimum(me + 1, n_col - 1), weights + 2 * chans : sums_end, :] * off_edge("col", n_col - 1)
    lane = lax.broadcasted_iota(jnp.int32, before.shape, 1)
    low = got_ref[me, weights : weights + chans, :] + jnp.where(lane < 16, before, 0.0)
    high = got_ref[me, weights + chans : weights + 2 * chans, :] + jnp.where(lane >= LANES - 16, after, 0.0)
    share = total[:weights, :] * (1.0 / whole)
    for j in range(n_row):
        out_ref[j, :weights, :] = share
        out_ref[j, weights : weights + chans, :] = low * scale
        out_ref[j, weights + chans : weights + 2 * chans, :] = high * scale
        if weights + 2 * chans < out_ref.shape[1]:
            out_ref[j, weights + 2 * chans :, :] = jnp.zeros((out_ref.shape[1] - weights - 2 * chans, LANES), F32)


def spread_kernel(n_row, got_ref, col_ref, one_ref, two_ref):
    weights, chans, _ = chunk_rows(n_row)
    for j in range(n_row):
        share = got_ref[j, :weights, :]
        one_ref[weights * j : weights * (j + 1), :] = share[:, :CH]
        two_ref[weights * j : weights * (j + 1), :] = share[:, CH:]
        col_ref[chans * j : chans * (j + 1), :LANES] = got_ref[j, weights : weights + chans, :]
        col_ref[chans * j : chans * (j + 1), LANES:] = got_ref[j, weights + chans : weights + 2 * chans, :]


PARAMS = pltpu.CompilerParams(vmem_limit_bytes=48 * 1024 * 1024)


def sds(shape, dtype=F32):
    return jax.ShapeDtypeStruct(shape, dtype)


def shards(n_row, n_col, grad_out, row_feat, col_feat, conv_one, bias_one, conv_two):
    cols = grad_out.shape[2]
    weights, chans, sums_end = chunk_rows(n_row)
    places = 8 * cols + LANES
    strip = pl.pallas_call(pack_kernel, out_shape=sds((16 + CH, LANES), BF16), compiler_params=PARAMS)(
        row_feat, col_feat.T
    )
    pairs = [
        (r * n_col + c, (r + 1) % n_row * n_col + (c + 1) % n_col) for r in range(n_row) for c in range(n_col)
    ]
    prev = lax.ppermute(strip, ("row", "col"), pairs)
    nxt = lax.ppermute(strip, ("row", "col"), [(target, source) for source, target in pairs])

    padded = jnp.pad(jnp.transpose(conv_two, (0, 3, 1, 2)), ((1, 1), (0, 0), (0, 0), (0, 0)))
    w2 = jnp.stack([padded[1:], padded[:-1]], axis=3).reshape(4 * CH, 6 * CH)
    k1c = jnp.transpose(conv_one, (0, 2, 1, 3)).reshape(3 * CH, 3 * CH)
    k1f = jnp.transpose(conv_one, (1, 2, 0, 3)).reshape(3 * CH, 3 * CH)

    held = pl.pallas_call(
        lambda *refs: own_kernel(n_col, *refs),
        out_shape=(
            sds((3, 2 * CH, places), BF16), sds((4 * CH, places)), sds((8, 2 * CH)), sds((CH, cols)),
            sds((24, places), BF16),
        ),
        scratch_shapes=[pltpu.VMEM((cols // LANES, CH * 16, LANES), F32)],
        compiler_params=PARAMS,
    )(grad_out, w2)
    chunks, own = pl.pallas_call(
        lambda *refs: main_kernel(n_row, n_col, *refs),
        out_shape=(sds((n_row, sums_end + 8, LANES), BF16), sds((8, LANES))),
        scratch_shapes=[
            pltpu.VMEM((4 * CH, places), F32),
            pltpu.VMEM((4 * CH, places), BF16),
            pltpu.VMEM((4 * CH, places), BF16),
            pltpu.VMEM((9 * CH, LANES), F32),
            pltpu.VMEM((n_row, sums_end + 8, LANES), F32),
        ],
        compiler_params=PARAMS,
    )(prev, nxt, row_feat, col_feat.T, k1c, k1c.T, k1f, bias_one[:, None], *held)
    got = lax.all_to_all(chunks, "row", 0, 0)
    copies = pl.pallas_call(
        lambda *refs: row_sum_kernel(n_row, n_col, *refs),
        out_shape=sds((n_col, sums_end + 8, LANES)),
        compiler_params=PARAMS,
    )(got, own)
    got = lax.all_to_all(copies, "col", 0, 0)
    end = -(-(weights + 2 * chans) // 8) * 8
    row_grad, bias_grad, copies = pl.pallas_call(
        lambda *refs: col_sum_kernel(n_row, n_col, cols, *refs),
        out_shape=(sds((16, CH)), sds((1, CH)), sds((n_row, end, LANES))),
        compiler_params=PARAMS,
    )(got)
    got = lax.all_to_all(copies, "row", 0, 0)
    col_grad, one, two = pl.pallas_call(
        lambda *refs: spread_kernel(n_row, *refs),
        out_shape=(sds((CH, cols)), sds((9 * CH, CH)), sds((9 * CH, CH))),
        compiler_params=PARAMS,
    )(got)
    shape = conv_one.shape
    return row_grad, col_grad.T, one.reshape(shape), bias_grad[0], two.reshape(shape)


def solution(mesh):
    in_specs = (P(None, "row", "col"), P("row", None), P("col", None), P(), P(), P())
    out_specs = (P("row", None), P("col", None), P(), P(), P())
    n_row, n_col = mesh.shape["row"], mesh.shape["col"]
    return jax.shard_map(
        lambda *args: shards(n_row, n_col, *args), mesh=mesh, in_specs=in_specs, out_specs=out_specs, check_vma=False
    )
```

time: 80.7 us -> 67.4 us (0.84)
  waiting for transfers between devices: 8.1 us -> 1.96 us
  starting transfers between devices: 12.9 us -> 7.75 us
  Pallas kernels: 9.04 us -> 6.56 us
  local copies, waits for them, and re-layouts: 3.97 us -> 5.53 us
  blocking collectives: 44.8 us -> 43.5 us
    ppermute x3 -> x2, waiting for transfers between devices: 8.1 us -> 1.96 us  [the longest x1 1.96 us: shards(): prev = lax.ppermute(strip, ('row', 'col'), pairs)]
    ppermute x3 -> x2, starting transfers between devices: 12.9 us -> 7.75 us  [the longest x1 7.75 us: shards(): lax.ppermute(strip, ('row', 'col'), [(target, source) for source, target...]
    all_to_all x1, blocking collectives: 17.4 us -> 13.4 us  [shards(): got = lax.all_to_all(chunks, 'row', 0, 0)]
    all_to_all x1, blocking collectives: 15.1 us -> 18 us  [shards(): got = lax.all_to_all(copies, 'col', 0, 0)]
    pallas_call x1, Pallas kernels: 6.09 us -> 3.68 us  [shards(): pl.pallas_call(lambda *refs: main_kernel(n_row, n_col, *refs), out_shape=...]
    unnamed x12, local copies, waits for them, and re-layouts: 3.03 us -> 1.52 us
    another operation x0 -> x2, local copies, waits for them, and re-layouts: none -> 1.4 us  [shards(): w2 = jnp.stack([padded[1:], padded[:-1]], axis=3).reshape(4 * CH, 6 * CH)]
    transpose x1, local copies, waits for them, and re-layouts: 0.13 us -> 1.04 us  [shards(): k1c = jnp.transpose(conv_one, (0, 2, 1, 3)).reshape(3 * CH, 3 * CH)]
  transfers between devices with their start and end apart: 3 -> 2, of which waited for: 1 -> 1; matrix products, arithmetic and copies ran while one was open for 1% -> 6% of each run, Pallas kernels for 0% -> 2%
where the time goes in v2:
time: 67.4 us; the launch traced here: 66.2 us
  blocking collectives  43.5 us (65%)
  starting transfers between devices  7.75 us (11%)
  Pallas kernels  6.56 us (10%)
  local copies, waits for them, and re-layouts  5.53 us (8%)
  waiting for transfers between devices  1.96 us (3%)
  between operations  0.76 us (1%)
    all_to_all x1, blocking collectives, shards(): got = lax.all_to_all(copies, 'col', 0, 0)  18 us
    all_to_all x1, blocking collectives, shards(): got = lax.all_to_all(chunks, 'row', 0, 0)  13.4 us
    all_to_all x1, blocking collectives, shards(): got = lax.all_to_all(copies, 'row', 0, 0)  12.1 us
    ppermute x1, starting transfers between devices, shards(): lax.ppermute(strip, ('row', 'col'), [(target, source) for source, target...  7.75 us
    pallas_call x1, Pallas kernels, shards(): pl.pallas_call(lambda *refs: main_kernel(n_row, n_col, *refs), out_shape=...  3.68 us
    ppermute x1, waiting for transfers between devices, shards(): prev = lax.ppermute(strip, ('row', 'col'), pairs)  1.96 us
    unnamed x12, local copies, waits for them, and re-layouts  1.52 us
    another operation x2, local copies, waits for them, and re-layouts, shards(): w2 = jnp.stack([padded[1:], padded[:-1]], axis=3).reshape(4 * CH, 6 * CH)  1.4 us
  transfers between devices with their start and end apart: 2, of which 1 were waited for; matrix products, arithmetic and copies ran while one was open for 6% of the time, Pallas kernels for 2%

profile of v2, /device:TPU:1, one launch (start us, length us, event | category | flops | bytes accessed | tf_op | source)
XLA Modules:
  0.0 66.2 jit_solution(7842250166568537772)
XLA Ops:
  0.6 0.0 copy-start
  0.6 0.0 copy-start.1
  0.7 0.8 %copy-done.1 = bf16[256,64]{0,1:T(8,128)(2,1)S(1)} copy-done((bf16[256,64]{0,1:T(8,128)(2,1)S(1)}, bf16[256,64]{0,1:T(8,128)(2,1)}, u32[]{:S(2)}) %copy-start.1) | copy-done | bytes 32792
  1.5 0.0 copy-start.3
  1.5 0.7 %copy-done.3 = bf16[16,64]{1,0:T(8,128)(2,1)S(1)} copy-done((bf16[16,64]{1,0:T(8,128)(2,1)S(1)}, bf16[16,64]{1,0:T(8,128)(2,1)}, u32[]{:S(2)}) %copy-start.3) | copy-done | bytes 2072
  2.2 7.7 %collective-permute-start.1 = (bf16[80,128]{1,0:T(8,128)(2,1)S(1)}, bf16[80,128]{1,0:T(8,128)(2,1)S(1)}, u32[]{:S(2)}, u32[]{:S(2)}) collective-permute-start(bf16[80,128]{1,0:T(8,128)(2,1)S(1)} %shard_map.101), channel_id=1, source_target_pairs={{9,0},{10,1},{11,2},{12,3},{13,4},{14,5},{15,6},{8,7},{17,8},{18,9... | collective-permute-start | bytes 61448 | tf_op jit(solution)/shard_map/ppermute | solution.py:302
  9.9 0.0 collective-permute-start
  9.9 1.0 %fusion = (bf16[4,64,3,1,64]{1,4,2,0,3:T(8,128)(2,1)S(1)}, bf16[4,64,3,1,64]{1,4,2,0,3:T(8,128)(2,1)S(1)}) fusion(bf16[3,64,3,64]{1,3,2,0:T(8,128)(2,1)} %bitcast.19), kind=kLoop, calls=%fused_computation.3 | loop fusion | bytes 270336 | tf_op jit(solution)/shard_map/stack | solution.py:305
  11.0 0.0 copy-start.2
  11.0 0.0 copy-start.4
  11.0 0.1 pad_maximum_fusion
  11.1 0.7 %copy.20.refs_7_ = f32[64,1]{1,0:T(8,128)S(1)} copy(f32[64,1]{0,1:T(1,128)} %bitcast.20) | data formatting | bytes 512 | tf_op jit(solution)/shard_map/broadcast_in_dim | solution.py:329
  11.8 1.0 %copy.16 = bf16[3,64,3,64]{3,2,1,0:T(4,128)(2,1)S(1)} copy(bf16[3,64,3,64]{3,1,2,0:T(8,128)(2,1)} %bitcast.17) | data formatting | bytes 147456 | tf_op jit(solution)/shard_map/transpose | solution.py:306
  12.9 0.2 reshape.25.refs_4_
  13.0 0.1 copy.17
  13.1 0.0 copy-done.5
  13.2 0.1 copy.18
  13.3 0.2 reshape.26.refs_6_
  13.5 0.4 copy.19
  13.8 0.3 reshape.27.refs_1_
  14.1 0.0 copy-done
  14.1 1.3 %shard_map.102 = (bf16[3,128,2176]{2,1,0:T(8,128)(2,1)S(1)}, f32[256,2176]{1,0:T(8,128)S(1)}, f32[8,128]{1,0:T(8,128)S(1)}, f32[64,256]{1,0:T(8,128)S(1)}, bf16[24,2176]{1,0:T(8,128)(2,1)S(1)}) custom-call(bf16[64,16,256]{2,1,0:T(8,128)(2,1)S(1)} %copy-done, bf16[256,384]{1,0:T(8,128)(2,1)S(1)} %reshape.27.refs_1_), custom_call_target="tpu_custom_call" | custom-call | tf_op jit(solution)/shard_map/pallas_call | solution.py:309
  15.4 0.0 collective-permute-done.1.refs_1_
  15.4 2.0 %collective-permute-done.refs_0_ = bf16[80,128]{1,0:T(8,128)(2,1)S(1)} collective-permute-done((bf16[80,128]{1,0:T(8,128)(2,1)S(1)}, bf16[80,128]{1,0:T(8,128)(2,1)S(1)}, u32[]{:S(2)}, u32[]{:S(2)}) %collective-permute-start) | collective-permute-done | bytes 20512 | tf_op jit(solution)/shard_map/ppermute | solution.py:301
  17.3 0.0 copy-done.2
  17.3 0.0 copy-done.4
  17.3 3.7 %shard_map.103 = (bf16[32,32,128]{2,1,0:T(8,128)(2,1)S(1)}, f32[8,128]{1,0:T(8,128)S(1)}) custom-call(bf16[80,128]{1,0:T(8,128)(2,1)S(1)} %collective-permute-done.refs_0_, bf16[80,128]{1,0:T(8,128)(2,1)S(1)} %collective-permute-done.1.refs_1_, bf16[16,64]{1,0:T(8,128)(2,1)S(1)} %copy-done.4, bf16[64,256]{1,0:T(8,128)(2,1)S(1)} %bitcast.16, ...), custom_call_target="tpu_custom_call" | custom-call | tf_op jit(solution)/shard_map/pallas_call | solution.py:318
  21.0 13.4 %all_to_all.15.refs_0_ = bf16[32,32,128]{2,1,0:T(8,128)(2,1)S(1)} all-to-all(bf16[32,32,128]{2,1,0:T(8,128)(2,1)S(1)} %get-tuple-element.23), channel_id=1, replica_groups=mesh['row'=32,'col'=8] {'row'}, dimensions={0} | all-to-all | bytes 524288 | tf_op jit(solution)/shard_map/all_to_all | solution.py:330
  34.4 18.0 %all_to_all.16.refs_0_ = f32[8,32,128]{2,1,0:T(8,128)S(1)} all-to-all(f32[8,32,128]{2,1,0:T(8,128)S(1)} %shard_map.104), channel_id=1, replica_groups=mesh['row'=32,'col'=8] {'col'}, dimensions={0} | all-to-all | bytes 262144 | tf_op jit(solution)/shard_map/all_to_all | solution.py:336
  52.5 0.7 %shard_map.105 = (f32[16,64]{1,0:T(8,128)}, f32[1,64]{1,0:T(1,128)}, f32[32,24,128]{2,1,0:T(8,128)S(1)}) custom-call(f32[8,32,128]{2,1,0:T(8,128)S(1)} %all_to_all.16.refs_0_), custom_call_target="tpu_custom_call" | custom-call | tf_op jit(solution)/shard_map/pallas_call | solution.py:338
  53.1 12.1 %all_to_all.17.refs_0_ = f32[32,24,128]{2,1,0:T(8,128)S(1)} all-to-all(f32[32,24,128]{2,1,0:T(8,128)S(1)} %get-tuple-element.26), channel_id=1, replica_groups=mesh['row'=32,'col'=8] {'row'}, dimensions={0} | all-to-all | bytes 786432 | tf_op jit(solution)/shard_map/all_to_all | solution.py:343
  65.3 0.9 %shard_map.106 = (f32[64,256]{1,0:T(8,128)}, f32[576,64]{1,0:T(8,128)}, f32[576,64]{1,0:T(8,128)}) custom-call(f32[32,24,128]{2,1,0:T(8,128)S(1)} %all_to_all.17.refs_0_), custom_call_target="tpu_custom_call" | custom-call | tf_op jit(solution)/shard_map/pallas_call | solution.py:344
  (3 shorter events, 0.1 us)
Async XLA Ops:
  0.6 13.5 %copy-start = (bf16[64,16,256]{2,1,0:T(8,128)(2,1)S(1)}, bf16[64,16,256]{2,1,0:T(8,128)(2,1)}, u32[]{:S(2)}) copy-start(bf16[64,16,256]{2,1,0:T(8,128)(2,1)} %refs_0_.1) | copy-start | bytes 1572868
  0.6 0.8 %copy-start.1 = (bf16[256,64]{0,1:T(8,128)(2,1)S(1)}, bf16[256,64]{0,1:T(8,128)(2,1)}, u32[]{:S(2)}) copy-start(bf16[256,64]{0,1:T(8,128)(2,1)} %param.8) | copy-start | bytes 98308
  1.5 0.7 %copy-start.3 = (bf16[16,64]{1,0:T(8,128)(2,1)S(1)}, bf16[16,64]{1,0:T(8,128)(2,1)}, u32[]{:S(2)}) copy-start(bf16[16,64]{1,0:T(8,128)(2,1)} %refs_2_.1) | copy-start | bytes 6148
  2.1 11.0 %copy-start.5 = (bf16[3,3,64,64]{3,2,1,0:T(8,128)(2,1)S(1)}, bf16[3,3,64,64]{3,2,1,0:T(8,128)(2,1)}, u32[]{:S(2)}) copy-start(bf16[3,3,64,64]{3,2,1,0:T(8,128)(2,1)} %param.9) | copy-start | bytes 221188
  2.2 13.2 %collective-permute-start.1 = (bf16[80,128]{1,0:T(8,128)(2,1)S(1)}, bf16[80,128]{1,0:T(8,128)(2,1)S(1)}, u32[]{:S(2)}, u32[]{:S(2)}) collective-permute-start(bf16[80,128]{1,0:T(8,128)(2,1)S(1)} %shard_map.101), channel_id=1, source_target_pairs={{9,0},{10,1},{11,2},{12,3},{13,4},{14,5},{15,6},{8,7},{17,8},{18,9... | collective-permute-start | bytes 61448 | tf_op jit(solution)/shard_map/ppermute | solution.py:302
  9.9 7.4 %collective-permute-start = (bf16[80,128]{1,0:T(8,128)(2,1)S(1)}, bf16[80,128]{1,0:T(8,128)(2,1)S(1)}, u32[]{:S(2)}, u32[]{:S(2)}) collective-permute-start(bf16[80,128]{1,0:T(8,128)(2,1)S(1)} %shard_map.101), channel_id=1, source_target_pairs={{0,9},{1,10},{2,11},{3,12},{4,13},{5,14},{6,15},{7,8},{8,17},{9,18... | collective-permute-start | bytes 61448 | tf_op jit(solution)/shard_map/ppermute | solution.py:301
  11.0 6.4 %copy-start.2 = (bf16[256,64]{0,1:T(8,128)(2,1)S(1)}, bf16[256,64]{0,1:T(8,128)(2,1)}, u32[]{:S(2)}) copy-start(bf16[256,64]{0,1:T(8,128)(2,1)} %param.8) | copy-start | bytes 98308
  11.0 6.4 %copy-start.4 = (bf16[16,64]{1,0:T(8,128)(2,1)S(1)}, bf16[16,64]{1,0:T(8,128)(2,1)}, u32[]{:S(2)}) copy-start(bf16[16,64]{1,0:T(8,128)(2,1)} %refs_2_.1) | copy-start | bytes 6148

commit v3 on v2

--- a/solution.py
+++ b/solution.py
@@ -37,7 +37,13 @@
     return dot(high, y, dims) + dot(low, y, dims)
 
 
-def pack_kernel(row_ref, col_ref, out_ref):
+def pack_kernel(row_hbm, col_hbm, out_ref, row_ref, col_ref, row_sem, col_sem):
+    row_copy = pltpu.make_async_copy(row_hbm, row_ref, row_sem)
+    col_copy = pltpu.make_async_copy(col_hbm, col_ref, col_sem)
+    row_copy.start()
+    col_copy.start()
+    row_copy.wait()
+    col_copy.wait()
     rows = row_ref[...].astype(F32)
     out_ref[:16, :] = jnp.concatenate([rows, jnp.zeros_like(rows)], axis=1).astype(BF16)
     cols = col_ref.shape[1]
@@ -66,8 +72,28 @@
     return jnp.concatenate(taps, axis=0).astype(BF16)
 
 
-def own_kernel(n_col, grad_ref, w2_ref, x_ref, back_ref, grad_rows_ref, grad_cols_ref, ind_ref, rows_scr):
+def own_kernel(
+    n_col, grad_ref, one_ref, two_ref, bias_ref,
+    x_ref, back_ref, grad_rows_ref, grad_cols_ref, ind_ref, k1c_ref, k1f_ref, bias_col_ref, rows_scr,
+):
     cols = grad_ref.shape[2]
+    one = [[one_ref[a, b].astype(F32) for b in range(3)] for a in range(3)]
+    for k in range(3):
+        rows = slice(CH * k, CH * (k + 1))
+        k1c_ref[rows, :] = jnp.concatenate(one[k], axis=1).astype(BF16)
+        k1f_ref[rows, :] = jnp.concatenate([one[a][k] for a in range(3)], axis=1).astype(BF16)
+    nil = jnp.zeros((CH, CH), F32)
+    two = [[two_ref[a, b].astype(F32) for b in range(3)] for a in range(3)]
+    w2 = jnp.concatenate(
+        [
+            jnp.concatenate([two[eb - gb][b] if 0 <= eb - gb <= 2 else nil for eb in range(4)], axis=1)
+            for b in range(3)
+            for gb in range(2)
+        ],
+        axis=0,
+    ).astype(BF16)
+    bias = jnp.concatenate([bias_ref[...], jnp.zeros((1, LANES - CH), F32)], axis=1)
+    bias_col_ref[...] = jnp.broadcast_to(bias, (8, LANES)).T[:CH, :]
     lane = lax.broadcasted_iota(jnp.int32, (CH, cols), 1)
     edge_lane = lax.broadcasted_iota(jnp.int32, (CH, LANES), 1)
     for piece in range(cols // LANES):
@@ -100,12 +126,12 @@
     span = lax.broadcasted_iota(jnp.int32, (8, 8 * cols), 1) // cols
     grad_rows_ref[...] = dot(jnp.where(row == span, 1.0, 0.0).astype(BF16), x_ref[1, :, : 8 * cols], NT)
     x_all = x_ref[...].reshape(6 * CH, x_ref.shape[2])
-    back_ref[...] = dot(w2_ref[...], x_all, NN)
+    back_ref[...] = dot(w2, x_all, TN)
 
 
 def main_kernel(
-    n_row, n_col, prev_ref, next_ref, row_ref, col_ref, k1c_ref, k1ct_ref, k1f_ref, bias_ref,
-    x_ref, back_ref, grad_rows_ref, grad_cols_ref, ind_ref,
+    n_row, n_col, prev_ref, next_ref, row_ref, col_ref,
+    x_ref, back_ref, grad_rows_ref, grad_cols_ref, ind_ref, k1c_ref, k1f_ref, bias_ref,
     out_ref, own_ref, pre_scr, act_scr, inner_scr, w_scr, chunk_scr,
 ):
     cols = col_ref.shape[1]
@@ -131,7 +157,7 @@
     col_cat = jnp.concatenate(taps, axis=0).astype(BF16)
     terms = dot(k1c_ref[...], col_cat, NN)
     low, mid, high = (terms[CH * a : CH * (a + 1)] for a in range(3))
-    mid = mid + bias_ref[...]
+    mid = mid + bias_ref[:, :1]
     col_part = [low + mid + high, top * low + mid + high, low + mid + bottom * high, low + mid + high]
     row_terms = dot(k1f_ref[...], row_cat, NT)
     row_part = jnp.concatenate(
@@ -191,8 +217,8 @@
     )
     high = col_sums.astype(BF16)
     rest = (col_sums - high.astype(F32)).astype(BF16)
-    k1ct = k1ct_ref[...]
-    spread_col = dot(k1ct, high, NN) + dot(k1ct, rest, NN)
+    k1c = k1c_ref[...]
+    spread_col = dot(k1c, high, TN) + dot(k1c, rest, TN)
     nothing = jnp.zeros((CH, LANES), F32)
     total = jnp.concatenate([nothing, grad_cols_ref[...], nothing], axis=1)
     for tap in range(3):
@@ -240,45 +266,47 @@
     before = got_ref[jnp.maximum(me - 1, 0)].astype(F32)[sums_end:]
     after = got_ref[jnp.minimum(me + 1, n_row - 1)].astype(F32)[sums_end:]
     rows = own_ref[...] + off_edge("row", 0) * before + off_edge("row", n_row - 1) * after
+    whole = jnp.concatenate([total, rows], axis=0).astype(BF16)
     for k in range(n_col):
-        out_ref[k, :sums_end, :] = total
-        out_ref[k, sums_end:, :] = rows
-
-
-def col_sum_kernel(n_row, n_col, cols, got_ref, row_ref, bias_ref, out_ref):
+        out_ref[k] = whole
+
+
+def col_sum_kernel(n_row, n_col, cols, got_ref, row_ref, bias_ref, out_ref, scr):
     weights, chans, sums_end = chunk_rows(n_row)
     me = lax.axis_index("col")
     whole = math.sqrt(16 * n_row * cols * n_col)
-    total = got_ref[0]
+    total = got_ref[0].astype(F32)
     for k in range(1, n_col):
-        total = total + got_ref[k]
+        total = total + got_ref[k].astype(F32)
     rows = total[sums_end:, :] * (1.0 / math.sqrt(cols * n_col))
     row_ref[0:8, :] = rows[:, :CH]
     row_ref[8:16, :] = rows[:, CH:]
     bias_ref[...] = total[sums_end - 1 : sums_end, 32 : 32 + CH] * (1.0 / whole)
+    before = got_ref[jnp.maximum(me - 1, 0)].astype(F32) * off_edge("col", 0)
+    after = got_ref[jnp.minimum(me + 1, n_col - 1)].astype(F32) * off_edge("col", n_col - 1)
+    mine = got_ref[me].astype(F32)
+    edge = slice(weights + 2 * chans, sums_end)
+    lane = lax.broadcasted_iota(jnp.int32, (chans, LANES), 1)
+    low = mine[weights : weights + chans] + jnp.where(lane < 16, before[edge], 0.0)
+    high = mine[weights + chans : weights + 2 * chans] + jnp.where(lane >= LANES - 16, after[edge], 0.0)
     scale = 1.0 / math.sqrt(16 * n_row)
-    before = got_ref[jnp.maximum(me - 1, 0), weights + 2 * chans : sums_end, :] * off_edge("col", 0)
-    after = got_ref[jnp.minimum(me + 1, n_col - 1), weights + 2 * chans : sums_end, :] * off_edge("col", n_col - 1)
-    lane = lax.broadcasted_iota(jnp.int32, before.shape, 1)
-    low = got_ref[me, weights : weights + chans, :] + jnp.where(lane < 16, before, 0.0)
-    high = got_ref[me, weights + chans : weights + 2 * chans, :] + jnp.where(lane >= LANES - 16, after, 0.0)
-    share = total[:weights, :] * (1.0 / whole)
+    scr[...] = jnp.zeros(scr.shape, F32)
+    scr[:weights, :] = total[:weights] * (1.0 / whole)
+    scr[weights : weights + chans, :] = low * scale
+    scr[weights + chans : weights + 2 * chans, :] = high * scale
+    share = scr[...].astype(BF16)
     for j in range(n_row):
-        out_ref[j, :weights, :] = share
-        out_ref[j, weights : weights + chans, :] = low * scale
-        out_ref[j, weights + chans : weights + 2 * chans, :] = high * scale
-        if weights + 2 * chans < out_ref.shape[1]:
-            out_ref[j, weights + 2 * chans :, :] = jnp.zeros((out_ref.shape[1] - weights - 2 * chans, LANES), F32)
+        out_ref[j] = share
 
 
 def spread_kernel(n_row, got_ref, col_ref, one_ref, two_ref):
     weights, chans, _ = chunk_rows(n_row)
     for j in range(n_row):
-        share = got_ref[j, :weights, :]
-        one_ref[weights * j : weights * (j + 1), :] = share[:, :CH]
-        two_ref[weights * j : weights * (j + 1), :] = share[:, CH:]
-        col_ref[chans * j : chans * (j + 1), :LANES] = got_ref[j, weights : weights + chans, :]
-        col_ref[chans * j : chans * (j + 1), LANES:] = got_ref[j, weights + chans : weights + 2 * chans, :]
+        chunk = got_ref[j].astype(F32)
+        one_ref[weights * j : weights * (j + 1), :] = chunk[:weights, :CH]
+        two_ref[weights * j : weights * (j + 1), :] = chunk[:weights, CH:]
+        col_ref[chans * j : chans * (j + 1), :LANES] = chunk[weights : weights + chans]
+        col_ref[chans * j : chans * (j + 1), LANES:] = chunk[weights + chans : weights + 2 * chans]
 
 
 PARAMS = pltpu.CompilerParams(vmem_limit_bytes=48 * 1024 * 1024)
@@ -292,29 +320,33 @@
     cols = grad_out.shape[2]
     weights, chans, sums_end = chunk_rows(n_row)
     places = 8 * cols + LANES
-    strip = pl.pallas_call(pack_kernel, out_shape=sds((16 + CH, LANES), BF16), compiler_params=PARAMS)(
-        row_feat, col_feat.T
-    )
+    strip = pl.pallas_call(
+        pack_kernel,
+        out_shape=sds((16 + CH, LANES), BF16),
+        in_specs=[pl.BlockSpec(memory_space=pltpu.HBM)] * 2,
+        scratch_shapes=[
+            pltpu.VMEM((16, CH), BF16),
+            pltpu.VMEM((CH, cols), BF16),
+            pltpu.SemaphoreType.DMA,
+            pltpu.SemaphoreType.DMA,
+        ],
+        compiler_params=PARAMS,
+    )(row_feat, col_feat.T)
     pairs = [
         (r * n_col + c, (r + 1) % n_row * n_col + (c + 1) % n_col) for r in range(n_row) for c in range(n_col)
     ]
     prev = lax.ppermute(strip, ("row", "col"), pairs)
     nxt = lax.ppermute(strip, ("row", "col"), [(target, source) for source, target in pairs])
 
-    padded = jnp.pad(jnp.transpose(conv_two, (0, 3, 1, 2)), ((1, 1), (0, 0), (0, 0), (0, 0)))
-    w2 = jnp.stack([padded[1:], padded[:-1]], axis=3).reshape(4 * CH, 6 * CH)
-    k1c = jnp.transpose(conv_one, (0, 2, 1, 3)).reshape(3 * CH, 3 * CH)
-    k1f = jnp.transpose(conv_one, (1, 2, 0, 3)).reshape(3 * CH, 3 * CH)
-
     held = pl.pallas_call(
         lambda *refs: own_kernel(n_col, *refs),
         out_shape=(
             sds((3, 2 * CH, places), BF16), sds((4 * CH, places)), sds((8, 2 * CH)), sds((CH, cols)),
-            sds((24, places), BF16),
+            sds((24, places), BF16), sds((3 * CH, 3 * CH), BF16), sds((3 * CH, 3 * CH), BF16), sds((CH, 8)),
         ),
         scratch_shapes=[pltpu.VMEM((cols // LANES, CH * 16, LANES), F32)],
         compiler_params=PARAMS,
-    )(grad_out, w2)
+    )(grad_out, conv_one, conv_two, bias_one.reshape(1, CH))
     chunks, own = pl.pallas_call(
         lambda *refs: main_kernel(n_row, n_col, *refs),
         out_shape=(sds((n_row, sums_end + 8, LANES), BF16), sds((8, LANES))),
@@ -326,18 +358,19 @@
             pltpu.VMEM((n_row, sums_end + 8, LANES), F32),
         ],
         compiler_params=PARAMS,
-    )(prev, nxt, row_feat, col_feat.T, k1c, k1c.T, k1f, bias_one[:, None], *held)
+    )(prev, nxt, row_feat, col_feat.T, *held)
     got = lax.all_to_all(chunks, "row", 0, 0)
     copies = pl.pallas_call(
         lambda *refs: row_sum_kernel(n_row, n_col, *refs),
-        out_shape=sds((n_col, sums_end + 8, LANES)),
+        out_shape=sds((n_col, sums_end + 8, LANES), BF16),
         compiler_params=PARAMS,
     )(got, own)
     got = lax.all_to_all(copies, "col", 0, 0)
-    end = -(-(weights + 2 * chans) // 8) * 8
+    end = -(-(weights + 2 * chans) // 16) * 16
     row_grad, bias_grad, copies = pl.pallas_call(
         lambda *refs: col_sum_kernel(n_row, n_col, cols, *refs),
-        out_shape=(sds((16, CH)), sds((1, CH)), sds((n_row, end, LANES))),
+        out_shape=(sds((16, CH)), sds((1, CH)), sds((n_row, end, LANES), BF16)),
+        scratch_shapes=[pltpu.VMEM((end, LANES), F32)],
         compiler_params=PARAMS,
     )(got)
     got = lax.all_to_all(copies, "row", 0, 0)

time: 67.4 us -> 66.5 us (0.987); the launches traced: 66.2 us -> 66 us
  blocking collectives: 43.5 us -> 41.9 us
  local copies, waits for them, and re-layouts: 5.53 us -> 6.4 us
    unnamed x12 -> x16, local copies, waits for them, and re-layouts: 1.52 us -> 6.4 us
    another operation x2 -> x0, local copies, waits for them, and re-layouts: 1.4 us -> none  [shards(): w2 = jnp.stack([padded[1:], padded[:-1]], axis=3).reshape(4 * CH, 6 * CH)]
    transpose x2 -> x0, local copies, waits for them, and re-layouts: 1.17 us -> none  [the longest x1 1.04 us: shards(): k1c = jnp.transpose(conv_one, (0, 2, 1, 3)).reshape(3 * CH, 3 * CH)]
    broadcast_in_dim x1 -> x0, local copies, waits for them, and re-layouts: 0.75 us -> none  [shards(): bias_one[:, None]]
    all_to_all x1, blocking collectives: 18 us -> 17.3 us  [shards(): got = lax.all_to_all(copies, 'col', 0, 0)]
    reshape x4 -> x0, local copies, waits for them, and re-layouts: 0.69 us -> none  [the longest x2 0.26 us: shards(): k1c = jnp.transpose(conv_one, (0, 2, 1, 3)).reshape(3 * CH, 3 * CH)]
  transfers between devices with their start and end apart: 2 -> 2, of which waited for: 1 -> 1; matrix products, arithmetic and copies ran while one was open for 6% -> 0% of each run, Pallas kernels for 2% -> 2%
where the time goes in v3:
time: 66.5 us; the launch traced here: 66 us
  blocking collectives  41.9 us (63%)
  starting transfers between devices  7.75 us (12%)
  Pallas kernels  6.77 us (10%)
  local copies, waits for them, and re-layouts  6.4 us (10%)
  waiting for transfers between devices  2.44 us (4%)
  between operations  0.68 us (1%)
    all_to_all x1, blocking collectives, shards(): got = lax.all_to_all(copies, 'col', 0, 0)  17.3 us
    all_to_all x1, blocking collectives, shards(): got = lax.all_to_all(chunks, 'row', 0, 0)  12.9 us
    all_to_all x1, blocking collectives, shards(): got = lax.all_to_all(copies, 'row', 0, 0)  11.8 us
    ppermute x1, starting transfers between devices, shards(): lax.ppermute(strip, ('row', 'col'), [(target, source) for source, target...  7.75 us
    unnamed x16, local copies, waits for them, and re-layouts  6.4 us
    pallas_call x1, Pallas kernels, shards(): pl.pallas_call(lambda *refs: main_kernel(n_row, n_col, *refs), out_shape=...  3.67 us
    ppermute x1, waiting for transfers between devices, shards(): prev = lax.ppermute(strip, ('row', 'col'), pairs)  2.43 us
    pallas_call x1, Pallas kernels, shards(): pl.pallas_call(lambda *refs: own_kernel(n_col, *refs), out_shape=(sds((3,...  1.45 us
  transfers between devices with their start and end apart: 2, of which 1 were waited for; matrix products, arithmetic and copies ran while one was open for 0% of the time, Pallas kernels for 2%

profile of v3, /device:TPU:1, one launch (start us, length us, event | category | flops | bytes accessed | tf_op | source)
XLA Modules:
  0.0 66.0 jit_solution(9449509183224938757)
XLA Ops:
  0.6 0.0 copy-start.3
  0.6 0.7 %copy-done.3 = bf16[256,64]{0,1:T(8,128)(2,1)S(1)} copy-done((bf16[256,64]{0,1:T(8,128)(2,1)S(1)}, bf16[256,64]{0,1:T(8,128)(2,1)}, u32[]{:S(2)}) %copy-start.3) | copy-done | bytes 32792
  1.4 0.0 copy-start.5
  1.4 0.7 %copy-done.5 = bf16[16,64]{1,0:T(8,128)(2,1)S(1)} copy-done((bf16[16,64]{1,0:T(8,128)(2,1)S(1)}, bf16[16,64]{1,0:T(8,128)(2,1)}, u32[]{:S(2)}) %copy-start.5) | copy-done | bytes 2072
  2.1 7.7 %collective-permute-start.1 = (bf16[80,128]{1,0:T(8,128)(2,1)S(1)}, bf16[80,128]{1,0:T(8,128)(2,1)S(1)}, u32[]{:S(2)}, u32[]{:S(2)}) collective-permute-start(bf16[80,128]{1,0:T(8,128)(2,1)S(1)} %shard_map.101), channel_id=1, source_target_pairs={{9,0},{10,1},{11,2},{12,3},{13,4},{14,5},{15,6},{8,7},{17,8},{18,9... | collective-permute-start | bytes 61448 | tf_op jit(solution)/shard_map/ppermute | solution.py:339
  9.9 0.0 collective-permute-start
  9.9 0.0 copy-start
  9.9 1.0 %copy-done = bf16[64,16,256]{2,1,0:T(8,128)(2,1)S(1)} copy-done((bf16[64,16,256]{2,1,0:T(8,128)(2,1)S(1)}, bf16[64,16,256]{2,1,0:T(8,128)(2,1)}, u32[]{:S(2)}) %copy-start) | copy-done | bytes 524312
  10.9 0.0 copy-start.1
  10.9 0.9 %copy-done.1 = bf16[3,3,64,64]{3,2,1,0:T(8,128)(2,1)S(1)} copy-done((bf16[3,3,64,64]{3,2,1,0:T(8,128)(2,1)S(1)}, bf16[3,3,64,64]{3,2,1,0:T(8,128)(2,1)}, u32[]{:S(2)}) %copy-start.1) | copy-done | bytes 73752
  11.8 0.0 copy-start.2
  11.8 0.9 %copy-done.2 = bf16[3,3,64,64]{3,2,1,0:T(8,128)(2,1)S(1)} copy-done((bf16[3,3,64,64]{3,2,1,0:T(8,128)(2,1)S(1)}, bf16[3,3,64,64]{3,2,1,0:T(8,128)(2,1)}, u32[]{:S(2)}) %copy-start.2) | copy-done | bytes 73752
  12.7 0.0 copy-start.7
  12.8 0.7 copy-done.7
  13.4 1.5 %shard_map.102 = (bf16[3,128,2176]{2,1,0:T(8,128)(2,1)S(1)}, f32[256,2176]{1,0:T(8,128)S(1)}, f32[8,128]{1,0:T(8,128)S(1)}, f32[64,256]{1,0:T(8,128)S(1)}, bf16[...) custom-call(bf16[64,16,256]{2,1,0:T(8,128)(2,1)S(1)} %copy-done, ...), custom_call_target="tpu_custom_call" | custom-call | tf_op jit(solution)/shard_map/pallas_call | solution.py:341
  14.9 0.0 collective-permute-done.1.refs_1_
  14.9 2.4 %collective-permute-done.refs_0_ = bf16[80,128]{1,0:T(8,128)(2,1)S(1)} collective-permute-done((bf16[80,128]{1,0:T(8,128)(2,1)S(1)}, bf16[80,128]{1,0:T(8,128)(2,1)S(1)}, u32[]{:S(2)}, u32[]{:S(2)}) %collective-permute-start) | collective-permute-done | bytes 20512 | tf_op jit(solution)/shard_map/ppermute | solution.py:338
  17.3 0.0 copy-start.4
  17.3 0.8 %copy-done.4 = bf16[256,64]{0,1:T(8,128)(2,1)S(1)} copy-done((bf16[256,64]{0,1:T(8,128)(2,1)S(1)}, bf16[256,64]{0,1:T(8,128)(2,1)}, u32[]{:S(2)}) %copy-start.4) | copy-done | bytes 32792
  18.1 0.0 copy-start.6
  18.1 0.7 %copy-done.6 = bf16[16,64]{1,0:T(8,128)(2,1)S(1)} copy-done((bf16[16,64]{1,0:T(8,128)(2,1)S(1)}, bf16[16,64]{1,0:T(8,128)(2,1)}, u32[]{:S(2)}) %copy-start.6) | copy-done | bytes 2072
  18.8 3.7 %shard_map.103 = (bf16[32,32,128]{2,1,0:T(8,128)(2,1)S(1)}, f32[8,128]{1,0:T(8,128)S(1)}) custom-call(bf16[80,128]{1,0:T(8,128)(2,1)S(1)} %collective-permute-done.refs_0_, bf16[80,128]{1,0:T(8,128)(2,1)S(1)} %collective-permute-done.1.refs_1_, bf16[16,64]{1,0:T(8,128)(2,1)S(1)} %copy-done.6, bf16[64,256]{1,0:T(8,128)(2,1)S(1)} %bitcast.7, ...), custom_call_target="tpu_custom_call" | custom-call | tf_op jit(solution)/shard_map/pallas_call | solution.py:350
  22.4 12.9 %all_to_all.15.refs_0_ = bf16[32,32,128]{2,1,0:T(8,128)(2,1)S(1)} all-to-all(bf16[32,32,128]{2,1,0:T(8,128)(2,1)S(1)} %get-tuple-element.29), channel_id=1, replica_groups=mesh['row'=32,'col'=8] {'row'}, dimensions={0} | all-to-all | bytes 524288 | tf_op jit(solution)/shard_map/all_to_all | solution.py:362
  35.4 17.3 %all_to_all.16.refs_0_ = bf16[8,32,128]{2,1,0:T(8,128)(2,1)S(1)} all-to-all(bf16[8,32,128]{2,1,0:T(8,128)(2,1)S(1)} %shard_map.104), channel_id=1, replica_groups=mesh['row'=32,'col'=8] {'col'}, dimensions={0} | all-to-all | bytes 131072 | tf_op jit(solution)/shard_map/all_to_all | solution.py:368
  52.6 0.7 %shard_map.105 = (f32[16,64]{1,0:T(8,128)}, f32[1,64]{1,0:T(1,128)}, bf16[32,32,128]{2,1,0:T(8,128)(2,1)S(1)}) custom-call(bf16[8,32,128]{2,1,0:T(8,128)(2,1)S(1)} %all_to_all.16.refs_0_), custom_call_target="tpu_custom_call" | custom-call | tf_op jit(solution)/shard_map/pallas_call | solution.py:370
  53.3 11.8 %all_to_all.17.refs_0_ = bf16[32,32,128]{2,1,0:T(8,128)(2,1)S(1)} all-to-all(bf16[32,32,128]{2,1,0:T(8,128)(2,1)S(1)} %get-tuple-element.32), channel_id=1, replica_groups=mesh['row'=32,'col'=8] {'row'}, dimensions={0} | all-to-all | bytes 524288 | tf_op jit(solution)/shard_map/all_to_all | solution.py:376
  65.1 0.9 %shard_map.106 = (f32[64,256]{1,0:T(8,128)}, f32[576,64]{1,0:T(8,128)}, f32[576,64]{1,0:T(8,128)}) custom-call(bf16[32,32,128]{2,1,0:T(8,128)(2,1)S(1)} %all_to_all.17.refs_0_), custom_call_target="tpu_custom_call" | custom-call | tf_op jit(solution)/shard_map/pallas_call | solution.py:377
  (2 shorter events, 0.1 us)
Async XLA Ops:
  0.6 0.8 %copy-start.3 = (bf16[256,64]{0,1:T(8,128)(2,1)S(1)}, bf16[256,64]{0,1:T(8,128)(2,1)}, u32[]{:S(2)}) copy-start(bf16[256,64]{0,1:T(8,128)(2,1)} %param.8) | copy-start | bytes 98308
  1.4 0.7 %copy-start.5 = (bf16[16,64]{1,0:T(8,128)(2,1)S(1)}, bf16[16,64]{1,0:T(8,128)(2,1)}, u32[]{:S(2)}) copy-start(bf16[16,64]{1,0:T(8,128)(2,1)} %refs_2_.3) | copy-start | bytes 6148
  2.1 12.7 %collective-permute-start.1 = (bf16[80,128]{1,0:T(8,128)(2,1)S(1)}, bf16[80,128]{1,0:T(8,128)(2,1)S(1)}, u32[]{:S(2)}, u32[]{:S(2)}) collective-permute-start(bf16[80,128]{1,0:T(8,128)(2,1)S(1)} %shard_map.101), channel_id=1, source_target_pairs={{9,0},{10,1},{11,2},{12,3},{13,4},{14,5},{15,6},{8,7},{17,8},{18,9... | collective-permute-start | bytes 61448 | tf_op jit(solution)/shard_map/ppermute | solution.py:339
  9.9 7.4 %collective-permute-start = (bf16[80,128]{1,0:T(8,128)(2,1)S(1)}, bf16[80,128]{1,0:T(8,128)(2,1)S(1)}, u32[]{:S(2)}, u32[]{:S(2)}) collective-permute-start(bf16[80,128]{1,0:T(8,128)(2,1)S(1)} %shard_map.101), channel_id=1, source_target_pairs={{0,9},{1,10},{2,11},{3,12},{4,13},{5,14},{6,15},{7,8},{8,17},{9,18... | collective-permute-start | bytes 61448 | tf_op jit(solution)/shard_map/ppermute | solution.py:338
  9.9 1.0 %copy-start = (bf16[64,16,256]{2,1,0:T(8,128)(2,1)S(1)}, bf16[64,16,256]{2,1,0:T(8,128)(2,1)}, u32[]{:S(2)}) copy-start(bf16[64,16,256]{2,1,0:T(8,128)(2,1)} %refs_0_.1) | copy-start | bytes 1572868
  10.9 0.9 %copy-start.1 = (bf16[3,3,64,64]{3,2,1,0:T(8,128)(2,1)S(1)}, bf16[3,3,64,64]{3,2,1,0:T(8,128)(2,1)}, u32[]{:S(2)}) copy-start(bf16[3,3,64,64]{3,2,1,0:T(8,128)(2,1)} %refs_1_.1) | copy-start | bytes 221188
  11.8 0.9 %copy-start.2 = (bf16[3,3,64,64]{3,2,1,0:T(8,128)(2,1)S(1)}, bf16[3,3,64,64]{3,2,1,0:T(8,128)(2,1)}, u32[]{:S(2)}) copy-start(bf16[3,3,64,64]{3,2,1,0:T(8,128)(2,1)} %refs_2_.2) | copy-start | bytes 221188
  12.7 0.7 copy-start.7
  17.3 0.8 %copy-start.4 = (bf16[256,64]{0,1:T(8,128)(2,1)S(1)}, bf16[256,64]{0,1:T(8,128)(2,1)}, u32[]{:S(2)}) copy-start(bf16[256,64]{0,1:T(8,128)(2,1)} %param.8) | copy-start | bytes 98308
  18.1 0.7 %copy-start.6 = (bf16[16,64]{1,0:T(8,128)(2,1)S(1)}, bf16[16,64]{1,0:T(8,128)(2,1)}, u32[]{:S(2)}) copy-start(bf16[16,64]{1,0:T(8,128)(2,1)} %refs_2_.3) | copy-start | bytes 6148

commit v4 on v3

--- a/solution.py
+++ b/solution.py
@@ -73,10 +73,22 @@
 
 
 def own_kernel(
-    n_col, grad_ref, one_ref, two_ref, bias_ref,
-    x_ref, back_ref, grad_rows_ref, grad_cols_ref, ind_ref, k1c_ref, k1f_ref, bias_col_ref, rows_scr,
+    n_col, grad_hbm, one_hbm, two_hbm, bias_hbm, row_hbm, col_hbm,
+    x_ref, back_ref, grad_rows_ref, grad_cols_ref, ind_ref, k1c_ref, k1f_ref, bias_col_ref, row_ref, col_ref,
+    rows_scr, grad_ref, one_ref, two_ref, bias_ref, sems,
 ):
     cols = grad_ref.shape[2]
+    pairs = (
+        (one_hbm, one_ref), (two_hbm, two_ref), (bias_hbm, bias_ref), (row_hbm, row_ref), (col_hbm, col_ref),
+        (grad_hbm, grad_ref),
+    )
+    copies = [pltpu.make_async_copy(source, target, sems.at[k]) for k, (source, target) in enumerate(pairs)]
+    for copy in copies:
+        copy.start()
+    hits = indicator(cols, n_col)
+    ind_ref[...] = hits
+    for copy in copies[:-1]:
+        copy.wait()
     one = [[one_ref[a, b].astype(F32) for b in range(3)] for a in range(3)]
     for k in range(3):
         rows = slice(CH * k, CH * (k + 1))
@@ -94,6 +106,7 @@
     ).astype(BF16)
     bias = jnp.concatenate([bias_ref[...], jnp.zeros((1, LANES - CH), F32)], axis=1)
     bias_col_ref[...] = jnp.broadcast_to(bias, (8, LANES)).T[:CH, :]
+    copies[-1].wait()
     lane = lax.broadcasted_iota(jnp.int32, (CH, cols), 1)
     edge_lane = lax.broadcasted_iota(jnp.int32, (CH, LANES), 1)
     for piece in range(cols // LANES):
@@ -120,8 +133,6 @@
         x_ref[1, rows, 8 * cols :] = jnp.zeros((CH, LANES), BF16)
         x_ref[2, rows, 8 * cols :] = right.astype(BF16)
     grad_cols_ref[...] = col_sum
-    hits = indicator(cols, n_col)
-    ind_ref[...] = hits
     row = lax.broadcasted_iota(jnp.int32, (8, 8 * cols), 0)
     span = lax.broadcasted_iota(jnp.int32, (8, 8 * cols), 1) // cols
     grad_rows_ref[...] = dot(jnp.where(row == span, 1.0, 0.0).astype(BF16), x_ref[1, :, : 8 * cols], NT)
@@ -130,8 +141,8 @@
 
 
 def main_kernel(
-    n_row, n_col, prev_ref, next_ref, row_ref, col_ref,
-    x_ref, back_ref, grad_rows_ref, grad_cols_ref, ind_ref, k1c_ref, k1f_ref, bias_ref,
+    n_row, n_col, prev_ref, next_ref,
+    x_ref, back_ref, grad_rows_ref, grad_cols_ref, ind_ref, k1c_ref, k1f_ref, bias_ref, row_ref, col_ref,
     out_ref, own_ref, pre_scr, act_scr, inner_scr, w_scr, chunk_scr,
 ):
     cols = col_ref.shape[1]
@@ -320,6 +331,10 @@
     cols = grad_out.shape[2]
     weights, chans, sums_end = chunk_rows(n_row)
     places = 8 * cols + LANES
+    grad_out, row_feat, col_turned, conv_one, conv_two, bias_row = (
+        pltpu.with_memory_space_constraint(x, pltpu.HBM)
+        for x in (grad_out, row_feat, col_feat.T, conv_one, conv_two, bias_one.reshape(1, CH))
+    )
     strip = pl.pallas_call(
         pack_kernel,
         out_shape=sds((16 + CH, LANES), BF16),
@@ -331,7 +346,7 @@
             pltpu.SemaphoreType.DMA,
         ],
         compiler_params=PARAMS,
-    )(row_feat, col_feat.T)
+    )(row_feat, col_turned)
     pairs = [
         (r * n_col + c, (r + 1) % n_row * n_col + (c + 1) % n_col) for r in range(n_row) for c in range(n_col)
     ]
@@ -343,10 +358,19 @@
         out_shape=(
             sds((3, 2 * CH, places), BF16), sds((4 * CH, places)), sds((8, 2 * CH)), sds((CH, cols)),
             sds((24, places), BF16), sds((3 * CH, 3 * CH), BF16), sds((3 * CH, 3 * CH), BF16), sds((CH, 8)),
+            sds((16, CH), BF16), sds((CH, cols), BF16),
         ),
-        scratch_shapes=[pltpu.VMEM((cols // LANES, CH * 16, LANES), F32)],
-        compiler_params=PARAMS,
-    )(grad_out, conv_one, conv_two, bias_one.reshape(1, CH))
+        in_specs=[pl.BlockSpec(memory_space=pltpu.HBM)] * 6,
+        scratch_shapes=[
+            pltpu.VMEM((cols // LANES, CH * 16, LANES), F32),
+            pltpu.VMEM(grad_out.shape, BF16),
+            pltpu.VMEM(conv_one.shape, BF16),
+            pltpu.VMEM(conv_two.shape, BF16),
+            pltpu.VMEM((1, CH), F32),
+            pltpu.SemaphoreType.DMA((6,)),
+        ],
+        compiler_params=PARAMS,
+    )(grad_out, conv_one, conv_two, bias_row, row_feat, col_turned)
     chunks, own = pl.pallas_call(
         lambda *refs: main_kernel(n_row, n_col, *refs),
         out_shape=(sds((n_row, sums_end + 8, LANES), BF16), sds((8, LANES))),
@@ -358,7 +382,7 @@
             pltpu.VMEM((n_row, sums_end + 8, LANES), F32),
         ],
         compiler_params=PARAMS,
-    )(prev, nxt, row_feat, col_feat.T, *held)
+    )(prev, nxt, *held)
     got = lax.all_to_all(chunks, "row", 0, 0)
     copies = pl.pallas_call(
         lambda *refs: row_sum_kernel(n_row, n_col, *refs),

time: 66.5 us -> 62.7 us (0.943)
  local copies, waits for them, and re-layouts: 6.4 us -> 0 us
  waiting for transfers between devices: 2.44 us -> 4.77 us
  Pallas kernels: 6.77 us -> 8.69 us
  blocking collectives: 41.9 us -> 40.5 us
    unnamed x16 -> x0, local copies, waits for them, and re-layouts: 6.4 us -> none
    ppermute x1, waiting for transfers between devices: 2.43 us -> 4.77 us  [shards(): prev = lax.ppermute(strip, ('row', 'col'), pairs)]
    all_to_all x1, blocking collectives: 12.9 us -> 11 us  [shards(): got = lax.all_to_all(chunks, 'row', 0, 0)]
    pallas_call x1, Pallas kernels: 1.45 us -> 2.63 us  [shards(): pl.pallas_call(lambda *refs: own_kernel(n_col, *refs), out_shape=(sds((3,...]
    all_to_all x1, blocking collectives: 17.3 us -> 18.2 us  [shards(): got = lax.all_to_all(copies, 'col', 0, 0)]
    pallas_call x1, Pallas kernels: 0.05 us -> 0.8 us  [shards(): pl.pallas_call(pack_kernel, out_shape=sds((16 + CH, LANES), BF16), in_spe...]
  transfers between devices with their start and end apart: 2 -> 2, of which waited for: 1 -> 1; matrix products, arithmetic and copies ran while one was open for 0% -> 0% of each run, Pallas kernels for 2% -> 4%
where the time goes in v4:
time: 62.7 us; the launch traced here: 62.4 us
  blocking collectives  40.5 us (65%)
  Pallas kernels  8.69 us (14%)
  starting transfers between devices  7.75 us (12%)
  waiting for transfers between devices  4.77 us (8%)
  between operations  0.67 us (1%)
    all_to_all x1, blocking collectives, shards(): got = lax.all_to_all(copies, 'col', 0, 0)  18.2 us
    all_to_all x1, blocking collectives, shards(): got = lax.all_to_all(copies, 'row', 0, 0)  11.3 us
    all_to_all x1, blocking collectives, shards(): got = lax.all_to_all(chunks, 'row', 0, 0)  11 us
    ppermute x1, starting transfers between devices, shards(): lax.ppermute(strip, ('row', 'col'), [(target, source) for source, target...  7.75 us
    ppermute x1, waiting for transfers between devices, shards(): prev = lax.ppermute(strip, ('row', 'col'), pairs)  4.77 us
    pallas_call x1, Pallas kernels, shards(): pl.pallas_call(lambda *refs: main_kernel(n_row, n_col, *refs), out_shape=...  3.66 us
    pallas_call x1, Pallas kernels, shards(): pl.pallas_call(lambda *refs: own_kernel(n_col, *refs), out_shape=(sds((3,...  2.63 us
  transfers between devices with their start and end apart: 2, of which 1 were waited for; matrix products, arithmetic and copies ran while one was open for 0% of the time, Pallas kernels for 4%

profile of v4, /device:TPU:1, one launch (start us, length us, event | category | flops | bytes accessed | tf_op | source)
XLA Modules:
  0.0 62.4 jit_solution(14327323168493917479)
XLA Ops:
  0.6 0.8 %shard_map.101 = bf16[80,128]{1,0:T(8,128)(2,1)S(1)} custom-call(bf16[16,64]{1,0:T(8,128)(2,1)} %refs_4_.1, bf16[64,256]{1,0:T(8,128)(2,1)} %bitcast.6), custom_call_target="tpu_custom_call" | custom-call | tf_op jit(solution)/shard_map/pallas_call | solution.py:338
  1.4 7.7 %collective-permute-start.1 = (bf16[80,128]{1,0:T(8,128)(2,1)S(1)}, bf16[80,128]{1,0:T(8,128)(2,1)S(1)}, u32[]{:S(2)}, u32[]{:S(2)}) collective-permute-start(bf16[80,128]{1,0:T(8,128)(2,1)S(1)} %shard_map.101), channel_id=1, source_target_pairs={{9,0},{10,1},{11,2},{12,3},{13,4},{14,5},{15,6},{8,7},{17,8},{18,9... | collective-permute-start | bytes 61448 | tf_op jit(solution)/shard_map/ppermute | solution.py:354
  9.2 0.0 collective-permute-start
  9.2 2.6 %shard_map.102 = (bf16[3,128,2176]{2,1,0:T(8,128)(2,1)S(1)}, f32[256,2176]{1,0:T(8,128)S(1)}, f32[8,128]{1,0:T(8,128)S(1)}, f32[64,256]{1,0:T(8,128)S(1)}, bf16[...) custom-call(bf16[64,16,256]{2,1,0:T(8,128)(2,1)} %refs_0_.1, ...), custom_call_target="tpu_custom_call" | custom-call | tf_op jit(solution)/shard_map/pallas_call | solution.py:356
  11.8 0.0 collective-permute-done.1.refs_1_
  11.8 4.8 %collective-permute-done.refs_0_ = bf16[80,128]{1,0:T(8,128)(2,1)S(1)} collective-permute-done((bf16[80,128]{1,0:T(8,128)(2,1)S(1)}, bf16[80,128]{1,0:T(8,128)(2,1)S(1)}, u32[]{:S(2)}, u32[]{:S(2)}) %collective-permute-start) | collective-permute-done | bytes 20512 | tf_op jit(solution)/shard_map/ppermute | solution.py:353
  16.6 3.7 %shard_map.103 = (bf16[32,32,128]{2,1,0:T(8,128)(2,1)S(1)}, f32[8,128]{1,0:T(8,128)S(1)}) custom-call(bf16[80,128]{1,0:T(8,128)(2,1)S(1)} %collective-permute-done.refs_0_, bf16[80,128]{1,0:T(8,128)(2,1)S(1)} %collective-permute-done.1.refs_1_, bf16[3,128,2176]{2,1,0:T(8,128)(2,1)S(1)} %get-tuple-element.23.refs_2_, ...), custom_call_target="tpu_custom_call" | custom-call | tf_op jit(solution)/shard_map/pallas_call | solution.py:374
  20.3 11.0 %all_to_all.15.refs_0_ = bf16[32,32,128]{2,1,0:T(8,128)(2,1)S(1)} all-to-all(bf16[32,32,128]{2,1,0:T(8,128)(2,1)S(1)} %get-tuple-element.33), channel_id=1, replica_groups=mesh['row'=32,'col'=8] {'row'}, dimensions={0} | all-to-all | bytes 524288 | tf_op jit(solution)/shard_map/all_to_all | solution.py:386
  31.3 18.2 %all_to_all.16.refs_0_ = bf16[8,32,128]{2,1,0:T(8,128)(2,1)S(1)} all-to-all(bf16[8,32,128]{2,1,0:T(8,128)(2,1)S(1)} %shard_map.104), channel_id=1, replica_groups=mesh['row'=32,'col'=8] {'col'}, dimensions={0} | all-to-all | bytes 131072 | tf_op jit(solution)/shard_map/all_to_all | solution.py:392
  49.5 0.7 %shard_map.105 = (f32[16,64]{1,0:T(8,128)}, f32[1,64]{1,0:T(1,128)}, bf16[32,32,128]{2,1,0:T(8,128)(2,1)S(1)}) custom-call(bf16[8,32,128]{2,1,0:T(8,128)(2,1)S(1)} %all_to_all.16.refs_0_), custom_call_target="tpu_custom_call" | custom-call | tf_op jit(solution)/shard_map/pallas_call | solution.py:394
  50.2 11.3 %all_to_all.17.refs_0_ = bf16[32,32,128]{2,1,0:T(8,128)(2,1)S(1)} all-to-all(bf16[32,32,128]{2,1,0:T(8,128)(2,1)S(1)} %get-tuple-element.36), channel_id=1, replica_groups=mesh['row'=32,'col'=8] {'row'}, dimensions={0} | all-to-all | bytes 524288 | tf_op jit(solution)/shard_map/all_to_all | solution.py:400
  61.5 0.9 %shard_map.106 = (f32[64,256]{1,0:T(8,128)}, f32[576,64]{1,0:T(8,128)}, f32[576,64]{1,0:T(8,128)}) custom-call(bf16[32,32,128]{2,1,0:T(8,128)(2,1)S(1)} %all_to_all.17.refs_0_), custom_call_target="tpu_custom_call" | custom-call | tf_op jit(solution)/shard_map/pallas_call | solution.py:401
  (1 shorter events, 0.0 us)
Async XLA Ops:
  1.4 10.4 %collective-permute-start.1 = (bf16[80,128]{1,0:T(8,128)(2,1)S(1)}, bf16[80,128]{1,0:T(8,128)(2,1)S(1)}, u32[]{:S(2)}, u32[]{:S(2)}) collective-permute-start(bf16[80,128]{1,0:T(8,128)(2,1)S(1)} %shard_map.101), channel_id=1, source_target_pairs={{9,0},{10,1},{11,2},{12,3},{13,4},{14,5},{15,6},{8,7},{17,8},{18,9... | collective-permute-start | bytes 61448 | tf_op jit(solution)/shard_map/ppermute | solution.py:354
  9.2 7.4 %collective-permute-start = (bf16[80,128]{1,0:T(8,128)(2,1)S(1)}, bf16[80,128]{1,0:T(8,128)(2,1)S(1)}, u32[]{:S(2)}, u32[]{:S(2)}) collective-permute-start(bf16[80,128]{1,0:T(8,128)(2,1)S(1)} %shard_map.101), channel_id=1, source_target_pairs={{0,9},{1,10},{2,11},{3,12},{4,13},{5,14},{6,15},{7,8},{8,17},{9,18... | collective-permute-start | bytes 61448 | tf_op jit(solution)/shard_map/ppermute | solution.py:353

commit v5 on v4

--- a/solution.py
+++ b/solution.py
@@ -141,7 +141,7 @@
 
 
 def main_kernel(
-    n_row, n_col, prev_ref, next_ref,
+    n_row, n_col, twin_ref, row_side_ref, col_side_ref,
     x_ref, back_ref, grad_rows_ref, grad_cols_ref, ind_ref, k1c_ref, k1f_ref, bias_ref, row_ref, col_ref,
     out_ref, own_ref, pre_scr, act_scr, inner_scr, w_scr, chunk_scr,
 ):
@@ -149,13 +149,15 @@
     top, bottom = off_edge("row", 0), off_edge("row", n_row - 1)
     left, right = off_edge("col", 0), off_edge("col", n_col - 1)
     edge_lane = lax.broadcasted_iota(jnp.int32, (CH, LANES), 1)
+    odd_row, odd_col = lax.axis_index("row") % 2 == 1, lax.axis_index("col") % 2 == 1
+    twin, other = twin_ref[:16, :CH].astype(F32), row_side_ref[:16, :CH].astype(F32)
     row_ext = jnp.concatenate(
-        [top * prev_ref[:16, :CH].astype(F32), row_ref[...].astype(F32), bottom * next_ref[:16, :CH].astype(F32)],
-        axis=0,
+        [jnp.where(odd_row, twin, other), row_ref[...].astype(F32), jnp.where(odd_row, other, twin)], axis=0
     )
     row_cat = jnp.concatenate([row_ext[8 * a : 8 * a + 32] for a in range(3)], axis=1).astype(BF16)
+    twin, other = twin_ref[16:, :].astype(F32), col_side_ref[16:, :].astype(F32)
     col_ext = jnp.concatenate(
-        [left * prev_ref[16:, :].astype(F32), col_ref[...].astype(F32), right * next_ref[16:, :].astype(F32)], axis=1
+        [jnp.where(odd_col, twin, other), col_ref[...].astype(F32), jnp.where(odd_col, other, twin)], axis=1
     )
     taps = []
     for tap in range(3):
@@ -347,11 +349,15 @@
         ],
         compiler_params=PARAMS,
     )(row_feat, col_turned)
-    pairs = [
-        (r * n_col + c, (r + 1) % n_row * n_col + (c + 1) % n_col) for r in range(n_row) for c in range(n_col)
-    ]
-    prev = lax.ppermute(strip, ("row", "col"), pairs)
-    nxt = lax.ppermute(strip, ("row", "col"), [(target, source) for source, target in pairs])
+    both = [(r * n_col + c, (r ^ 1) * n_col + (c ^ 1)) for r in range(n_row) for c in range(n_col)]
+
+    def others(count):
+        ups = [(k, k + 1) for k in range(1, count - 1, 2)]
+        return ups + [(high, low) for low, high in ups]
+
+    twin = lax.ppermute(strip, ("row", "col"), both)
+    row_side = lax.ppermute(strip, "row", others(n_row))
+    col_side = lax.ppermute(strip, "col", others(n_col))
 
     held = pl.pallas_call(
         lambda *refs: own_kernel(n_col, *refs),
@@ -382,7 +388,7 @@
             pltpu.VMEM((n_row, sums_end + 8, LANES), F32),
         ],
         compiler_params=PARAMS,
-    )(prev, nxt, *held)
+    )(twin, row_side, col_side, *held)
     got = lax.all_to_all(chunks, "row", 0, 0)
     copies = pl.pallas_call(
         lambda *refs: row_sum_kernel(n_row, n_col, *refs),

time: 62.7 us -> 63.9 us (1.019)
  blocking collectives: 40.5 us -> 46.6 us
  waiting for transfers between devices: 4.77 us -> 0.53 us
  starting transfers between devices: 7.75 us -> 7.04 us
    all_to_all x1, blocking collectives: 11 us -> 19.8 us  [shards(): got = lax.all_to_all(chunks, 'row', 0, 0)]
    ppermute x2 -> x3, waiting for transfers between devices: 4.77 us -> 0.53 us  [the longest x1 0.52 us: shards(): twin = lax.ppermute(strip, ('row', 'col'), both)]
    all_to_all x1, blocking collectives: 18.2 us -> 15.4 us  [shards(): got = lax.all_to_all(copies, 'col', 0, 0)]
    ppermute x2 -> x3, starting transfers between devices: 7.75 us -> 7.04 us  [the longest x1 6.29 us: shards(): col_side = lax.ppermute(strip, 'col', others(n_col))]
  transfers between devices with their start and end apart: 2 -> 3, of which waited for: 1 -> 1; matrix products, arithmetic and copies ran while one was open for 0% -> 0% of each run, Pallas kernels for 4% -> 4%
where the time goes in v5:
time: 63.9 us; the launch traced here: 63.6 us
  blocking collectives  46.6 us (73%)
  Pallas kernels  8.69 us (14%)
  starting transfers between devices  7.04 us (11%)
  between operations  0.7 us (1%)
    all_to_all x1, blocking collectives, shards(): got = lax.all_to_all(chunks, 'row', 0, 0)  19.8 us
    all_to_all x1, blocking collectives, shards(): got = lax.all_to_all(copies, 'col', 0, 0)  15.4 us
    all_to_all x1, blocking collectives, shards(): got = lax.all_to_all(copies, 'row', 0, 0)  11.4 us
    ppermute x1, starting transfers between devices, shards(): col_side = lax.ppermute(strip, 'col', others(n_col))  6.29 us
    pallas_call x1, Pallas kernels, shards(): pl.pallas_call(lambda *refs: main_kernel(n_row, n_col, *refs), out_shape=...  3.65 us
    pallas_call x1, Pallas kernels, shards(): pl.pallas_call(lambda *refs: own_kernel(n_col, *refs), out_shape=(sds((3,...  2.64 us
  transfers between devices with their start and end apart: 3, of which 1 were waited for; matrix products, arithmetic and copies ran while one was open for 0% of the time, Pallas kernels for 4%

profile of v5, /device:TPU:1, one launch (start us, length us, event | category | flops | bytes accessed | tf_op | source)
XLA Modules:
  0.0 63.6 jit_solution(6482370345933040217)
XLA Ops:
  0.6 0.8 %shard_map.101 = bf16[80,128]{1,0:T(8,128)(2,1)S(1)} custom-call(bf16[16,64]{1,0:T(8,128)(2,1)} %refs_4_.1, bf16[64,256]{1,0:T(8,128)(2,1)} %bitcast.6), custom_call_target="tpu_custom_call" | custom-call | tf_op jit(solution)/shard_map/pallas_call | solution.py:340
  1.4 6.3 %collective-permute-start.2 = (bf16[80,128]{1,0:T(8,128)(2,1)S(1)}, bf16[80,128]{1,0:T(8,128)(2,1)S(1)}, u32[]{:S(2)}, u32[]{:S(2)}) collective-permute-start(bf16[80,128]{1,0:T(8,128)(2,1)S(1)} %shard_map.101), channel_id=1, source_target_pairs={{1,2},{3,4},{5,6},{2,1},{4,3},{6,5},{9,10},{11,12},{13,14},{10,9},... | collective-permute-start | bytes 61448 | tf_op jit(solution)/shard_map/ppermute | solution.py:360
  7.7 0.7 %collective-permute-start.1 = (bf16[80,128]{1,0:T(8,128)(2,1)S(1)}, bf16[80,128]{1,0:T(8,128)(2,1)S(1)}, u32[]{:S(2)}, u32[]{:S(2)}) collective-permute-start(bf16[80,128]{1,0:T(8,128)(2,1)S(1)} %shard_map.101), channel_id=1, source_target_pairs={{8,16},{24,32},{40,48},{56,64},{72,80},{88,96},{104,112},{120,128}... | collective-permute-start | bytes 61448 | tf_op jit(solution)/shard_map/ppermute | solution.py:359
  8.4 0.1 collective-permute-start
  8.5 2.6 %shard_map.102 = (bf16[3,128,2176]{2,1,0:T(8,128)(2,1)S(1)}, f32[256,2176]{1,0:T(8,128)S(1)}, f32[8,128]{1,0:T(8,128)S(1)}, f32[64,256]{1,0:T(8,128)S(1)}, bf16[...) custom-call(bf16[64,16,256]{2,1,0:T(8,128)(2,1)} %refs_0_.1, ...), custom_call_target="tpu_custom_call" | custom-call | tf_op jit(solution)/shard_map/pallas_call | solution.py:362
  11.2 0.0 collective-permute-done.2.refs_2_
  11.2 0.0 collective-permute-done.1.refs_1_
  11.2 0.5 collective-permute-done.refs_0_
  11.7 3.6 %shard_map.103 = (bf16[32,32,128]{2,1,0:T(8,128)(2,1)S(1)}, f32[8,128]{1,0:T(8,128)S(1)}) custom-call(bf16[80,128]{1,0:T(8,128)(2,1)S(1)} %collective-permute-done.refs_0_, bf16[80,128]{1,0:T(8,128)(2,1)S(1)} %collective-permute-done.1.refs_1_, bf16[80,128]{1,0:T(8,128)(2,1)S(1)} %collective-permute-done.2.refs_2_, ...), custom_call_target="tpu_custom_call" | custom-call | tf_op jit(solution)/shard_map/pallas_call | solution.py:380
  15.4 19.8 %all_to_all.15.refs_0_ = bf16[32,32,128]{2,1,0:T(8,128)(2,1)S(1)} all-to-all(bf16[32,32,128]{2,1,0:T(8,128)(2,1)S(1)} %get-tuple-element.33), channel_id=1, replica_groups=mesh['row'=32,'col'=8] {'row'}, dimensions={0} | all-to-all | bytes 524288 | tf_op jit(solution)/shard_map/all_to_all | solution.py:392
  35.2 15.4 %all_to_all.16.refs_0_ = bf16[8,32,128]{2,1,0:T(8,128)(2,1)S(1)} all-to-all(bf16[8,32,128]{2,1,0:T(8,128)(2,1)S(1)} %shard_map.104), channel_id=1, replica_groups=mesh['row'=32,'col'=8] {'col'}, dimensions={0} | all-to-all | bytes 131072 | tf_op jit(solution)/shard_map/all_to_all | solution.py:398
  50.6 0.7 %shard_map.105 = (f32[16,64]{1,0:T(8,128)}, f32[1,64]{1,0:T(1,128)}, bf16[32,32,128]{2,1,0:T(8,128)(2,1)S(1)}) custom-call(bf16[8,32,128]{2,1,0:T(8,128)(2,1)S(1)} %all_to_all.16.refs_0_), custom_call_target="tpu_custom_call" | custom-call | tf_op jit(solution)/shard_map/pallas_call | solution.py:400
  51.3 11.4 %all_to_all.17.refs_0_ = bf16[32,32,128]{2,1,0:T(8,128)(2,1)S(1)} all-to-all(bf16[32,32,128]{2,1,0:T(8,128)(2,1)S(1)} %get-tuple-element.36), channel_id=1, replica_groups=mesh['row'=32,'col'=8] {'row'}, dimensions={0} | all-to-all | bytes 524288 | tf_op jit(solution)/shard_map/all_to_all | solution.py:406
  62.7 0.9 %shard_map.106 = (f32[64,256]{1,0:T(8,128)}, f32[576,64]{1,0:T(8,128)}, f32[576,64]{1,0:T(8,128)}) custom-call(bf16[32,32,128]{2,1,0:T(8,128)(2,1)S(1)} %all_to_all.17.refs_0_), custom_call_target="tpu_custom_call" | custom-call | tf_op jit(solution)/shard_map/pallas_call | solution.py:407
  (1 shorter events, 0.0 us)
Async XLA Ops:
  1.4 9.7 %collective-permute-start.2 = (bf16[80,128]{1,0:T(8,128)(2,1)S(1)}, bf16[80,128]{1,0:T(8,128)(2,1)S(1)}, u32[]{:S(2)}, u32[]{:S(2)}) collective-permute-start(bf16[80,128]{1,0:T(8,128)(2,1)S(1)} %shard_map.101), channel_id=1, source_target_pairs={{1,2},{3,4},{5,6},{2,1},{4,3},{6,5},{9,10},{11,12},{13,14},{10,9},... | collective-permute-start | bytes 61448 | tf_op jit(solution)/shard_map/ppermute | solution.py:360
  7.7 3.4 %collective-permute-start.1 = (bf16[80,128]{1,0:T(8,128)(2,1)S(1)}, bf16[80,128]{1,0:T(8,128)(2,1)S(1)}, u32[]{:S(2)}, u32[]{:S(2)}) collective-permute-start(bf16[80,128]{1,0:T(8,128)(2,1)S(1)} %shard_map.101), channel_id=1, source_target_pairs={{8,16},{24,32},{40,48},{56,64},{72,80},{88,96},{104,112},{120,128}... | collective-permute-start | bytes 61448 | tf_op jit(solution)/shard_map/ppermute | solution.py:359
  8.4 3.3 %collective-permute-start = (bf16[80,128]{1,0:T(8,128)(2,1)S(1)}, bf16[80,128]{1,0:T(8,128)(2,1)S(1)}, u32[]{:S(2)}, u32[]{:S(2)}) collective-permute-start(bf16[80,128]{1,0:T(8,128)(2,1)S(1)} %shard_map.101), channel_id=1, source_target_pairs={{0,9},{1,8},{2,11},{3,10},{4,13},{5,12},{6,15},{7,14},{8,1},{9,0},... | collective-permute-start | bytes 61448 | tf_op jit(solution)/shard_map/ppermute | solution.py:358

commit v6 on v5

--- a/solution.py
+++ b/solution.py
@@ -141,7 +141,7 @@
 
 
 def main_kernel(
-    n_row, n_col, twin_ref, row_side_ref, col_side_ref,
+    n_row, n_col, twin_ref, far_ref,
     x_ref, back_ref, grad_rows_ref, grad_cols_ref, ind_ref, k1c_ref, k1f_ref, bias_ref, row_ref, col_ref,
     out_ref, own_ref, pre_scr, act_scr, inner_scr, w_scr, chunk_scr,
 ):
@@ -150,12 +150,12 @@
     left, right = off_edge("col", 0), off_edge("col", n_col - 1)
     edge_lane = lax.broadcasted_iota(jnp.int32, (CH, LANES), 1)
     odd_row, odd_col = lax.axis_index("row") % 2 == 1, lax.axis_index("col") % 2 == 1
-    twin, other = twin_ref[:16, :CH].astype(F32), row_side_ref[:16, :CH].astype(F32)
+    twin, other = twin_ref[:16, :CH].astype(F32), far_ref[:16, :CH].astype(F32) * (top * bottom)
     row_ext = jnp.concatenate(
         [jnp.where(odd_row, twin, other), row_ref[...].astype(F32), jnp.where(odd_row, other, twin)], axis=0
     )
     row_cat = jnp.concatenate([row_ext[8 * a : 8 * a + 32] for a in range(3)], axis=1).astype(BF16)
-    twin, other = twin_ref[16:, :].astype(F32), col_side_ref[16:, :].astype(F32)
+    twin, other = twin_ref[16:, :].astype(F32), far_ref[16:, :].astype(F32) * (left * right)
     col_ext = jnp.concatenate(
         [jnp.where(odd_col, twin, other), col_ref[...].astype(F32), jnp.where(odd_col, other, twin)], axis=1
     )
@@ -351,13 +351,14 @@
     )(row_feat, col_turned)
     both = [(r * n_col + c, (r ^ 1) * n_col + (c ^ 1)) for r in range(n_row) for c in range(n_col)]
 
-    def others(count):
-        ups = [(k, k + 1) for k in range(1, count - 1, 2)]
-        return ups + [(high, low) for low, high in ups]
-
+    def other(index, count):
+        return min(max(index + (1 if index % 2 else -1), 0), count - 1)
+
+    rest = [
+        (r * n_col + c, other(r, n_row) * n_col + other(c, n_col)) for r in range(n_row) for c in range(n_col)
+    ]
     twin = lax.ppermute(strip, ("row", "col"), both)
-    row_side = lax.ppermute(strip, "row", others(n_row))
-    col_side = lax.ppermute(strip, "col", others(n_col))
+    far = lax.ppermute(strip, ("row", "col"), rest)
 
     held = pl.pallas_call(
         lambda *refs: own_kernel(n_col, *refs),
@@ -388,7 +389,7 @@
             pltpu.VMEM((n_row, sums_end + 8, LANES), F32),
         ],
         compiler_params=PARAMS,
-    )(twin, row_side, col_side, *held)
+    )(twin, far, *held)
     got = lax.all_to_all(chunks, "row", 0, 0)
     copies = pl.pallas_call(
         lambda *refs: row_sum_kernel(n_row, n_col, *refs),

time: 63.9 us -> 62.6 us (0.980)
  starting transfers between devices: 7.04 us -> 6.38 us
    all_to_all x1, blocking collectives: 19.8 us -> 16.8 us  [shards(): got = lax.all_to_all(chunks, 'row', 0, 0)]
    all_to_all x1, blocking collectives: 15.4 us -> 17.8 us  [shards(): got = lax.all_to_all(copies, 'col', 0, 0)]
    ppermute x2 -> x1, starting transfers between devices: 6.95 us -> 6.29 us  [shards(): far = lax.ppermute(strip, ('row', 'col'), rest)]
  transfers between devices with their start and end apart: 3 -> 2, of which waited for: 1 -> 1; matrix products, arithmetic and copies ran while one was open for 0% -> 0% of each run, Pallas kernels for 4% -> 4%
where the time goes in v6:
time: 62.6 us; the launch traced here: 62.3 us
  blocking collectives  46 us (73%)
  Pallas kernels  8.7 us (14%)
  starting transfers between devices  6.38 us (10%)
  between operations  0.68 us (1%)
    all_to_all x1, blocking collectives, shards(): got = lax.all_to_all(copies, 'col', 0, 0)  17.8 us
    all_to_all x1, blocking collectives, shards(): got = lax.all_to_all(chunks, 'row', 0, 0)  16.8 us
    all_to_all x1, blocking collectives, shards(): got = lax.all_to_all(copies, 'row', 0, 0)  11.4 us
    ppermute x1, starting transfers between devices, shards(): far = lax.ppermute(strip, ('row', 'col'), rest)  6.29 us
    pallas_call x1, Pallas kernels, shards(): pl.pallas_call(lambda *refs: main_kernel(n_row, n_col, *refs), out_shape=...  3.66 us
    pallas_call x1, Pallas kernels, shards(): pl.pallas_call(lambda *refs: own_kernel(n_col, *refs), out_shape=(sds((3,...  2.64 us
  transfers between devices with their start and end apart: 2, of which 1 were waited for; matrix products, arithmetic and copies ran while one was open for 0% of the time, Pallas kernels for 4%

profile of v6, /device:TPU:1, one launch (start us, length us, event | category | flops | bytes accessed | tf_op | source)
XLA Modules:
  0.0 62.3 jit_solution(7481145358887508886)
XLA Ops:
  0.6 0.8 %shard_map.101 = bf16[80,128]{1,0:T(8,128)(2,1)S(1)} custom-call(bf16[16,64]{1,0:T(8,128)(2,1)} %refs_4_.1, bf16[64,256]{1,0:T(8,128)(2,1)} %bitcast.6), custom_call_target="tpu_custom_call" | custom-call | tf_op jit(solution)/shard_map/pallas_call | solution.py:340
  1.4 6.3 %collective-permute-start.1 = (bf16[80,128]{1,0:T(8,128)(2,1)S(1)}, bf16[80,128]{1,0:T(8,128)(2,1)S(1)}, u32[]{:S(2)}, u32[]{:S(2)}) collective-permute-start(bf16[80,128]{1,0:T(8,128)(2,1)S(1)} %shard_map.101), channel_id=1, source_target_pairs={{0,0},{1,2},{2,1},{3,4},{4,3},{5,6},{6,5},{7,7},{8,16},{9,18},{10,... | collective-permute-start | bytes 61448 | tf_op jit(solution)/shard_map/ppermute | solution.py:361
  7.7 0.1 collective-permute-start
  7.8 2.6 %shard_map.102 = (bf16[3,128,2176]{2,1,0:T(8,128)(2,1)S(1)}, f32[256,2176]{1,0:T(8,128)S(1)}, f32[8,128]{1,0:T(8,128)S(1)}, f32[64,256]{1,0:T(8,128)S(1)}, bf16[...) custom-call(bf16[64,16,256]{2,1,0:T(8,128)(2,1)} %refs_0_.1, ...), custom_call_target="tpu_custom_call" | custom-call | tf_op jit(solution)/shard_map/pallas_call | solution.py:363
  10.5 0.0 collective-permute-done.1.refs_1_
  10.5 0.5 collective-permute-done.refs_0_
  11.0 3.7 %shard_map.103 = (bf16[32,32,128]{2,1,0:T(8,128)(2,1)S(1)}, f32[8,128]{1,0:T(8,128)S(1)}) custom-call(bf16[80,128]{1,0:T(8,128)(2,1)S(1)} %collective-permute-done.refs_0_, bf16[80,128]{1,0:T(8,128)(2,1)S(1)} %collective-permute-done.1.refs_1_, bf16[3,128,2176]{2,1,0:T(8,128)(2,1)S(1)} %get-tuple-element.23.refs_2_, ...), custom_call_target="tpu_custom_call" | custom-call | tf_op jit(solution)/shard_map/pallas_call | solution.py:381
  14.7 16.8 %all_to_all.15.refs_0_ = bf16[32,32,128]{2,1,0:T(8,128)(2,1)S(1)} all-to-all(bf16[32,32,128]{2,1,0:T(8,128)(2,1)S(1)} %get-tuple-element.33), channel_id=1, replica_groups=mesh['row'=32,'col'=8] {'row'}, dimensions={0} | all-to-all | bytes 524288 | tf_op jit(solution)/shard_map/all_to_all | solution.py:393
  31.5 17.8 %all_to_all.16.refs_0_ = bf16[8,32,128]{2,1,0:T(8,128)(2,1)S(1)} all-to-all(bf16[8,32,128]{2,1,0:T(8,128)(2,1)S(1)} %shard_map.104), channel_id=1, replica_groups=mesh['row'=32,'col'=8] {'col'}, dimensions={0} | all-to-all | bytes 131072 | tf_op jit(solution)/shard_map/all_to_all | solution.py:399
  49.4 0.7 %shard_map.105 = (f32[16,64]{1,0:T(8,128)}, f32[1,64]{1,0:T(1,128)}, bf16[32,32,128]{2,1,0:T(8,128)(2,1)S(1)}) custom-call(bf16[8,32,128]{2,1,0:T(8,128)(2,1)S(1)} %all_to_all.16.refs_0_), custom_call_target="tpu_custom_call" | custom-call | tf_op jit(solution)/shard_map/pallas_call | solution.py:401
  50.0 11.4 %all_to_all.17.refs_0_ = bf16[32,32,128]{2,1,0:T(8,128)(2,1)S(1)} all-to-all(bf16[32,32,128]{2,1,0:T(8,128)(2,1)S(1)} %get-tuple-element.36), channel_id=1, replica_groups=mesh['row'=32,'col'=8] {'row'}, dimensions={0} | all-to-all | bytes 524288 | tf_op jit(solution)/shard_map/all_to_all | solution.py:407
  61.4 0.9 %shard_map.106 = (f32[64,256]{1,0:T(8,128)}, f32[576,64]{1,0:T(8,128)}, f32[576,64]{1,0:T(8,128)}) custom-call(bf16[32,32,128]{2,1,0:T(8,128)(2,1)S(1)} %all_to_all.17.refs_0_), custom_call_target="tpu_custom_call" | custom-call | tf_op jit(solution)/shard_map/pallas_call | solution.py:408
  (1 shorter events, 0.0 us)
Async XLA Ops:
  1.4 9.0 %collective-permute-start.1 = (bf16[80,128]{1,0:T(8,128)(2,1)S(1)}, bf16[80,128]{1,0:T(8,128)(2,1)S(1)}, u32[]{:S(2)}, u32[]{:S(2)}) collective-permute-start(bf16[80,128]{1,0:T(8,128)(2,1)S(1)} %shard_map.101), channel_id=1, source_target_pairs={{0,0},{1,2},{2,1},{3,4},{4,3},{5,6},{6,5},{7,7},{8,16},{9,18},{10,... | collective-permute-start | bytes 61448 | tf_op jit(solution)/shard_map/ppermute | solution.py:361
  7.7 3.3 %collective-permute-start = (bf16[80,128]{1,0:T(8,128)(2,1)S(1)}, bf16[80,128]{1,0:T(8,128)(2,1)S(1)}, u32[]{:S(2)}, u32[]{:S(2)}) collective-permute-start(bf16[80,128]{1,0:T(8,128)(2,1)S(1)} %shard_map.101), channel_id=1, source_target_pairs={{0,9},{1,8},{2,11},{3,10},{4,13},{5,12},{6,15},{7,14},{8,1},{9,0},... | collective-permute-start | bytes 61448 | tf_op jit(solution)/shard_map/ppermute | solution.py:360

commit v7 on v6

--- a/solution.py
+++ b/solution.py
@@ -17,12 +17,6 @@
 
 def dot(x, y, dims):
     return lax.dot_general(x, y, dims, preferred_element_type=F32)
-
-
-def dot_exact(x, y, dims):
-    return lax.dot_general(
-        x.astype(F32), y.astype(F32), dims, precision=lax.Precision.HIGHEST, preferred_element_type=F32
-    )
 
 
 def chunk_rows(n_row):
@@ -141,21 +135,21 @@
 
 
 def main_kernel(
-    n_row, n_col, twin_ref, far_ref,
+    n_row, n_col, row_twin_ref, col_twin_ref,
     x_ref, back_ref, grad_rows_ref, grad_cols_ref, ind_ref, k1c_ref, k1f_ref, bias_ref, row_ref, col_ref,
-    out_ref, own_ref, pre_scr, act_scr, inner_scr, w_scr, chunk_scr,
+    out_ref, own_ref, act_scr, inner_scr, w_scr, chunk_scr,
 ):
     cols = col_ref.shape[1]
     top, bottom = off_edge("row", 0), off_edge("row", n_row - 1)
     left, right = off_edge("col", 0), off_edge("col", n_col - 1)
     edge_lane = lax.broadcasted_iota(jnp.int32, (CH, LANES), 1)
     odd_row, odd_col = lax.axis_index("row") % 2 == 1, lax.axis_index("col") % 2 == 1
-    twin, other = twin_ref[:16, :CH].astype(F32), far_ref[:16, :CH].astype(F32) * (top * bottom)
+    twin, other = row_twin_ref[:16, :CH].astype(F32), col_twin_ref[:16, :CH].astype(F32) * (top * bottom)
     row_ext = jnp.concatenate(
         [jnp.where(odd_row, twin, other), row_ref[...].astype(F32), jnp.where(odd_row, other, twin)], axis=0
     )
     row_cat = jnp.concatenate([row_ext[8 * a : 8 * a + 32] for a in range(3)], axis=1).astype(BF16)
-    twin, other = twin_ref[16:, :].astype(F32), far_ref[16:, :].astype(F32) * (left * right)
+    twin, other = col_twin_ref[16:, :].astype(F32), row_twin_ref[16:, :].astype(F32) * (left * right)
     col_ext = jnp.concatenate(
         [jnp.where(odd_col, twin, other), col_ref[...].astype(F32), jnp.where(odd_col, other, twin)], axis=1
     )
@@ -173,42 +167,46 @@
     mid = mid + bias_ref[:, :1]
     col_part = [low + mid + high, top * low + mid + high, low + mid + bottom * high, low + mid + high]
     row_terms = dot(k1f_ref[...], row_cat, NT)
-    row_part = jnp.concatenate(
-        [
-            jnp.concatenate([row_terms[CH * b : CH * (b + 1), 8 * eb : 8 * eb + 8] for b in range(3)], axis=1)
-            for eb in range(4)
-        ],
-        axis=0,
-    )
-    hits = ind_ref[...]
-    pre_scr[...] = dot_split(row_part, hits, NN)
-    on_map = jnp.where(edge_lane % 16 < 8, left, right)
-    sums_of = []
-    for eb in range(4):
-        rows = slice(CH * eb, CH * (eb + 1))
-        total = jnp.zeros((CH, cols), F32)
-        for k in range(9):
-            span = slice(k * cols, (k + 1) * cols) if k < 8 else slice(8 * cols, 8 * cols + LANES)
-            pre = pre_scr[rows, span] + (col_part[eb][:, :cols] if k < 8 else col_part[eb][:, cols:])
-            sig = 1.0 / (1.0 + jnp.exp(-pre))
-            held = sig
-            if eb == 0:
-                held = held * top
-            if eb == 3:
-                held = held * bottom
-            if k == 8:
-                held = held * on_map
-            act_scr[rows, span] = (pre * held).astype(BF16)
-            inner = (back_ref[rows, span] * (held * (1.0 + pre * (1.0 - sig)))).astype(BF16)
-            inner_scr[rows, span] = inner
-            if k < 8:
-                total = total + inner.astype(F32)
-            else:
-                total = jnp.concatenate([total, inner.astype(F32)], axis=1)
-        sums_of.append(total)
+    by_tap = [row_terms[CH * b : CH * (b + 1)] for b in range(3)]
+    row_part = by_tap[0] + by_tap[1] + by_tap[2]
+
+    def spread_over(terms, k):
+        return jnp.concatenate(
+            [jnp.broadcast_to(terms[:, 8 * eb + k : 8 * eb + k + 1], (CH, LANES)) for eb in range(4)], axis=0
+        )
+
+    side_lane = lax.broadcasted_iota(jnp.int32, (4 * CH, LANES), 1)
+    first_off = jnp.where(side_lane < 8, left - 1.0, 0.0)
+    last_off = jnp.where(side_lane >= LANES - 8, right - 1.0, 0.0)
+    edge_part = jnp.zeros((4 * CH, LANES), F32)
+    on_map = jnp.where(side_lane % 16 < 8, left, right)
+    col_part = jnp.concatenate(col_part, axis=0)
+    main_sum = jnp.zeros((4 * CH, cols), F32)
+    for k in range(9):
+        span = slice(k * cols, (k + 1) * cols) if k < 8 else slice(8 * cols, 8 * cols + LANES)
+        if k < 8:
+            each = spread_over(row_part, k)
+            edge_part = jnp.where(side_lane // 16 == k, each, edge_part)
+            pieces = [each] * (cols // LANES)
+            pieces[0] = pieces[0] + first_off * spread_over(by_tap[0], k)
+            pieces[-1] = pieces[-1] + last_off * spread_over(by_tap[2], k)
+            pre = jnp.concatenate(pieces, axis=1) + col_part[:, :cols]
+        else:
+            pre = edge_part + col_part[:, cols:]
+        sig = 1.0 / (1.0 + jnp.exp(-pre))
+        held = jnp.concatenate([sig[:CH] * top, sig[CH : 3 * CH], sig[3 * CH :] * bottom], axis=0)
+        if k == 8:
+            held = held * on_map
+        act_scr[:, span] = (pre * held).astype(BF16)
+        inner = (back_ref[:, span] * (held * (1.0 + pre * (1.0 - sig)))).astype(BF16)
+        inner_scr[:, span] = inner
+        if k < 8:
+            main_sum = main_sum + inner.astype(F32)
+    sums = jnp.concatenate([main_sum, inner.astype(F32)], axis=1)
+    sums_of = [sums[CH * eb : CH * (eb + 1)] for eb in range(4)]
 
     full = dot(x_ref[...].reshape(6 * CH, x_ref.shape[2]), act_scr[...], NT)
-    sums = dot(hits, inner_scr[...], NT)
+    sums = dot(ind_ref[...], inner_scr[...], NT)
     row_sums = jnp.concatenate(
         [
             jnp.concatenate([sums[8 * b : 8 * b + 8, CH * eb : CH * (eb + 1)] for b in range(3)], axis=1)
@@ -245,8 +243,8 @@
         total = total + (pltpu.roll(piece, (8 * (tap - 1)) % (cols + 2 * LANES), 1) if tap != 1 else piece)
     one_row = dot_split(row_sums, row_cat, TN)
     one_col = dot(high, col_cat, NT) + dot(rest, col_cat, NT)
-    gap = jnp.zeros((32, cols + LANES), F32)
-    bias_row = dot_exact(jnp.ones((8, cols + LANES), F32), jnp.concatenate([gap, whole, gap], axis=0), NT)
+    bias_row = jnp.sum(row_sums[:, :LANES], axis=0, keepdims=True)
+    bias_row = pltpu.roll(jnp.where(lax.broadcasted_iota(jnp.int32, (8, LANES), 1) >= CH, bias_row, 0.0), 96, 1)
     for a in range(3):
         for b in range(3):
             one = one_row[CH * b : CH * (b + 1), CH * a : CH * (a + 1)]
@@ -349,16 +347,23 @@
         ],
         compiler_params=PARAMS,
     )(row_feat, col_turned)
-    both = [(r * n_col + c, (r ^ 1) * n_col + (c ^ 1)) for r in range(n_row) for c in range(n_col)]
+
+    def twin(index, count):
+        return index ^ 1
 
     def other(index, count):
         return min(max(index + (1 if index % 2 else -1), 0), count - 1)
 
-    rest = [
-        (r * n_col + c, other(r, n_row) * n_col + other(c, n_col)) for r in range(n_row) for c in range(n_col)
-    ]
-    twin = lax.ppermute(strip, ("row", "col"), both)
-    far = lax.ppermute(strip, ("row", "col"), rest)
+    def swap(along_row, along_col):
+        pairs = [
+            (r * n_col + c, along_row(r, n_row) * n_col + along_col(c, n_col))
+            for r in range(n_row)
+            for c in range(n_col)
+        ]
+        return lax.ppermute(strip, ("row", "col"), pairs)
+
+    row_twin = swap(twin, other)
+    col_twin = swap(other, twin)
 
     held = pl.pallas_call(
         lambda *refs: own_kernel(n_col, *refs),
@@ -382,14 +387,13 @@
         lambda *refs: main_kernel(n_row, n_col, *refs),
         out_shape=(sds((n_row, sums_end + 8, LANES), BF16), sds((8, LANES))),
         scratch_shapes=[
-            pltpu.VMEM((4 * CH, places), F32),
             pltpu.VMEM((4 * CH, places), BF16),
             pltpu.VMEM((4 * CH, places), BF16),
             pltpu.VMEM((9 * CH, LANES), F32),
             pltpu.VMEM((n_row, sums_end + 8, LANES), F32),
         ],
         compiler_params=PARAMS,
-    )(twin, far, *held)
+    )(row_twin, col_twin, *held)
     got = lax.all_to_all(chunks, "row", 0, 0)
     copies = pl.pallas_call(
         lambda *refs: row_sum_kernel(n_row, n_col, *refs),

time: 62.6 us -> 58.9 us (0.941)
  blocking collectives: 46 us -> 43.3 us
    all_to_all x1, blocking collectives: 17.8 us -> 15.5 us  [shards(): got = lax.all_to_all(copies, 'col', 0, 0)]
  transfers between devices with their start and end apart: 2 -> 2, of which waited for: 1 -> 0; matrix products, arithmetic and copies ran while one was open for 0% -> 0% of each run, Pallas kernels for 4% -> 4%
where the time goes in v7:
time: 58.9 us; the launch traced here: 58.6 us
  blocking collectives  43.3 us (74%)
  Pallas kernels  8.12 us (14%)
  starting transfers between devices  6.5 us (11%)
  between operations  0.67 us (1%)
    all_to_all x1, blocking collectives, shards(): got = lax.all_to_all(chunks, 'row', 0, 0)  16.4 us
    all_to_all x1, blocking collectives, shards(): got = lax.all_to_all(copies, 'col', 0, 0)  15.5 us
    all_to_all x1, blocking collectives, shards(): got = lax.all_to_all(copies, 'row', 0, 0)  11.4 us
    ppermute x2, starting transfers between devices, swap(): return lax.ppermute(strip, ('row', 'col'), pairs)  6.5 us
    pallas_call x1, Pallas kernels, shards(): pl.pallas_call(lambda *refs: main_kernel(n_row, n_col, *refs), out_shape=...  3.09 us
    pallas_call x1, Pallas kernels, shards(): pl.pallas_call(lambda *refs: own_kernel(n_col, *refs), out_shape=(sds((3,...  2.63 us
  transfers between devices with their start and end apart: 2, of which 0 were waited for; matrix products, arithmetic and copies ran while one was open for 0% of the time, Pallas kernels for 4%

profile of v7, /device:TPU:1, one launch (start us, length us, event | category | flops | bytes accessed | tf_op | source)
XLA Modules:
  0.0 58.6 jit_solution(2626414947560800097)
XLA Ops:
  0.6 0.8 %shard_map.101 = bf16[80,128]{1,0:T(8,128)(2,1)S(1)} custom-call(bf16[16,64]{1,0:T(8,128)(2,1)} %refs_4_.1, bf16[64,256]{1,0:T(8,128)(2,1)} %bitcast.6), custom_call_target="tpu_custom_call" | custom-call | tf_op jit(solution)/shard_map/pallas_call | solution.py:338
  1.4 3.3 %collective-permute-start.1 = (bf16[80,128]{1,0:T(8,128)(2,1)S(1)}, bf16[80,128]{1,0:T(8,128)(2,1)S(1)}, u32[]{:S(2)}, u32[]{:S(2)}) collective-permute-start(bf16[80,128]{1,0:T(8,128)(2,1)S(1)} %shard_map.101), channel_id=1, source_target_pairs={{0,1},{1,0},{2,3},{3,2},{4,5},{5,4},{6,7},{7,6},{8,17},{9,16},{10,... | collective-permute-start | bytes 61448 | tf_op jit(solution)/shard_map/ppermute | solution.py:363
  4.8 3.2 %collective-permute-start = (bf16[80,128]{1,0:T(8,128)(2,1)S(1)}, bf16[80,128]{1,0:T(8,128)(2,1)S(1)}, u32[]{:S(2)}, u32[]{:S(2)}) collective-permute-start(bf16[80,128]{1,0:T(8,128)(2,1)S(1)} %shard_map.101), channel_id=1, source_target_pairs={{0,8},{1,10},{2,9},{3,12},{4,11},{5,14},{6,13},{7,15},{8,0},{9,2},... | collective-permute-start | bytes 61448 | tf_op jit(solution)/shard_map/ppermute | solution.py:363
  7.9 2.6 %shard_map.102 = (bf16[3,128,2176]{2,1,0:T(8,128)(2,1)S(1)}, f32[256,2176]{1,0:T(8,128)S(1)}, f32[8,128]{1,0:T(8,128)S(1)}, f32[64,256]{1,0:T(8,128)S(1)}, bf16[...) custom-call(bf16[64,16,256]{2,1,0:T(8,128)(2,1)} %refs_0_.1, ...), custom_call_target="tpu_custom_call" | custom-call | tf_op jit(solution)/shard_map/pallas_call | solution.py:368
  10.6 0.0 collective-permute-done.1.refs_1_
  10.6 0.0 collective-permute-done.refs_0_
  10.6 3.1 %shard_map.103 = (bf16[32,32,128]{2,1,0:T(8,128)(2,1)S(1)}, f32[8,128]{1,0:T(8,128)S(1)}) custom-call(bf16[80,128]{1,0:T(8,128)(2,1)S(1)} %collective-permute-done.refs_0_, bf16[80,128]{1,0:T(8,128)(2,1)S(1)} %collective-permute-done.1.refs_1_, bf16[3,128,2176]{2,1,0:T(8,128)(2,1)S(1)} %get-tuple-element.23.refs_2_, ...), custom_call_target="tpu_custom_call" | custom-call | tf_op jit(solution)/shard_map/pallas_call | solution.py:386
  13.7 16.4 %all_to_all.15.refs_0_ = bf16[32,32,128]{2,1,0:T(8,128)(2,1)S(1)} all-to-all(bf16[32,32,128]{2,1,0:T(8,128)(2,1)S(1)} %get-tuple-element.33), channel_id=1, replica_groups=mesh['row'=32,'col'=8] {'row'}, dimensions={0} | all-to-all | bytes 524288 | tf_op jit(solution)/shard_map/all_to_all | solution.py:397
  30.2 15.5 %all_to_all.16.refs_0_ = bf16[8,32,128]{2,1,0:T(8,128)(2,1)S(1)} all-to-all(bf16[8,32,128]{2,1,0:T(8,128)(2,1)S(1)} %shard_map.104), channel_id=1, replica_groups=mesh['row'=32,'col'=8] {'col'}, dimensions={0} | all-to-all | bytes 131072 | tf_op jit(solution)/shard_map/all_to_all | solution.py:403
  45.6 0.7 %shard_map.105 = (f32[16,64]{1,0:T(8,128)}, f32[1,64]{1,0:T(1,128)}, bf16[32,32,128]{2,1,0:T(8,128)(2,1)S(1)}) custom-call(bf16[8,32,128]{2,1,0:T(8,128)(2,1)S(1)} %all_to_all.16.refs_0_), custom_call_target="tpu_custom_call" | custom-call | tf_op jit(solution)/shard_map/pallas_call | solution.py:405
  46.3 11.4 %all_to_all.17.refs_0_ = bf16[32,32,128]{2,1,0:T(8,128)(2,1)S(1)} all-to-all(bf16[32,32,128]{2,1,0:T(8,128)(2,1)S(1)} %get-tuple-element.36), channel_id=1, replica_groups=mesh['row'=32,'col'=8] {'row'}, dimensions={0} | all-to-all | bytes 524288 | tf_op jit(solution)/shard_map/all_to_all | solution.py:411
  57.7 0.9 %shard_map.106 = (f32[64,256]{1,0:T(8,128)}, f32[576,64]{1,0:T(8,128)}, f32[576,64]{1,0:T(8,128)}) custom-call(bf16[32,32,128]{2,1,0:T(8,128)(2,1)S(1)} %all_to_all.17.refs_0_), custom_call_target="tpu_custom_call" | custom-call | tf_op jit(solution)/shard_map/pallas_call | solution.py:412
  (1 shorter events, 0.0 us)
Async XLA Ops:
  1.4 9.1 %collective-permute-start.1 = (bf16[80,128]{1,0:T(8,128)(2,1)S(1)}, bf16[80,128]{1,0:T(8,128)(2,1)S(1)}, u32[]{:S(2)}, u32[]{:S(2)}) collective-permute-start(bf16[80,128]{1,0:T(8,128)(2,1)S(1)} %shard_map.101), channel_id=1, source_target_pairs={{0,1},{1,0},{2,3},{3,2},{4,5},{5,4},{6,7},{7,6},{8,17},{9,16},{10,... | collective-permute-start | bytes 61448 | tf_op jit(solution)/shard_map/ppermute | solution.py:363
  4.8 5.8 %collective-permute-start = (bf16[80,128]{1,0:T(8,128)(2,1)S(1)}, bf16[80,128]{1,0:T(8,128)(2,1)S(1)}, u32[]{:S(2)}, u32[]{:S(2)}) collective-permute-start(bf16[80,128]{1,0:T(8,128)(2,1)S(1)} %shard_map.101), channel_id=1, source_target_pairs={{0,8},{1,10},{2,9},{3,12},{4,11},{5,14},{6,13},{7,15},{8,0},{9,2},... | collective-permute-start | bytes 61448 | tf_op jit(solution)/shard_map/ppermute | solution.py:363

commit v8 on v7

--- a/solution.py
+++ b/solution.py
@@ -13,6 +13,7 @@
 TN = (((0,), (0,)), ((), ()))
 CH = 64
 LANES = 128
+GRAD_COPIES = 1
 
 
 def dot(x, y, dims):
@@ -31,19 +32,58 @@
     return dot(high, y, dims) + dot(low, y, dims)
 
 
-def pack_kernel(row_hbm, col_hbm, out_ref, row_ref, col_ref, row_sem, col_sem):
-    row_copy = pltpu.make_async_copy(row_hbm, row_ref, row_sem)
-    col_copy = pltpu.make_async_copy(col_hbm, col_ref, col_sem)
-    row_copy.start()
-    col_copy.start()
-    row_copy.wait()
-    col_copy.wait()
+def shares(n_row, j):
+    weights = 9 * CH // n_row
+    main = weights // 8 * 8
+    pieces = [(slice(0, main), slice(main * j, main * (j + 1)))]
+    if main < weights:
+        rest = weights - main
+        pieces.append((slice(main, weights), slice(main * n_row + rest * j, main * n_row + rest * (j + 1))))
+    return pieces
+
+
+def pack_kernel(
+    n_col, row_hbm, col_hbm, one_hbm, two_hbm, bias_hbm, grad_hbm,
+    out_ref, row_ref, col_ref, grad_ref, ind_ref, k1c_ref, k1f_ref, w2_ref, bias_col_ref,
+    one_ref, two_ref, bias_ref, sems,
+):
+    pairs = [
+        (row_hbm, row_ref), (col_hbm, col_ref), (one_hbm, one_ref), (two_hbm, two_ref), (bias_hbm, bias_ref),
+    ]
+    step = CH // GRAD_COPIES
+    for k in range(GRAD_COPIES):
+        part = slice(step * k, step * (k + 1))
+        pairs.append((grad_hbm.at[part], grad_ref.at[part]))
+    copies = [pltpu.make_async_copy(x, y, sems.at[k]) for k, (x, y) in enumerate(pairs)]
+    for copy in copies:
+        copy.start()
+    for copy in copies[:2]:
+        copy.wait()
     rows = row_ref[...].astype(F32)
     out_ref[:16, :] = jnp.concatenate([rows, jnp.zeros_like(rows)], axis=1).astype(BF16)
     cols = col_ref.shape[1]
     lane = lax.broadcasted_iota(jnp.int32, (CH, LANES), 1)
     first, last = col_ref[:, :LANES].astype(F32), col_ref[:, cols - LANES :].astype(F32)
     out_ref[16:, :] = jnp.where(lane < LANES // 2, first, last).astype(BF16)
+    ind_ref[...] = indicator(cols, n_col)
+    for copy in copies[2:5]:
+        copy.wait()
+    one = [[one_ref[a, b].astype(F32) for b in range(3)] for a in range(3)]
+    for k in range(3):
+        rows = slice(CH * k, CH * (k + 1))
+        k1c_ref[rows, :] = jnp.concatenate(one[k], axis=1).astype(BF16)
+        k1f_ref[rows, :] = jnp.concatenate([one[a][k] for a in range(3)], axis=1).astype(BF16)
+    nil = jnp.zeros((CH, CH), F32)
+    two = [[two_ref[a, b].astype(F32) for b in range(3)] for a in range(3)]
+    for b in range(3):
+        for gb in range(2):
+            blocks = [two[eb - gb][b] if 0 <= eb - gb <= 2 else nil for eb in range(4)]
+            at = CH * (2 * b + gb)
+            w2_ref[at : at + CH, :] = jnp.concatenate(blocks, axis=1).astype(BF16)
+    bias = jnp.concatenate([bias_ref[...], jnp.zeros((1, LANES - CH), F32)], axis=1)
+    bias_col_ref[...] = jnp.broadcast_to(bias, (8, LANES)).T[:CH, :]
+    for copy in copies[5:]:
+        copy.wait()
 
 
 def off_edge(axis, index):
@@ -66,41 +106,8 @@
     return jnp.concatenate(taps, axis=0).astype(BF16)
 
 
-def own_kernel(
-    n_col, grad_hbm, one_hbm, two_hbm, bias_hbm, row_hbm, col_hbm,
-    x_ref, back_ref, grad_rows_ref, grad_cols_ref, ind_ref, k1c_ref, k1f_ref, bias_col_ref, row_ref, col_ref,
-    rows_scr, grad_ref, one_ref, two_ref, bias_ref, sems,
-):
+def own_kernel(grad_ref, w2_ref, x_ref, back_ref, grad_rows_ref, grad_cols_ref, rows_scr):
     cols = grad_ref.shape[2]
-    pairs = (
-        (one_hbm, one_ref), (two_hbm, two_ref), (bias_hbm, bias_ref), (row_hbm, row_ref), (col_hbm, col_ref),
-        (grad_hbm, grad_ref),
-    )
-    copies = [pltpu.make_async_copy(source, target, sems.at[k]) for k, (source, target) in enumerate(pairs)]
-    for copy in copies:
-        copy.start()
-    hits = indicator(cols, n_col)
-    ind_ref[...] = hits
-    for copy in copies[:-1]:
-        copy.wait()
-    one = [[one_ref[a, b].astype(F32) for b in range(3)] for a in range(3)]
-    for k in range(3):
-        rows = slice(CH * k, CH * (k + 1))
-        k1c_ref[rows, :] = jnp.concatenate(one[k], axis=1).astype(BF16)
-        k1f_ref[rows, :] = jnp.concatenate([one[a][k] for a in range(3)], axis=1).astype(BF16)
-    nil = jnp.zeros((CH, CH), F32)
-    two = [[two_ref[a, b].astype(F32) for b in range(3)] for a in range(3)]
-    w2 = jnp.concatenate(
-        [
-            jnp.concatenate([two[eb - gb][b] if 0 <= eb - gb <= 2 else nil for eb in range(4)], axis=1)
-            for b in range(3)
-            for gb in range(2)
-        ],
-        axis=0,
-    ).astype(BF16)
-    bias = jnp.concatenate([bias_ref[...], jnp.zeros((1, LANES - CH), F32)], axis=1)
-    bias_col_ref[...] = jnp.broadcast_to(bias, (8, LANES)).T[:CH, :]
-    copies[-1].wait()
     lane = lax.broadcasted_iota(jnp.int32, (CH, cols), 1)
     edge_lane = lax.broadcasted_iota(jnp.int32, (CH, LANES), 1)
     for piece in range(cols // LANES):
@@ -131,12 +138,12 @@
     span = lax.broadcasted_iota(jnp.int32, (8, 8 * cols), 1) // cols
     grad_rows_ref[...] = dot(jnp.where(row == span, 1.0, 0.0).astype(BF16), x_ref[1, :, : 8 * cols], NT)
     x_all = x_ref[...].reshape(6 * CH, x_ref.shape[2])
-    back_ref[...] = dot(w2, x_all, TN)
+    back_ref[...] = dot(w2_ref[...], x_all, TN)
 
 
 def main_kernel(
-    n_row, n_col, row_twin_ref, col_twin_ref,
-    x_ref, back_ref, grad_rows_ref, grad_cols_ref, ind_ref, k1c_ref, k1f_ref, bias_ref, row_ref, col_ref,
+    n_row, n_col, row_twin_ref, col_twin_ref, row_ref, col_ref,
+    x_ref, back_ref, grad_rows_ref, grad_cols_ref, ind_ref, k1c_ref, k1f_ref, bias_ref,
     out_ref, own_ref, act_scr, inner_scr, w_scr, chunk_scr,
 ):
     cols = col_ref.shape[1]
@@ -258,7 +265,8 @@
     tail = total[:, :LANES] + total[:, cols + LANES :] + bias_row[:1, :]
     before = lax.axis_index("row") - 1
     for j in range(n_row):
-        chunk_scr[j, :weights, :] = w_scr[weights * j : weights * (j + 1), :]
+        for there, here in shares(n_row, j):
+            chunk_scr[j, there, :] = w_scr[here, :]
         share = slice(chans * j, chans * (j + 1))
         chunk_scr[j, weights : weights + chans, :] = total[share, LANES : 2 * LANES]
         chunk_scr[j, weights + chans : weights + 2 * chans, :] = total[share, cols : cols + LANES]
@@ -282,17 +290,15 @@
         out_ref[k] = whole
 
 
-def col_sum_kernel(n_row, n_col, cols, got_ref, row_ref, bias_ref, out_ref, scr):
+def col_sum_kernel(n_row, n_col, cols, got_ref, kept_ref, out_ref, scr):
     weights, chans, sums_end = chunk_rows(n_row)
     me = lax.axis_index("col")
     whole = math.sqrt(16 * n_row * cols * n_col)
     total = got_ref[0].astype(F32)
     for k in range(1, n_col):
         total = total + got_ref[k].astype(F32)
-    rows = total[sums_end:, :] * (1.0 / math.sqrt(cols * n_col))
-    row_ref[0:8, :] = rows[:, :CH]
-    row_ref[8:16, :] = rows[:, CH:]
-    bias_ref[...] = total[sums_end - 1 : sums_end, 32 : 32 + CH] * (1.0 / whole)
+    kept_ref[:8, :] = total[sums_end:, :] * (1.0 / math.sqrt(cols * n_col))
+    kept_ref[8:, :] = total[sums_end - 8 : sums_end, :] * (1.0 / whole)
     before = got_ref[jnp.maximum(me - 1, 0)].astype(F32) * off_edge("col", 0)
     after = got_ref[jnp.minimum(me + 1, n_col - 1)].astype(F32) * off_edge("col", n_col - 1)
     mine = got_ref[me].astype(F32)
@@ -310,12 +316,16 @@
         out_ref[j] = share
 
 
-def spread_kernel(n_row, got_ref, col_ref, one_ref, two_ref):
+def spread_kernel(n_row, got_ref, kept_ref, row_ref, col_ref, one_ref, bias_ref, two_ref):
     weights, chans, _ = chunk_rows(n_row)
+    row_ref[:8, :] = kept_ref[:8, :CH]
+    row_ref[8:, :] = kept_ref[:8, CH:]
+    bias_ref[...] = kept_ref[15:, 32 : 32 + CH]
     for j in range(n_row):
         chunk = got_ref[j].astype(F32)
-        one_ref[weights * j : weights * (j + 1), :] = chunk[:weights, :CH]
-        two_ref[weights * j : weights * (j + 1), :] = chunk[:weights, CH:]
+        for there, here in shares(n_row, j):
+            one_ref[here, :] = chunk[there, :CH]
+            two_ref[here, :] = chunk[there, CH:]
         col_ref[chans * j : chans * (j + 1), :LANES] = chunk[weights : weights + chans]
         col_ref[chans * j : chans * (j + 1), LANES:] = chunk[weights + chans : weights + 2 * chans]
 
@@ -335,18 +345,23 @@
         pltpu.with_memory_space_constraint(x, pltpu.HBM)
         for x in (grad_out, row_feat, col_feat.T, conv_one, conv_two, bias_one.reshape(1, CH))
     )
-    strip = pl.pallas_call(
-        pack_kernel,
-        out_shape=sds((16 + CH, LANES), BF16),
-        in_specs=[pl.BlockSpec(memory_space=pltpu.HBM)] * 2,
+    square = (3 * CH, 3 * CH)
+    strip, row_feat, col_turned, grad_out, hits, k1c, k1f, w2, bias_col = pl.pallas_call(
+        lambda *refs: pack_kernel(n_col, *refs),
+        out_shape=(
+            sds((16 + CH, LANES), BF16), sds(row_feat.shape, BF16), sds(col_turned.shape, BF16),
+            sds(grad_out.shape, BF16), sds((24, places), BF16), sds(square, BF16), sds(square, BF16),
+            sds((6 * CH, 4 * CH), BF16), sds((CH, 8)),
+        ),
+        in_specs=[pl.BlockSpec(memory_space=pltpu.HBM)] * 6,
         scratch_shapes=[
-            pltpu.VMEM((16, CH), BF16),
-            pltpu.VMEM((CH, cols), BF16),
-            pltpu.SemaphoreType.DMA,
-            pltpu.SemaphoreType.DMA,
+            pltpu.VMEM(conv_one.shape, BF16),
+            pltpu.VMEM(conv_two.shape, BF16),
+            pltpu.VMEM((1, CH), F32),
+            pltpu.SemaphoreType.DMA((5 + GRAD_COPIES,)),
         ],
         compiler_params=PARAMS,
-    )(row_feat, col_turned)
+    )(row_feat, col_turned, conv_one, conv_two, bias_row, grad_out)
 
     def twin(index, count):
         return index ^ 1
@@ -365,24 +380,12 @@
     row_twin = swap(twin, other)
     col_twin = swap(other, twin)
 
-    held = pl.pallas_call(
-        lambda *refs: own_kernel(n_col, *refs),
-        out_shape=(
-            sds((3, 2 * CH, places), BF16), sds((4 * CH, places)), sds((8, 2 * CH)), sds((CH, cols)),
-            sds((24, places), BF16), sds((3 * CH, 3 * CH), BF16), sds((3 * CH, 3 * CH), BF16), sds((CH, 8)),
-            sds((16, CH), BF16), sds((CH, cols), BF16),
-        ),
-        in_specs=[pl.BlockSpec(memory_space=pltpu.HBM)] * 6,
-        scratch_shapes=[
-            pltpu.VMEM((cols // LANES, CH * 16, LANES), F32),
-            pltpu.VMEM(grad_out.shape, BF16),
-            pltpu.VMEM(conv_one.shape, BF16),
-            pltpu.VMEM(conv_two.shape, BF16),
-            pltpu.VMEM((1, CH), F32),
-            pltpu.SemaphoreType.DMA((6,)),
-        ],
-        compiler_params=PARAMS,
-    )(grad_out, conv_one, conv_two, bias_row, row_feat, col_turned)
+    x, back, grad_rows, grad_cols = pl.pallas_call(
+        own_kernel,
+        out_shape=(sds((3, 2 * CH, places), BF16), sds((4 * CH, places)), sds((8, 2 * CH)), sds((CH, cols))),
+        scratch_shapes=[pltpu.VMEM((cols // LANES, CH * 16, LANES), F32)],
+        compiler_params=PARAMS,
+    )(grad_out, w2)
     chunks, own = pl.pallas_call(
         lambda *refs: main_kernel(n_row, n_col, *refs),
         out_shape=(sds((n_row, sums_end + 8, LANES), BF16), sds((8, LANES))),
@@ -393,7 +396,7 @@
             pltpu.VMEM((n_row, sums_end + 8, LANES), F32),
         ],
         compiler_params=PARAMS,
-    )(row_twin, col_twin, *held)
+    )(row_twin, col_twin, row_feat, col_turned, x, back, grad_rows, grad_cols, hits, k1c, k1f, bias_col)
     got = lax.all_to_all(chunks, "row", 0, 0)
     copies = pl.pallas_call(
         lambda *refs: row_sum_kernel(n_row, n_col, *refs),
@@ -402,18 +405,18 @@
     )(got, own)
     got = lax.all_to_all(copies, "col", 0, 0)
     end = -(-(weights + 2 * chans) // 16) * 16
-    row_grad, bias_grad, copies = pl.pallas_call(
+    kept, copies = pl.pallas_call(
         lambda *refs: col_sum_kernel(n_row, n_col, cols, *refs),
-        out_shape=(sds((16, CH)), sds((1, CH)), sds((n_row, end, LANES), BF16)),
+        out_shape=(sds((16, LANES)), sds((n_row, end, LANES), BF16)),
         scratch_shapes=[pltpu.VMEM((end, LANES), F32)],
         compiler_params=PARAMS,
     )(got)
     got = lax.all_to_all(copies, "row", 0, 0)
-    col_grad, one, two = pl.pallas_call(
+    row_grad, col_grad, one, bias_grad, two = pl.pallas_call(
         lambda *refs: spread_kernel(n_row, *refs),
-        out_shape=(sds((CH, cols)), sds((9 * CH, CH)), sds((9 * CH, CH))),
-        compiler_params=PARAMS,
-    )(got)
+        out_shape=(sds((16, CH)), sds((CH, cols)), sds((9 * CH, CH)), sds((1, CH)), sds((9 * CH, CH))),
+        compiler_params=PARAMS,
+    )(got, kept)
     shape = conv_one.shape
     return row_grad, col_grad.T, one.reshape(shape), bias_grad[0], two.reshape(shape)
 

time: 58.9 us -> 59.7 us (1.014)
  blocking collectives: 43.3 us -> 46.5 us
  Pallas kernels: 8.12 us -> 6.69 us
  starting transfers between devices: 6.5 us -> 5.48 us
    all_to_all x1, blocking collectives: 16.4 us -> 19.5 us  [shards(): got = lax.all_to_all(chunks, 'row', 0, 0)]
    ppermute x2, starting transfers between devices: 6.5 us -> 5.48 us  [swap(): return lax.ppermute(strip, ('row', 'col'), pairs)]
    pallas_call x2, Pallas kernels: 3.43 us -> 2.62 us  [the longest x1 1.32 us: shards(): pl.pallas_call(own_kernel, out_shape=(sds((3, 2 * CH, places), BF16), sds...]
    all_to_all x1, blocking collectives: 11.4 us -> 12.2 us  [shards(): got = lax.all_to_all(copies, 'row', 0, 0)]
    all_to_all x1, blocking collectives: 15.5 us -> 14.8 us  [shards(): got = lax.all_to_all(copies, 'col', 0, 0)]
    pallas_call x1, Pallas kernels: 0.68 us -> 0.04 us  [shards(): pl.pallas_call(lambda *refs: col_sum_kernel(n_row, n_col, cols, *refs), o...]
  transfers between devices with their start and end apart: 2 -> 2, of which waited for: 0 -> 1; matrix products, arithmetic and copies ran while one was open for 0% -> 0% of each run, Pallas kernels for 4% -> 2%
where the time goes in v8:
time: 59.7 us; the launch traced here: 59.5 us
  blocking collectives  46.5 us (78%)
  Pallas kernels  6.69 us (11%)
  starting transfers between devices  5.48 us (9%)
  between operations  0.66 us (1%)
    all_to_all x1, blocking collectives, shards(): got = lax.all_to_all(chunks, 'row', 0, 0)  19.5 us
    all_to_all x1, blocking collectives, shards(): got = lax.all_to_all(copies, 'col', 0, 0)  14.8 us
    all_to_all x1, blocking collectives, shards(): got = lax.all_to_all(copies, 'row', 0, 0)  12.2 us
    ppermute x2, starting transfers between devices, swap(): return lax.ppermute(strip, ('row', 'col'), pairs)  5.48 us
    pallas_call x1, Pallas kernels, shards(): pl.pallas_call(lambda *refs: main_kernel(n_row, n_col, *refs), out_shape=...  3.11 us
    pallas_call x1, Pallas kernels, shards(): pl.pallas_call(own_kernel, out_shape=(sds((3, 2 * CH, places), BF16), sds...  1.32 us
    pallas_call x1, Pallas kernels, shards(): pl.pallas_call(lambda *refs: pack_kernel(n_col, *refs), out_shape=(sds((1...  1.29 us
  transfers between devices with their start and end apart: 2, of which 1 were waited for; matrix products, arithmetic and copies ran while one was open for 0% of the time, Pallas kernels for 2%

profile of v8, /device:TPU:1, one launch (start us, length us, event | category | flops | bytes accessed | tf_op | source)
XLA Modules:
  0.0 59.5 jit_solution(6191369254848923006)
XLA Ops:
  0.6 1.3 %shard_map.101 = (bf16[80,128]{1,0:T(8,128)(2,1)S(1)}, bf16[16,64]{1,0:T(8,128)(2,1)S(1)}, bf16[64,256]{1,0:T(8,128)(2,1)S(1)}, bf16[64,16,256]{2,1,0:T(8,128)(2...) custom-call(bf16[16,64]{1,0:T(8,128)(2,1)} %refs_0_.1, ...), custom_call_target="tpu_custom_call" | custom-call | tf_op jit(solution)/shard_map/pallas_call | solution.py:349
  1.9 5.5 %collective-permute-start = (bf16[80,128]{1,0:T(8,128)(2,1)S(1)}, bf16[80,128]{1,0:T(8,128)(2,1)S(1)}, u32[]{:S(2)}, u32[]{:S(2)}) collective-permute-start(bf16[80,128]{1,0:T(8,128)(2,1)S(1)} %get-tuple-element.27), channel_id=1, source_target_pairs={{0,8},{1,10},{2,9},{3,12},{4,11},{5,14},{6,13},{7,15},{8,0},{9,2},... | collective-permute-start | bytes 61448 | tf_op jit(solution)/shard_map/ppermute | solution.py:378
  7.4 0.0 collective-permute-start.1
  7.4 1.3 %shard_map.102 = (bf16[3,128,2176]{2,1,0:T(8,128)(2,1)S(1)}, f32[256,2176]{1,0:T(8,128)S(1)}, f32[8,128]{1,0:T(8,128)S(1)}, f32[64,256]{1,0:T(8,128)S(1)}) custom-call(bf16[64,16,256]{2,1,0:T(8,128)(2,1)S(1)} %get-tuple-element.30.grad_ref, bf16[384,256]{1,0:T(8,128)(2,1)S(1)} %get-tuple-element.31.w2_ref), custom_call_target="tpu_custom_call" | custom-call | tf_op jit(solution)/shard_map/pallas_call | solution.py:383
  8.7 0.1 collective-permute-done.refs_0_
  8.9 0.0 collective-permute-done.1.refs_1_
  8.9 3.1 %shard_map.103 = (bf16[32,32,128]{2,1,0:T(8,128)(2,1)S(1)}, f32[8,128]{1,0:T(8,128)S(1)}) custom-call(bf16[80,128]{1,0:T(8,128)(2,1)S(1)} %collective-permute-done.refs_0_, bf16[80,128]{1,0:T(8,128)(2,1)S(1)} %collective-permute-done.1.refs_1_, bf16[16,64]{1,0:T(8,128)(2,1)S(1)} %get-tuple-element.28.refs_2_, bf16[64,256]{1,0:T(8,128)(2,1)S(1)} %get-tuple-element.29.refs_3_, ...), custom_call_target="tpu_custom_call" | custom-call | tf_op jit(solution)/shard_map/pallas_call | solution.py:389
  12.0 19.5 %all_to_all.15.refs_0_ = bf16[32,32,128]{2,1,0:T(8,128)(2,1)S(1)} all-to-all(bf16[32,32,128]{2,1,0:T(8,128)(2,1)S(1)} %get-tuple-element.40), channel_id=1, replica_groups=mesh['row'=32,'col'=8] {'row'}, dimensions={0} | all-to-all | bytes 524288 | tf_op jit(solution)/shard_map/all_to_all | solution.py:400
  31.5 14.8 %all_to_all.16.refs_0_ = bf16[8,32,128]{2,1,0:T(8,128)(2,1)S(1)} all-to-all(bf16[8,32,128]{2,1,0:T(8,128)(2,1)S(1)} %shard_map.104), channel_id=1, replica_groups=mesh['row'=32,'col'=8] {'col'}, dimensions={0} | all-to-all | bytes 131072 | tf_op jit(solution)/shard_map/all_to_all | solution.py:406
  46.4 12.2 %all_to_all.17.refs_0_ = bf16[32,32,128]{2,1,0:T(8,128)(2,1)S(1)} all-to-all(bf16[32,32,128]{2,1,0:T(8,128)(2,1)S(1)} %get-tuple-element.42), channel_id=1, replica_groups=mesh['row'=32,'col'=8] {'row'}, dimensions={0} | all-to-all | bytes 524288 | tf_op jit(solution)/shard_map/all_to_all | solution.py:414
  58.6 0.9 %shard_map.106 = (f32[16,64]{1,0:T(8,128)}, f32[64,256]{1,0:T(8,128)}, f32[576,64]{1,0:T(8,128)}, f32[1,64]{1,0:T(1,128)}, f32[576,64]{1,0:T(8,128)}) custom-call(bf16[32,32,128]{2,1,0:T(8,128)(2,1)S(1)} %all_to_all.17.refs_0_, f32[16,128]{1,0:T(8,128)S(1)} %get-tuple-element.43.refs_1_), custom_call_target="tpu_custom_call" | custom-call | tf_op jit(solution)/shard_map/pallas_call | solution.py:415
  (2 shorter events, 0.1 us)
Async XLA Ops:
  1.9 6.9 %collective-permute-start = (bf16[80,128]{1,0:T(8,128)(2,1)S(1)}, bf16[80,128]{1,0:T(8,128)(2,1)S(1)}, u32[]{:S(2)}, u32[]{:S(2)}) collective-permute-start(bf16[80,128]{1,0:T(8,128)(2,1)S(1)} %get-tuple-element.27), channel_id=1, source_target_pairs={{0,8},{1,10},{2,9},{3,12},{4,11},{5,14},{6,13},{7,15},{8,0},{9,2},... | collective-permute-start | bytes 61448 | tf_op jit(solution)/shard_map/ppermute | solution.py:378
  7.4 1.5 %collective-permute-start.1 = (bf16[80,128]{1,0:T(8,128)(2,1)S(1)}, bf16[80,128]{1,0:T(8,128)(2,1)S(1)}, u32[]{:S(2)}, u32[]{:S(2)}) collective-permute-start(bf16[80,128]{1,0:T(8,128)(2,1)S(1)} %get-tuple-element.27), channel_id=1, source_target_pairs={{0,1},{1,0},{2,3},{3,2},{4,5},{5,4},{6,7},{7,6},{8,17},{9,16},{10,... | collective-permute-start | bytes 61448 | tf_op jit(solution)/shard_map/ppermute | solution.py:378

commit v9 on v8

--- a/solution.py
+++ b/solution.py
@@ -142,7 +142,7 @@
 
 
 def main_kernel(
-    n_row, n_col, row_twin_ref, col_twin_ref, row_ref, col_ref,
+    n_row, n_col, col_twin_ref, row_twin_ref, row_ref, col_ref,
     x_ref, back_ref, grad_rows_ref, grad_cols_ref, ind_ref, k1c_ref, k1f_ref, bias_ref,
     out_ref, own_ref, act_scr, inner_scr, w_scr, chunk_scr,
 ):
@@ -377,8 +377,8 @@
         ]
         return lax.ppermute(strip, ("row", "col"), pairs)
 
+    col_twin = swap(other, twin)
     row_twin = swap(twin, other)
-    col_twin = swap(other, twin)
 
     x, back, grad_rows, grad_cols = pl.pallas_call(
         own_kernel,
@@ -396,7 +396,7 @@
             pltpu.VMEM((n_row, sums_end + 8, LANES), F32),
         ],
         compiler_params=PARAMS,
-    )(row_twin, col_twin, row_feat, col_turned, x, back, grad_rows, grad_cols, hits, k1c, k1f, bias_col)
+    )(col_twin, row_twin, row_feat, col_turned, x, back, grad_rows, grad_cols, hits, k1c, k1f, bias_col)
     got = lax.all_to_all(chunks, "row", 0, 0)
     copies = pl.pallas_call(
         lambda *refs: row_sum_kernel(n_row, n_col, *refs),

time: 59.7 us -> 58.7 us (0.983)
  blocking collectives: 46.5 us -> 44.1 us
  starting transfers between devices: 5.48 us -> 6.5 us
    all_to_all x1, blocking collectives: 19.5 us -> 14.9 us  [shards(): got = lax.all_to_all(chunks, 'row', 0, 0)]
    all_to_all x1, blocking collectives: 14.8 us -> 17.9 us  [shards(): got = lax.all_to_all(copies, 'col', 0, 0)]
    ppermute x2, starting transfers between devices: 5.48 us -> 6.5 us  [swap(): return lax.ppermute(strip, ('row', 'col'), pairs)]
    all_to_all x1, blocking collectives: 12.2 us -> 11.4 us  [shards(): got = lax.all_to_all(copies, 'row', 0, 0)]
where the time goes in v9:
time: 58.7 us; the launch traced here: 58.5 us
  blocking collectives  44.1 us (75%)
  Pallas kernels  6.69 us (11%)
  starting transfers between devices  6.5 us (11%)
  between operations  0.66 us (1%)
    all_to_all x1, blocking collectives, shards(): got = lax.all_to_all(copies, 'col', 0, 0)  17.9 us
    all_to_all x1, blocking collectives, shards(): got = lax.all_to_all(chunks, 'row', 0, 0)  14.9 us
    all_to_all x1, blocking collectives, shards(): got = lax.all_to_all(copies, 'row', 0, 0)  11.4 us
    ppermute x2, starting transfers between devices, swap(): return lax.ppermute(strip, ('row', 'col'), pairs)  6.5 us
    pallas_call x1, Pallas kernels, shards(): pl.pallas_call(lambda *refs: main_kernel(n_row, n_col, *refs), out_shape=...  3.11 us
    pallas_call x1, Pallas kernels, shards(): pl.pallas_call(own_kernel, out_shape=(sds((3, 2 * CH, places), BF16), sds...  1.32 us
    pallas_call x1, Pallas kernels, shards(): pl.pallas_call(lambda *refs: pack_kernel(n_col, *refs), out_shape=(sds((1...  1.29 us
  transfers between devices with their start and end apart: 2, of which 1 were waited for; matrix products, arithmetic and copies ran while one was open for 0% of the time, Pallas kernels for 2%

profile of v9, /device:TPU:1, one launch (start us, length us, event | category | flops | bytes accessed | tf_op | source)
XLA Modules:
  0.0 58.5 jit_solution(1676452460900383322)
XLA Ops:
  0.6 1.3 %shard_map.101 = (bf16[80,128]{1,0:T(8,128)(2,1)S(1)}, bf16[16,64]{1,0:T(8,128)(2,1)S(1)}, bf16[64,256]{1,0:T(8,128)(2,1)S(1)}, bf16[64,16,256]{2,1,0:T(8,128)(2...) custom-call(bf16[16,64]{1,0:T(8,128)(2,1)} %refs_0_.1, ...), custom_call_target="tpu_custom_call" | custom-call | tf_op jit(solution)/shard_map/pallas_call | solution.py:349
  1.9 3.3 %collective-permute-start = (bf16[80,128]{1,0:T(8,128)(2,1)S(1)}, bf16[80,128]{1,0:T(8,128)(2,1)S(1)}, u32[]{:S(2)}, u32[]{:S(2)}) collective-permute-start(bf16[80,128]{1,0:T(8,128)(2,1)S(1)} %get-tuple-element.27), channel_id=1, source_target_pairs={{0,1},{1,0},{2,3},{3,2},{4,5},{5,4},{6,7},{7,6},{8,17},{9,16},{10,... | collective-permute-start | bytes 61448 | tf_op jit(solution)/shard_map/ppermute | solution.py:378
  5.3 3.2 %collective-permute-start.1 = (bf16[80,128]{1,0:T(8,128)(2,1)S(1)}, bf16[80,128]{1,0:T(8,128)(2,1)S(1)}, u32[]{:S(2)}, u32[]{:S(2)}) collective-permute-start(bf16[80,128]{1,0:T(8,128)(2,1)S(1)} %get-tuple-element.27), channel_id=1, source_target_pairs={{0,8},{1,10},{2,9},{3,12},{4,11},{5,14},{6,13},{7,15},{8,0},{9,2},... | collective-permute-start | bytes 61448 | tf_op jit(solution)/shard_map/ppermute | solution.py:378
  8.4 1.3 %shard_map.102 = (bf16[3,128,2176]{2,1,0:T(8,128)(2,1)S(1)}, f32[256,2176]{1,0:T(8,128)S(1)}, f32[8,128]{1,0:T(8,128)S(1)}, f32[64,256]{1,0:T(8,128)S(1)}) custom-call(bf16[64,16,256]{2,1,0:T(8,128)(2,1)S(1)} %get-tuple-element.30.grad_ref, bf16[384,256]{1,0:T(8,128)(2,1)S(1)} %get-tuple-element.31.w2_ref), custom_call_target="tpu_custom_call" | custom-call | tf_op jit(solution)/shard_map/pallas_call | solution.py:383
  9.8 0.0 collective-permute-done.refs_0_
  9.8 0.5 collective-permute-done.1.refs_1_
  10.3 3.1 %shard_map.103 = (bf16[32,32,128]{2,1,0:T(8,128)(2,1)S(1)}, f32[8,128]{1,0:T(8,128)S(1)}) custom-call(bf16[80,128]{1,0:T(8,128)(2,1)S(1)} %collective-permute-done.refs_0_, bf16[80,128]{1,0:T(8,128)(2,1)S(1)} %collective-permute-done.1.refs_1_, bf16[16,64]{1,0:T(8,128)(2,1)S(1)} %get-tuple-element.28.refs_2_, bf16[64,256]{1,0:T(8,128)(2,1)S(1)} %get-tuple-element.29.refs_3_, ...), custom_call_target="tpu_custom_call" | custom-call | tf_op jit(solution)/shard_map/pallas_call | solution.py:389
  13.4 14.9 %all_to_all.15.refs_0_ = bf16[32,32,128]{2,1,0:T(8,128)(2,1)S(1)} all-to-all(bf16[32,32,128]{2,1,0:T(8,128)(2,1)S(1)} %get-tuple-element.40), channel_id=1, replica_groups=mesh['row'=32,'col'=8] {'row'}, dimensions={0} | all-to-all | bytes 524288 | tf_op jit(solution)/shard_map/all_to_all | solution.py:400
  28.3 17.9 %all_to_all.16.refs_0_ = bf16[8,32,128]{2,1,0:T(8,128)(2,1)S(1)} all-to-all(bf16[8,32,128]{2,1,0:T(8,128)(2,1)S(1)} %shard_map.104), channel_id=1, replica_groups=mesh['row'=32,'col'=8] {'col'}, dimensions={0} | all-to-all | bytes 131072 | tf_op jit(solution)/shard_map/all_to_all | solution.py:406
  46.2 11.4 %all_to_all.17.refs_0_ = bf16[32,32,128]{2,1,0:T(8,128)(2,1)S(1)} all-to-all(bf16[32,32,128]{2,1,0:T(8,128)(2,1)S(1)} %get-tuple-element.42), channel_id=1, replica_groups=mesh['row'=32,'col'=8] {'row'}, dimensions={0} | all-to-all | bytes 524288 | tf_op jit(solution)/shard_map/all_to_all | solution.py:414
  57.6 0.9 %shard_map.106 = (f32[16,64]{1,0:T(8,128)}, f32[64,256]{1,0:T(8,128)}, f32[576,64]{1,0:T(8,128)}, f32[1,64]{1,0:T(1,128)}, f32[576,64]{1,0:T(8,128)}) custom-call(bf16[32,32,128]{2,1,0:T(8,128)(2,1)S(1)} %all_to_all.17.refs_0_, f32[16,128]{1,0:T(8,128)S(1)} %get-tuple-element.43.refs_1_), custom_call_target="tpu_custom_call" | custom-call | tf_op jit(solution)/shard_map/pallas_call | solution.py:415
  (2 shorter events, 0.1 us)
Async XLA Ops:
  1.9 7.8 %collective-permute-start = (bf16[80,128]{1,0:T(8,128)(2,1)S(1)}, bf16[80,128]{1,0:T(8,128)(2,1)S(1)}, u32[]{:S(2)}, u32[]{:S(2)}) collective-permute-start(bf16[80,128]{1,0:T(8,128)(2,1)S(1)} %get-tuple-element.27), channel_id=1, source_target_pairs={{0,1},{1,0},{2,3},{3,2},{4,5},{5,4},{6,7},{7,6},{8,17},{9,16},{10,... | collective-permute-start | bytes 61448 | tf_op jit(solution)/shard_map/ppermute | solution.py:378
  5.3 5.0 %collective-permute-start.1 = (bf16[80,128]{1,0:T(8,128)(2,1)S(1)}, bf16[80,128]{1,0:T(8,128)(2,1)S(1)}, u32[]{:S(2)}, u32[]{:S(2)}) collective-permute-start(bf16[80,128]{1,0:T(8,128)(2,1)S(1)} %get-tuple-element.27), channel_id=1, source_target_pairs={{0,8},{1,10},{2,9},{3,12},{4,11},{5,14},{6,13},{7,15},{8,0},{9,2},... | collective-permute-start | bytes 61448 | tf_op jit(solution)/shard_map/ppermute | solution.py:378

commit v10 on v7

--- a/solution.py
+++ b/solution.py
@@ -24,20 +24,31 @@
     return weights, chans, weights + 3 * chans
 
 
-def dot_split(x, y, dims):
+def split(x):
     high = x.astype(BF16)
-    low = (x - high.astype(F32)).astype(BF16)
-    y = y.astype(BF16)
-    return dot(high, y, dims) + dot(low, y, dims)
-
-
-def pack_kernel(row_hbm, col_hbm, out_ref, row_ref, col_ref, row_sem, col_sem):
-    row_copy = pltpu.make_async_copy(row_hbm, row_ref, row_sem)
-    col_copy = pltpu.make_async_copy(col_hbm, col_ref, col_sem)
-    row_copy.start()
-    col_copy.start()
-    row_copy.wait()
-    col_copy.wait()
+    return high, (x - high.astype(F32)).astype(BF16)
+
+
+def shares(n_row, j):
+    weights = 9 * CH // n_row
+    main = weights // 8 * 8
+    pieces = [(slice(0, main), slice(main * j, main * (j + 1)))]
+    if main < weights:
+        rest = weights - main
+        pieces.append((slice(main, weights), slice(main * n_row + rest * j, main * n_row + rest * (j + 1))))
+    return pieces
+
+
+def start_copies(sources, targets, sems):
+    copies = [pltpu.make_async_copy(x, y, sems.at[k]) for k, (x, y) in enumerate(zip(sources, targets, strict=True))]
+    for copy in copies:
+        copy.start()
+    return copies
+
+
+def pack_kernel(row_hbm, col_hbm, out_ref, row_ref, col_ref, sems):
+    for copy in start_copies((row_hbm, col_hbm), (row_ref, col_ref), sems):
+        copy.wait()
     rows = row_ref[...].astype(F32)
     out_ref[:16, :] = jnp.concatenate([rows, jnp.zeros_like(rows)], axis=1).astype(BF16)
     cols = col_ref.shape[1]
@@ -67,27 +78,21 @@
 
 
 def own_kernel(
-    n_col, grad_hbm, one_hbm, two_hbm, bias_hbm, row_hbm, col_hbm,
-    x_ref, back_ref, grad_rows_ref, grad_cols_ref, ind_ref, k1c_ref, k1f_ref, bias_col_ref, row_ref, col_ref,
-    rows_scr, grad_ref, one_ref, two_ref, bias_ref, sems,
+    n_col, one_hbm, two_hbm, bias_hbm, grad_hbm,
+    x_ref, back_ref, grad_rows_ref, grad_cols_ref, ind_ref, k1c_ref, k1ct_ref, k1f_ref, bias_col_ref,
+    rows_scr, one_ref, two_ref, bias_ref, grad_ref, sems,
 ):
+    copies = start_copies((one_hbm, two_hbm, bias_hbm, grad_hbm), (one_ref, two_ref, bias_ref, grad_ref), sems)
     cols = grad_ref.shape[2]
-    pairs = (
-        (one_hbm, one_ref), (two_hbm, two_ref), (bias_hbm, bias_ref), (row_hbm, row_ref), (col_hbm, col_ref),
-        (grad_hbm, grad_ref),
-    )
-    copies = [pltpu.make_async_copy(source, target, sems.at[k]) for k, (source, target) in enumerate(pairs)]
-    for copy in copies:
-        copy.start()
-    hits = indicator(cols, n_col)
-    ind_ref[...] = hits
-    for copy in copies[:-1]:
+    ind_ref[...] = indicator(cols, n_col)
+    for copy in copies[:3]:
         copy.wait()
     one = [[one_ref[a, b].astype(F32) for b in range(3)] for a in range(3)]
     for k in range(3):
         rows = slice(CH * k, CH * (k + 1))
         k1c_ref[rows, :] = jnp.concatenate(one[k], axis=1).astype(BF16)
         k1f_ref[rows, :] = jnp.concatenate([one[a][k] for a in range(3)], axis=1).astype(BF16)
+        k1ct_ref[rows, :] = jnp.concatenate([one[a][k].T for a in range(3)], axis=1).astype(BF16)
     nil = jnp.zeros((CH, CH), F32)
     two = [[two_ref[a, b].astype(F32) for b in range(3)] for a in range(3)]
     w2 = jnp.concatenate(
@@ -100,7 +105,7 @@
     ).astype(BF16)
     bias = jnp.concatenate([bias_ref[...], jnp.zeros((1, LANES - CH), F32)], axis=1)
     bias_col_ref[...] = jnp.broadcast_to(bias, (8, LANES)).T[:CH, :]
-    copies[-1].wait()
+    copies[3].wait()
     lane = lax.broadcasted_iota(jnp.int32, (CH, cols), 1)
     edge_lane = lax.broadcasted_iota(jnp.int32, (CH, LANES), 1)
     for piece in range(cols // LANES):
@@ -135,9 +140,9 @@
 
 
 def main_kernel(
-    n_row, n_col, row_twin_ref, col_twin_ref,
-    x_ref, back_ref, grad_rows_ref, grad_cols_ref, ind_ref, k1c_ref, k1f_ref, bias_ref, row_ref, col_ref,
-    out_ref, own_ref, act_scr, inner_scr, w_scr, chunk_scr,
+    n_row, n_col, row_twin_ref, col_twin_ref, row_ref, col_ref,
+    x_ref, back_ref, grad_rows_ref, grad_cols_ref, ind_ref, k1c_ref, k1ct_ref, k1f_ref, bias_ref,
+    out_ref, own_ref, w_scr, chunk_scr,
 ):
     cols = col_ref.shape[1]
     top, bottom = off_edge("row", 0), off_edge("row", n_row - 1)
@@ -148,6 +153,7 @@
     row_ext = jnp.concatenate(
         [jnp.where(odd_row, twin, other), row_ref[...].astype(F32), jnp.where(odd_row, other, twin)], axis=0
     )
+    row_taps = [row_ext[8 * a : 8 * a + 32].astype(BF16) for a in range(3)]
     row_cat = jnp.concatenate([row_ext[8 * a : 8 * a + 32] for a in range(3)], axis=1).astype(BF16)
     twin, other = col_twin_ref[16:, :].astype(F32), row_twin_ref[16:, :].astype(F32) * (left * right)
     col_ext = jnp.concatenate(
@@ -160,8 +166,8 @@
         edge = jnp.where(edge_lane < 8, low, jnp.where(edge_lane < 16, high, 0.0))
         for width in (16, 32, 64):
             edge = edge + pltpu.roll(edge, width, 1)
-        taps.append(jnp.concatenate([moved[:, LANES : LANES + cols], edge], axis=1))
-    col_cat = jnp.concatenate(taps, axis=0).astype(BF16)
+        taps.append(jnp.concatenate([moved[:, LANES : LANES + cols], edge], axis=1).astype(BF16))
+    col_cat = jnp.concatenate(taps, axis=0)
     terms = dot(k1c_ref[...], col_cat, NN)
     low, mid, high = (terms[CH * a : CH * (a + 1)] for a in range(3))
     mid = mid + bias_ref[:, :1]
@@ -182,6 +188,9 @@
     on_map = jnp.where(side_lane % 16 < 8, left, right)
     col_part = jnp.concatenate(col_part, axis=0)
     main_sum = jnp.zeros((4 * CH, cols), F32)
+    full = jnp.zeros((6 * CH, 4 * CH), F32)
+    row_of = jnp.zeros((24, 4 * CH), F32)
+    x_all = x_ref[...].reshape(6 * CH, x_ref.shape[2])
     for k in range(9):
         span = slice(k * cols, (k + 1) * cols) if k < 8 else slice(8 * cols, 8 * cols + LANES)
         if k < 8:
@@ -197,24 +206,24 @@
         held = jnp.concatenate([sig[:CH] * top, sig[CH : 3 * CH], sig[3 * CH :] * bottom], axis=0)
         if k == 8:
             held = held * on_map
-        act_scr[:, span] = (pre * held).astype(BF16)
+        full = full + dot(x_all[:, span], (pre * held).astype(BF16), NT)
         inner = (back_ref[:, span] * (held * (1.0 + pre * (1.0 - sig)))).astype(BF16)
-        inner_scr[:, span] = inner
+        row_of = row_of + dot(ind_ref[:, span], inner, NT)
         if k < 8:
             main_sum = main_sum + inner.astype(F32)
     sums = jnp.concatenate([main_sum, inner.astype(F32)], axis=1)
     sums_of = [sums[CH * eb : CH * (eb + 1)] for eb in range(4)]
 
-    full = dot(x_ref[...].reshape(6 * CH, x_ref.shape[2]), act_scr[...], NT)
-    sums = dot(ind_ref[...], inner_scr[...], NT)
     row_sums = jnp.concatenate(
         [
-            jnp.concatenate([sums[8 * b : 8 * b + 8, CH * eb : CH * (eb + 1)] for b in range(3)], axis=1)
+            jnp.concatenate([row_of[8 * b : 8 * b + 8, CH * eb : CH * (eb + 1)] for b in range(3)], axis=1)
             for eb in range(4)
         ],
         axis=0,
     )
-    spread_row = dot_split(row_sums, k1f_ref[...], NN)
+    row_split = jnp.concatenate(split(row_sums), axis=0)
+    spread_row = dot(row_split, k1f_ref[...], NN)
+    spread_row = spread_row[:32] + spread_row[32:]
 
     def part(eb, a):
         return spread_row[8 * eb : 8 * eb + 8, CH * a : CH * (a + 1)]
@@ -226,10 +235,9 @@
     col_sums = jnp.concatenate(
         [whole - (1.0 - top) * sums_of[1], whole, whole - (1.0 - bottom) * sums_of[2]], axis=0
     )
-    high = col_sums.astype(BF16)
-    rest = (col_sums - high.astype(F32)).astype(BF16)
-    k1c = k1c_ref[...]
-    spread_col = dot(k1c, high, TN) + dot(k1c, rest, TN)
+    col_split = jnp.concatenate(split(col_sums), axis=1)
+    spread_col = dot(k1ct_ref[...], col_split, NN)
+    spread_col = spread_col[:, : cols + LANES] + spread_col[:, cols + LANES :]
     nothing = jnp.zeros((CH, LANES), F32)
     total = jnp.concatenate([nothing, grad_cols_ref[...], nothing], axis=1)
     for tap in range(3):
@@ -241,14 +249,13 @@
         high_edge = jnp.where(edge_lane < 8, pltpu.roll(edge, LANES - 8, 1), 0.0)
         piece = jnp.concatenate([low, piece[:, :cols], high_edge], axis=1)
         total = total + (pltpu.roll(piece, (8 * (tap - 1)) % (cols + 2 * LANES), 1) if tap != 1 else piece)
-    one_row = dot_split(row_sums, row_cat, TN)
-    one_col = dot(high, col_cat, NT) + dot(rest, col_cat, NT)
+    one_row = [dot(row_split, jnp.concatenate([piece, piece], axis=0), TN) for piece in row_taps]
+    one_col = [dot(col_split, jnp.concatenate([piece, piece], axis=1), NT) for piece in taps]
     bias_row = jnp.sum(row_sums[:, :LANES], axis=0, keepdims=True)
     bias_row = pltpu.roll(jnp.where(lax.broadcasted_iota(jnp.int32, (8, LANES), 1) >= CH, bias_row, 0.0), 96, 1)
     for a in range(3):
         for b in range(3):
-            one = one_row[CH * b : CH * (b + 1), CH * a : CH * (a + 1)]
-            one = one + one_col[CH * a : CH * (a + 1), CH * b : CH * (b + 1)]
+            one = one_row[a][CH * b : CH * (b + 1)] + one_col[b][CH * a : CH * (a + 1)]
             two = [
                 full[CH * (2 * b + gb) : CH * (2 * b + gb + 1), CH * (a + gb) : CH * (a + gb + 1)] for gb in range(2)
             ]
@@ -258,7 +265,8 @@
     tail = total[:, :LANES] + total[:, cols + LANES :] + bias_row[:1, :]
     before = lax.axis_index("row") - 1
     for j in range(n_row):
-        chunk_scr[j, :weights, :] = w_scr[weights * j : weights * (j + 1), :]
+        for there, here in shares(n_row, j):
+            chunk_scr[j, there, :] = w_scr[here, :]
         share = slice(chans * j, chans * (j + 1))
         chunk_scr[j, weights : weights + chans, :] = total[share, LANES : 2 * LANES]
         chunk_scr[j, weights + chans : weights + 2 * chans, :] = total[share, cols : cols + LANES]
@@ -282,17 +290,15 @@
         out_ref[k] = whole
 
 
-def col_sum_kernel(n_row, n_col, cols, got_ref, row_ref, bias_ref, out_ref, scr):
+def col_sum_kernel(n_row, n_col, cols, got_ref, kept_ref, out_ref, scr):
     weights, chans, sums_end = chunk_rows(n_row)
     me = lax.axis_index("col")
     whole = math.sqrt(16 * n_row * cols * n_col)
     total = got_ref[0].astype(F32)
     for k in range(1, n_col):
         total = total + got_ref[k].astype(F32)
-    rows = total[sums_end:, :] * (1.0 / math.sqrt(cols * n_col))
-    row_ref[0:8, :] = rows[:, :CH]
-    row_ref[8:16, :] = rows[:, CH:]
-    bias_ref[...] = total[sums_end - 1 : sums_end, 32 : 32 + CH] * (1.0 / whole)
+    kept_ref[:8, :] = total[sums_end:, :] * (1.0 / math.sqrt(cols * n_col))
+    kept_ref[8:, :] = total[sums_end - 8 : sums_end, :] * (1.0 / whole)
     before = got_ref[jnp.maximum(me - 1, 0)].astype(F32) * off_edge("col", 0)
     after = got_ref[jnp.minimum(me + 1, n_col - 1)].astype(F32) * off_edge("col", n_col - 1)
     mine = got_ref[me].astype(F32)
@@ -310,12 +316,16 @@
         out_ref[j] = share
 
 
-def spread_kernel(n_row, got_ref, col_ref, one_ref, two_ref):
+def spread_kernel(n_row, got_ref, kept_ref, row_ref, col_ref, one_ref, bias_ref, two_ref):
     weights, chans, _ = chunk_rows(n_row)
+    row_ref[:8, :] = kept_ref[:8, :CH]
+    row_ref[8:, :] = kept_ref[:8, CH:]
+    bias_ref[...] = kept_ref[15:, 32 : 32 + CH]
     for j in range(n_row):
         chunk = got_ref[j].astype(F32)
-        one_ref[weights * j : weights * (j + 1), :] = chunk[:weights, :CH]
-        two_ref[weights * j : weights * (j + 1), :] = chunk[:weights, CH:]
+        for there, here in shares(n_row, j):
+            one_ref[here, :] = chunk[there, :CH]
+            two_ref[here, :] = chunk[there, CH:]
         col_ref[chans * j : chans * (j + 1), :LANES] = chunk[weights : weights + chans]
         col_ref[chans * j : chans * (j + 1), LANES:] = chunk[weights + chans : weights + 2 * chans]
 
@@ -335,16 +345,11 @@
         pltpu.with_memory_space_constraint(x, pltpu.HBM)
         for x in (grad_out, row_feat, col_feat.T, conv_one, conv_two, bias_one.reshape(1, CH))
     )
-    strip = pl.pallas_call(
+    strip, *feats = pl.pallas_call(
         pack_kernel,
-        out_shape=sds((16 + CH, LANES), BF16),
+        out_shape=(sds((16 + CH, LANES), BF16), sds(row_feat.shape, BF16), sds(col_turned.shape, BF16)),
         in_specs=[pl.BlockSpec(memory_space=pltpu.HBM)] * 2,
-        scratch_shapes=[
-            pltpu.VMEM((16, CH), BF16),
-            pltpu.VMEM((CH, cols), BF16),
-            pltpu.SemaphoreType.DMA,
-            pltpu.SemaphoreType.DMA,
-        ],
+        scratch_shapes=[pltpu.SemaphoreType.DMA((2,))],
         compiler_params=PARAMS,
     )(row_feat, col_turned)
 
@@ -362,38 +367,36 @@
         ]
         return lax.ppermute(strip, ("row", "col"), pairs)
 
+    col_twin = swap(other, twin)
     row_twin = swap(twin, other)
-    col_twin = swap(other, twin)
-
+
+    square = sds((3 * CH, 3 * CH), BF16)
     held = pl.pallas_call(
         lambda *refs: own_kernel(n_col, *refs),
         out_shape=(
             sds((3, 2 * CH, places), BF16), sds((4 * CH, places)), sds((8, 2 * CH)), sds((CH, cols)),
-            sds((24, places), BF16), sds((3 * CH, 3 * CH), BF16), sds((3 * CH, 3 * CH), BF16), sds((CH, 8)),
-            sds((16, CH), BF16), sds((CH, cols), BF16),
+            sds((24, places), BF16), square, square, square, sds((CH, 8)),
         ),
-        in_specs=[pl.BlockSpec(memory_space=pltpu.HBM)] * 6,
+        in_specs=[pl.BlockSpec(memory_space=pltpu.HBM)] * 4,
         scratch_shapes=[
             pltpu.VMEM((cols // LANES, CH * 16, LANES), F32),
-            pltpu.VMEM(grad_out.shape, BF16),
             pltpu.VMEM(conv_one.shape, BF16),
             pltpu.VMEM(conv_two.shape, BF16),
             pltpu.VMEM((1, CH), F32),
-            pltpu.SemaphoreType.DMA((6,)),
+            pltpu.VMEM(grad_out.shape, BF16),
+            pltpu.SemaphoreType.DMA((4,)),
         ],
         compiler_params=PARAMS,
-    )(grad_out, conv_one, conv_two, bias_row, row_feat, col_turned)
+    )(conv_one, conv_two, bias_row, grad_out)
     chunks, own = pl.pallas_call(
         lambda *refs: main_kernel(n_row, n_col, *refs),
         out_shape=(sds((n_row, sums_end + 8, LANES), BF16), sds((8, LANES))),
         scratch_shapes=[
-            pltpu.VMEM((4 * CH, places), BF16),
-            pltpu.VMEM((4 * CH, places), BF16),
             pltpu.VMEM((9 * CH, LANES), F32),
             pltpu.VMEM((n_row, sums_end + 8, LANES), F32),
         ],
         compiler_params=PARAMS,
-    )(row_twin, col_twin, *held)
+    )(row_twin, col_twin, *feats, *held)
     got = lax.all_to_all(chunks, "row", 0, 0)
     copies = pl.pallas_call(
         lambda *refs: row_sum_kernel(n_row, n_col, *refs),
@@ -402,18 +405,18 @@
     )(got, own)
     got = lax.all_to_all(copies, "col", 0, 0)
     end = -(-(weights + 2 * chans) // 16) * 16
-    row_grad, bias_grad, copies = pl.pallas_call(
+    kept, copies = pl.pallas_call(
         lambda *refs: col_sum_kernel(n_row, n_col, cols, *refs),
-        out_shape=(sds((16, CH)), sds((1, CH)), sds((n_row, end, LANES), BF16)),
+        out_shape=(sds((16, LANES)), sds((n_row, end, LANES), BF16)),
         scratch_shapes=[pltpu.VMEM((end, LANES), F32)],
         compiler_params=PARAMS,
     )(got)
     got = lax.all_to_all(copies, "row", 0, 0)
-    col_grad, one, two = pl.pallas_call(
+    row_grad, col_grad, one, bias_grad, two = pl.pallas_call(
         lambda *refs: spread_kernel(n_row, *refs),
-        out_shape=(sds((CH, cols)), sds((9 * CH, CH)), sds((9 * CH, CH))),
-        compiler_params=PARAMS,
-    )(got)
+        out_shape=(sds((16, CH)), sds((CH, cols)), sds((9 * CH, CH)), sds((1, CH)), sds((9 * CH, CH))),
+        compiler_params=PARAMS,
+    )(got, kept)
     shape = conv_one.shape
     return row_grad, col_grad.T, one.reshape(shape), bias_grad[0], two.reshape(shape)
 

time: 58.9 us -> 58.1 us (0.986)
  Pallas kernels: 8.12 us -> 7.33 us
    pallas_call x1, Pallas kernels: 0.68 us -> 0.04 us  [shards(): pl.pallas_call(lambda *refs: col_sum_kernel(n_row, n_col, cols, *refs), o...]
  transfers between devices with their start and end apart: 2 -> 2, of which waited for: 0 -> 0; matrix products, arithmetic and copies ran while one was open for 0% -> 0% of each run, Pallas kernels for 4% -> 5%
where the time goes in v10:
time: 58.1 us; the launch traced here: 57.8 us
  blocking collectives  43.3 us (75%)
  Pallas kernels  7.33 us (13%)
  starting transfers between devices  6.5 us (11%)
  between operations  0.67 us (1%)
    all_to_all x1, blocking collectives, shards(): got = lax.all_to_all(chunks, 'row', 0, 0)  16.4 us
    all_to_all x1, blocking collectives, shards(): got = lax.all_to_all(copies, 'col', 0, 0)  15.5 us
    all_to_all x1, blocking collectives, shards(): got = lax.all_to_all(copies, 'row', 0, 0)  11.4 us
    ppermute x2, starting transfers between devices, swap(): return lax.ppermute(strip, ('row', 'col'), pairs)  6.5 us
    pallas_call x1, Pallas kernels, shards(): pl.pallas_call(lambda *refs: main_kernel(n_row, n_col, *refs), out_shape=...  2.93 us
    pallas_call x1, Pallas kernels, shards(): pl.pallas_call(lambda *refs: own_kernel(n_col, *refs), out_shape=(sds((3,...  2.63 us
  transfers between devices with their start and end apart: 2, of which 0 were waited for; matrix products, arithmetic and copies ran while one was open for 0% of the time, Pallas kernels for 5%

profile of v10, /device:TPU:1, one launch (start us, length us, event | category | flops | bytes accessed | tf_op | source)
XLA Modules:
  0.0 57.8 jit_solution(10877278067676892314)
XLA Ops:
  0.6 0.8 %shard_map.101 = (bf16[80,128]{1,0:T(8,128)(2,1)S(1)}, bf16[16,64]{1,0:T(8,128)(2,1)S(1)}, bf16[64,256]{1,0:T(8,128)(2,1)S(1)}) custom-call(bf16[16,64]{1,0:T(8,128)(2,1)} %row_hbm.1, bf16[64,256]{1,0:T(8,128)(2,1)} %bitcast.6), custom_call_target="tpu_custom_call" | custom-call | tf_op jit(solution)/shard_map/pallas_call | solution.py:348
  1.4 3.3 %collective-permute-start.1 = (bf16[80,128]{1,0:T(8,128)(2,1)S(1)}, bf16[80,128]{1,0:T(8,128)(2,1)S(1)}, u32[]{:S(2)}, u32[]{:S(2)}) collective-permute-start(bf16[80,128]{1,0:T(8,128)(2,1)S(1)} %get-tuple-element.26), channel_id=1, source_target_pairs={{0,1},{1,0},{2,3},{3,2},{4,5},{5,4},{6,7},{7,6},{8,17},{9,16},{10,... | collective-permute-start | bytes 61448 | tf_op jit(solution)/shard_map/ppermute | solution.py:368
  4.8 3.2 %collective-permute-start = (bf16[80,128]{1,0:T(8,128)(2,1)S(1)}, bf16[80,128]{1,0:T(8,128)(2,1)S(1)}, u32[]{:S(2)}, u32[]{:S(2)}) collective-permute-start(bf16[80,128]{1,0:T(8,128)(2,1)S(1)} %get-tuple-element.26), channel_id=1, source_target_pairs={{0,8},{1,10},{2,9},{3,12},{4,11},{5,14},{6,13},{7,15},{8,0},{9,2},... | collective-permute-start | bytes 61448 | tf_op jit(solution)/shard_map/ppermute | solution.py:368
  7.9 2.6 %shard_map.102 = (bf16[3,128,2176]{2,1,0:T(8,128)(2,1)S(1)}, f32[256,2176]{1,0:T(8,128)S(1)}, f32[8,128]{1,0:T(8,128)S(1)}, f32[64,256]{1,0:T(8,128)S(1)}, bf16[...) custom-call(bf16[3,3,64,64]{3,2,1,0:T(8,128)(2,1)} %refs_0_.1, ...), custom_call_target="tpu_custom_call" | custom-call | tf_op jit(solution)/shard_map/pallas_call | solution.py:374
  10.6 0.0 collective-permute-done.1.refs_1_
  10.6 0.0 collective-permute-done.refs_0_
  10.6 2.9 %shard_map.103 = (bf16[32,32,128]{2,1,0:T(8,128)(2,1)S(1)}, f32[8,128]{1,0:T(8,128)S(1)}) custom-call(bf16[80,128]{1,0:T(8,128)(2,1)S(1)} %collective-permute-done.refs_0_, bf16[80,128]{1,0:T(8,128)(2,1)S(1)} %collective-permute-done.1.refs_1_, bf16[16,64]{1,0:T(8,128)(2,1)S(1)} %get-tuple-element.27.refs_2_, bf16[64,256]{1,0:T(8,128)(2,1)S(1)} %get-tuple-element.28.refs_3_, ...), custom_call_target="tpu_custom_call" | custom-call | tf_op jit(solution)/shard_map/pallas_call | solution.py:391
  13.5 16.4 %all_to_all.15.refs_0_ = bf16[32,32,128]{2,1,0:T(8,128)(2,1)S(1)} all-to-all(bf16[32,32,128]{2,1,0:T(8,128)(2,1)S(1)} %get-tuple-element.38), channel_id=1, replica_groups=mesh['row'=32,'col'=8] {'row'}, dimensions={0} | all-to-all | bytes 524288 | tf_op jit(solution)/shard_map/all_to_all | solution.py:400
  30.0 15.5 %all_to_all.16.refs_0_ = bf16[8,32,128]{2,1,0:T(8,128)(2,1)S(1)} all-to-all(bf16[8,32,128]{2,1,0:T(8,128)(2,1)S(1)} %shard_map.104), channel_id=1, replica_groups=mesh['row'=32,'col'=8] {'col'}, dimensions={0} | all-to-all | bytes 131072 | tf_op jit(solution)/shard_map/all_to_all | solution.py:406
  45.5 11.4 %all_to_all.17.refs_0_ = bf16[32,32,128]{2,1,0:T(8,128)(2,1)S(1)} all-to-all(bf16[32,32,128]{2,1,0:T(8,128)(2,1)S(1)} %get-tuple-element.40), channel_id=1, replica_groups=mesh['row'=32,'col'=8] {'row'}, dimensions={0} | all-to-all | bytes 524288 | tf_op jit(solution)/shard_map/all_to_all | solution.py:414
  56.9 0.9 %shard_map.106 = (f32[16,64]{1,0:T(8,128)}, f32[64,256]{1,0:T(8,128)}, f32[576,64]{1,0:T(8,128)}, f32[1,64]{1,0:T(1,128)}, f32[576,64]{1,0:T(8,128)}) custom-call(bf16[32,32,128]{2,1,0:T(8,128)(2,1)S(1)} %all_to_all.17.refs_0_, f32[16,128]{1,0:T(8,128)S(1)} %get-tuple-element.41.refs_1_), custom_call_target="tpu_custom_call" | custom-call | tf_op jit(solution)/shard_map/pallas_call | solution.py:415
  (2 shorter events, 0.1 us)
Async XLA Ops:
  1.4 9.1 %collective-permute-start.1 = (bf16[80,128]{1,0:T(8,128)(2,1)S(1)}, bf16[80,128]{1,0:T(8,128)(2,1)S(1)}, u32[]{:S(2)}, u32[]{:S(2)}) collective-permute-start(bf16[80,128]{1,0:T(8,128)(2,1)S(1)} %get-tuple-element.26), channel_id=1, source_target_pairs={{0,1},{1,0},{2,3},{3,2},{4,5},{5,4},{6,7},{7,6},{8,17},{9,16},{10,... | collective-permute-start | bytes 61448 | tf_op jit(solution)/shard_map/ppermute | solution.py:368
  4.8 5.8 %collective-permute-start = (bf16[80,128]{1,0:T(8,128)(2,1)S(1)}, bf16[80,128]{1,0:T(8,128)(2,1)S(1)}, u32[]{:S(2)}, u32[]{:S(2)}) collective-permute-start(bf16[80,128]{1,0:T(8,128)(2,1)S(1)} %get-tuple-element.26), channel_id=1, source_target_pairs={{0,8},{1,10},{2,9},{3,12},{4,11},{5,14},{6,13},{7,15},{8,0},{9,2},... | collective-permute-start | bytes 61448 | tf_op jit(solution)/shard_map/ppermute | solution.py:368

commit v11 on v10

--- a/solution.py
+++ b/solution.py
@@ -44,17 +44,6 @@
     for copy in copies:
         copy.start()
     return copies
-
-
-def pack_kernel(row_hbm, col_hbm, out_ref, row_ref, col_ref, sems):
-    for copy in start_copies((row_hbm, col_hbm), (row_ref, col_ref), sems):
-        copy.wait()
-    rows = row_ref[...].astype(F32)
-    out_ref[:16, :] = jnp.concatenate([rows, jnp.zeros_like(rows)], axis=1).astype(BF16)
-    cols = col_ref.shape[1]
-    lane = lax.broadcasted_iota(jnp.int32, (CH, LANES), 1)
-    first, last = col_ref[:, :LANES].astype(F32), col_ref[:, cols - LANES :].astype(F32)
-    out_ref[16:, :] = jnp.where(lane < LANES // 2, first, last).astype(BF16)
 
 
 def off_edge(axis, index):
@@ -78,14 +67,18 @@
 
 
 def own_kernel(
-    n_col, one_hbm, two_hbm, bias_hbm, grad_hbm,
-    x_ref, back_ref, grad_rows_ref, grad_cols_ref, ind_ref, k1c_ref, k1ct_ref, k1f_ref, bias_col_ref,
+    n_col, one_hbm, two_hbm, bias_hbm, row_hbm, col_hbm, grad_hbm,
+    x_ref, back_ref, grad_rows_ref, grad_cols_ref, ind_ref, k1c_ref, k1ct_ref, k1f_ref, bias_col_ref, row_ref, col_ref,
     rows_scr, one_ref, two_ref, bias_ref, grad_ref, sems,
 ):
-    copies = start_copies((one_hbm, two_hbm, bias_hbm, grad_hbm), (one_ref, two_ref, bias_ref, grad_ref), sems)
+    copies = start_copies(
+        (one_hbm, two_hbm, bias_hbm, row_hbm, col_hbm, grad_hbm),
+        (one_ref, two_ref, bias_ref, row_ref, col_ref, grad_ref),
+        sems,
+    )
     cols = grad_ref.shape[2]
     ind_ref[...] = indicator(cols, n_col)
-    for copy in copies[:3]:
+    for copy in copies[:5]:
         copy.wait()
     one = [[one_ref[a, b].astype(F32) for b in range(3)] for a in range(3)]
     for k in range(3):
@@ -105,7 +98,7 @@
     ).astype(BF16)
     bias = jnp.concatenate([bias_ref[...], jnp.zeros((1, LANES - CH), F32)], axis=1)
     bias_col_ref[...] = jnp.broadcast_to(bias, (8, LANES)).T[:CH, :]
-    copies[3].wait()
+    copies[5].wait()
     lane = lax.broadcasted_iota(jnp.int32, (CH, cols), 1)
     edge_lane = lax.broadcasted_iota(jnp.int32, (CH, LANES), 1)
     for piece in range(cols // LANES):
@@ -140,25 +133,25 @@
 
 
 def main_kernel(
-    n_row, n_col, row_twin_ref, col_twin_ref, row_ref, col_ref,
+    n_row, n_col, row_twin_ref, row_other_ref, col_other_ref, col_twin_ref,
     x_ref, back_ref, grad_rows_ref, grad_cols_ref, ind_ref, k1c_ref, k1ct_ref, k1f_ref, bias_ref,
-    out_ref, own_ref, w_scr, chunk_scr,
+    row_ref, col_ref, out_ref, own_ref, w_scr, chunk_scr,
 ):
     cols = col_ref.shape[1]
     top, bottom = off_edge("row", 0), off_edge("row", n_row - 1)
     left, right = off_edge("col", 0), off_edge("col", n_col - 1)
     edge_lane = lax.broadcasted_iota(jnp.int32, (CH, LANES), 1)
     odd_row, odd_col = lax.axis_index("row") % 2 == 1, lax.axis_index("col") % 2 == 1
-    twin, other = row_twin_ref[:16, :CH].astype(F32), col_twin_ref[:16, :CH].astype(F32) * (top * bottom)
+    twin, other = row_twin_ref[...].astype(F32), row_other_ref[...].astype(F32) * (top * bottom)
     row_ext = jnp.concatenate(
         [jnp.where(odd_row, twin, other), row_ref[...].astype(F32), jnp.where(odd_row, other, twin)], axis=0
     )
     row_taps = [row_ext[8 * a : 8 * a + 32].astype(BF16) for a in range(3)]
     row_cat = jnp.concatenate([row_ext[8 * a : 8 * a + 32] for a in range(3)], axis=1).astype(BF16)
-    twin, other = col_twin_ref[16:, :].astype(F32), row_twin_ref[16:, :].astype(F32) * (left * right)
-    col_ext = jnp.concatenate(
-        [jnp.where(odd_col, twin, other), col_ref[...].astype(F32), jnp.where(odd_col, other, twin)], axis=1
-    )
+    twin, other = col_twin_ref[...].astype(F32), col_other_ref[...].astype(F32) * (left * right)
+    before = jnp.where(odd_col, twin[:, cols - LANES :], other[:, cols - LANES :])
+    after = jnp.where(odd_col, other[:, :LANES], twin[:, :LANES])
+    col_ext = jnp.concatenate([before, col_ref[...].astype(F32), after], axis=1)
     taps = []
     for tap in range(3):
         moved = pltpu.roll(col_ext, (8 * (1 - tap)) % (cols + 2 * LANES), 1) if tap != 1 else col_ext
@@ -188,9 +181,9 @@
     on_map = jnp.where(side_lane % 16 < 8, left, right)
     col_part = jnp.concatenate(col_part, axis=0)
     main_sum = jnp.zeros((4 * CH, cols), F32)
-    full = jnp.zeros((6 * CH, 4 * CH), F32)
+    two = jnp.zeros((3 * CH, 3 * CH), F32)
     row_of = jnp.zeros((24, 4 * CH), F32)
-    x_all = x_ref[...].reshape(6 * CH, x_ref.shape[2])
+    x_half = [jnp.concatenate([x_ref[b, CH * gb : CH * (gb + 1), :] for b in range(3)], axis=0) for gb in range(2)]
     for k in range(9):
         span = slice(k * cols, (k + 1) * cols) if k < 8 else slice(8 * cols, 8 * cols + LANES)
         if k < 8:
@@ -206,7 +199,8 @@
         held = jnp.concatenate([sig[:CH] * top, sig[CH : 3 * CH], sig[3 * CH :] * bottom], axis=0)
         if k == 8:
             held = held * on_map
-        full = full + dot(x_all[:, span], (pre * held).astype(BF16), NT)
+        act = (pre * held).astype(BF16)
+        two = two + dot(x_half[0][:, span], act[: 3 * CH], NT) + dot(x_half[1][:, span], act[CH:], NT)
         inner = (back_ref[:, span] * (held * (1.0 + pre * (1.0 - sig)))).astype(BF16)
         row_of = row_of + dot(ind_ref[:, span], inner, NT)
         if k < 8:
@@ -256,10 +250,8 @@
     for a in range(3):
         for b in range(3):
             one = one_row[a][CH * b : CH * (b + 1)] + one_col[b][CH * a : CH * (a + 1)]
-            two = [
-                full[CH * (2 * b + gb) : CH * (2 * b + gb + 1), CH * (a + gb) : CH * (a + gb + 1)] for gb in range(2)
-            ]
-            w_scr[CH * (3 * a + b) : CH * (3 * a + b + 1), :] = jnp.concatenate([one, two[0] + two[1]], axis=1)
+            pair = jnp.concatenate([one, two[CH * b : CH * (b + 1), CH * a : CH * (a + 1)]], axis=1)
+            w_scr[CH * (3 * a + b) : CH * (3 * a + b + 1), :] = pair
 
     weights, chans, sums_end = chunk_rows(n_row)
     tail = total[:, :LANES] + total[:, cols + LANES :] + bias_row[:1, :]
@@ -341,17 +333,11 @@
     cols = grad_out.shape[2]
     weights, chans, sums_end = chunk_rows(n_row)
     places = 8 * cols + LANES
+    rows, columns = row_feat, col_feat.T
     grad_out, row_feat, col_turned, conv_one, conv_two, bias_row = (
         pltpu.with_memory_space_constraint(x, pltpu.HBM)
         for x in (grad_out, row_feat, col_feat.T, conv_one, conv_two, bias_one.reshape(1, CH))
     )
-    strip, *feats = pl.pallas_call(
-        pack_kernel,
-        out_shape=(sds((16 + CH, LANES), BF16), sds(row_feat.shape, BF16), sds(col_turned.shape, BF16)),
-        in_specs=[pl.BlockSpec(memory_space=pltpu.HBM)] * 2,
-        scratch_shapes=[pltpu.SemaphoreType.DMA((2,))],
-        compiler_params=PARAMS,
-    )(row_feat, col_turned)
 
     def twin(index, count):
         return index ^ 1
@@ -359,16 +345,16 @@
     def other(index, count):
         return min(max(index + (1 if index % 2 else -1), 0), count - 1)
 
-    def swap(along_row, along_col):
+    def swap(x, along_row, along_col):
         pairs = [
             (r * n_col + c, along_row(r, n_row) * n_col + along_col(c, n_col))
             for r in range(n_row)
             for c in range(n_col)
         ]
-        return lax.ppermute(strip, ("row", "col"), pairs)
-
-    col_twin = swap(other, twin)
-    row_twin = swap(twin, other)
+        return lax.ppermute(x, ("row", "col"), pairs)
+
+    row_other, row_twin = swap(rows, other, twin), swap(rows, twin, other)
+    col_twin, col_other = swap(columns, other, twin), swap(columns, twin, other)
 
     square = sds((3 * CH, 3 * CH), BF16)
     held = pl.pallas_call(
@@ -376,18 +362,19 @@
         out_shape=(
             sds((3, 2 * CH, places), BF16), sds((4 * CH, places)), sds((8, 2 * CH)), sds((CH, cols)),
             sds((24, places), BF16), square, square, square, sds((CH, 8)),
+            sds(row_feat.shape, BF16), sds(col_turned.shape, BF16),
         ),
-        in_specs=[pl.BlockSpec(memory_space=pltpu.HBM)] * 4,
+        in_specs=[pl.BlockSpec(memory_space=pltpu.HBM)] * 6,
         scratch_shapes=[
             pltpu.VMEM((cols // LANES, CH * 16, LANES), F32),
             pltpu.VMEM(conv_one.shape, BF16),
             pltpu.VMEM(conv_two.shape, BF16),
             pltpu.VMEM((1, CH), F32),
             pltpu.VMEM(grad_out.shape, BF16),
-            pltpu.SemaphoreType.DMA((4,)),
+            pltpu.SemaphoreType.DMA((6,)),
         ],
         compiler_params=PARAMS,
-    )(conv_one, conv_two, bias_row, grad_out)
+    )(conv_one, conv_two, bias_row, row_feat, col_turned, grad_out)
     chunks, own = pl.pallas_call(
         lambda *refs: main_kernel(n_row, n_col, *refs),
         out_shape=(sds((n_row, sums_end + 8, LANES), BF16), sds((8, LANES))),
@@ -396,7 +383,7 @@
             pltpu.VMEM((n_row, sums_end + 8, LANES), F32),
         ],
         compiler_params=PARAMS,
-    )(row_twin, col_twin, *feats, *held)
+    )(row_twin, row_other, col_other, col_twin, *held)
     got = lax.all_to_all(chunks, "row", 0, 0)
     copies = pl.pallas_call(
         lambda *refs: row_sum_kernel(n_row, n_col, *refs),

time: 58.1 us -> 62.6 us (1.077)
  blocking collectives: 43.3 us -> 46.4 us
  waiting for transfers between devices: 0.01 us -> 2.02 us
  Pallas kernels: 7.33 us -> 6.36 us
    all_to_all x1, blocking collectives: 15.5 us -> 18 us  [shards(): got = lax.all_to_all(copies, 'col', 0, 0)]
    ppermute x2 -> x4, waiting for transfers between devices: 0.01 us -> 2.02 us  [swap(): return lax.ppermute(x, ('row', 'col'), pairs)]
    pallas_call x1 -> x0, Pallas kernels: 0.8 us -> none  [shards(): pl.pallas_call(pack_kernel, out_shape=(sds((16 + CH, LANES), BF16), sds(r...]
    ppermute x2 -> x4, starting transfers between devices: 6.5 us -> 6.87 us  [swap(): return lax.ppermute(x, ('row', 'col'), pairs)]
  transfers between devices with their start and end apart: 2 -> 4, of which waited for: 0 -> 1; matrix products, arithmetic and copies ran while one was open for 0% -> 0% of each run, Pallas kernels for 5% -> 4%
where the time goes in v11:
time: 62.6 us; the launch traced here: 62.3 us
  blocking collectives  46.4 us (74%)
  starting transfers between devices  6.87 us (11%)
  Pallas kernels  6.36 us (10%)
  waiting for transfers between devices  2.02 us (3%)
  between operations  0.66 us (1%)
    all_to_all x1, blocking collectives, shards(): got = lax.all_to_all(copies, 'col', 0, 0)  18 us
    all_to_all x1, blocking collectives, shards(): got = lax.all_to_all(chunks, 'row', 0, 0)  17 us
    all_to_all x1, blocking collectives, shards(): got = lax.all_to_all(copies, 'row', 0, 0)  11.4 us
    ppermute x4, starting transfers between devices, swap(): return lax.ppermute(x, ('row', 'col'), pairs)  6.87 us
    pallas_call x1, Pallas kernels, shards(): pl.pallas_call(lambda *refs: main_kernel(n_row, n_col, *refs), out_shape=...  2.76 us
    pallas_call x1, Pallas kernels, shards(): pl.pallas_call(lambda *refs: own_kernel(n_col, *refs), out_shape=(sds((3,...  2.64 us
    ppermute x4, waiting for transfers between devices, swap(): return lax.ppermute(x, ('row', 'col'), pairs)  2.02 us
  transfers between devices with their start and end apart: 4, of which 1 were waited for; matrix products, arithmetic and copies ran while one was open for 0% of the time, Pallas kernels for 4%

profile of v11, /device:TPU:1, one launch (start us, length us, event | category | flops | bytes accessed | tf_op | source)
XLA Modules:
  0.0 62.3 jit_solution(15873814463498467884)
XLA Ops:
  0.6 3.3 %collective-permute-start.3 = (bf16[64,256]{1,0:T(8,128)(2,1)}, bf16[64,256]{1,0:T(8,128)(2,1)S(1)}, u32[]{:S(2)}, u32[]{:S(2)}) collective-permute-start(bf16[64,256]{1,0:T(8,128)(2,1)} %bitcast.6), channel_id=1, source_target_pairs={{0,1},{1,0},{2,3},{3,2},{4,5},{5,4},{6,7},{7,6},{8,17},{9,16},{10,... | collective-permute-start | bytes 98312 | tf_op jit(solution)/shard_map/ppermute | solution.py:354
  4.0 3.2 %collective-permute-start.2 = (bf16[64,256]{1,0:T(8,128)(2,1)}, bf16[64,256]{1,0:T(8,128)(2,1)S(1)}, u32[]{:S(2)}, u32[]{:S(2)}) collective-permute-start(bf16[64,256]{1,0:T(8,128)(2,1)} %bitcast.7), channel_id=1, source_target_pairs={{0,8},{1,10},{2,9},{3,12},{4,11},{5,14},{6,13},{7,15},{8,0},{9,2},... | collective-permute-start | bytes 98312 | tf_op jit(solution)/shard_map/ppermute | solution.py:354
  7.1 0.4 collective-permute-start
  7.5 0.0 collective-permute-start.1
  7.5 2.6 %shard_map.101 = (bf16[3,128,2176]{2,1,0:T(8,128)(2,1)S(1)}, f32[256,2176]{1,0:T(8,128)S(1)}, f32[8,128]{1,0:T(8,128)S(1)}, f32[64,256]{1,0:T(8,128)S(1)}, bf16[...) custom-call(bf16[3,3,64,64]{3,2,1,0:T(8,128)(2,1)} %refs_0_.1, ...), custom_call_target="tpu_custom_call" | custom-call | tf_op jit(solution)/shard_map/pallas_call | solution.py:360
  10.2 2.0 %collective-permute-done.refs_0_ = bf16[16,64]{1,0:T(8,128)(2,1)S(1)} collective-permute-done((bf16[16,64]{1,0:T(8,128)(2,1)}, bf16[16,64]{1,0:T(8,128)(2,1)S(1)}, u32[]{:S(2)}, u32[]{:S(2)}) %collective-permute-start) | collective-permute-done | bytes 2080 | tf_op jit(solution)/shard_map/ppermute | solution.py:354
  12.2 0.0 collective-permute-done.1.refs_1_
  12.2 0.0 collective-permute-done.3.refs_3_
  12.2 0.0 collective-permute-done.2.refs_2_
  12.2 2.8 %shard_map.102 = (bf16[32,32,128]{2,1,0:T(8,128)(2,1)S(1)}, f32[8,128]{1,0:T(8,128)S(1)}) custom-call(bf16[16,64]{1,0:T(8,128)(2,1)S(1)} %collective-permute-done.refs_0_, bf16[16,64]{1,0:T(8,128)(2,1)S(1)} %collective-permute-done.1.refs_1_, bf16[64,256]{1,0:T(8,128)(2,1)S(1)} %collective-permute-done.2.refs_2_, ...), custom_call_target="tpu_custom_call" | custom-call | tf_op jit(solution)/shard_map/pallas_call | solution.py:378
  15.0 17.0 %all_to_all.15.refs_0_ = bf16[32,32,128]{2,1,0:T(8,128)(2,1)S(1)} all-to-all(bf16[32,32,128]{2,1,0:T(8,128)(2,1)S(1)} %get-tuple-element.36), channel_id=1, replica_groups=mesh['row'=32,'col'=8] {'row'}, dimensions={0} | all-to-all | bytes 524288 | tf_op jit(solution)/shard_map/all_to_all | solution.py:387
  32.0 18.0 %all_to_all.16.refs_0_ = bf16[8,32,128]{2,1,0:T(8,128)(2,1)S(1)} all-to-all(bf16[8,32,128]{2,1,0:T(8,128)(2,1)S(1)} %shard_map.103), channel_id=1, replica_groups=mesh['row'=32,'col'=8] {'col'}, dimensions={0} | all-to-all | bytes 131072 | tf_op jit(solution)/shard_map/all_to_all | solution.py:393
  50.0 11.4 %all_to_all.17.refs_0_ = bf16[32,32,128]{2,1,0:T(8,128)(2,1)S(1)} all-to-all(bf16[32,32,128]{2,1,0:T(8,128)(2,1)S(1)} %get-tuple-element.38), channel_id=1, replica_groups=mesh['row'=32,'col'=8] {'row'}, dimensions={0} | all-to-all | bytes 524288 | tf_op jit(solution)/shard_map/all_to_all | solution.py:401
  61.5 0.9 %shard_map.105 = (f32[16,64]{1,0:T(8,128)}, f32[64,256]{1,0:T(8,128)}, f32[576,64]{1,0:T(8,128)}, f32[1,64]{1,0:T(1,128)}, f32[576,64]{1,0:T(8,128)}) custom-call(bf16[32,32,128]{2,1,0:T(8,128)(2,1)S(1)} %all_to_all.17.refs_0_, f32[16,128]{1,0:T(8,128)S(1)} %get-tuple-element.39.refs_1_), custom_call_target="tpu_custom_call" | custom-call | tf_op jit(solution)/shard_map/pallas_call | solution.py:402
  (2 shorter events, 0.1 us)
Async XLA Ops:
  0.6 11.5 %collective-permute-start.3 = (bf16[64,256]{1,0:T(8,128)(2,1)}, bf16[64,256]{1,0:T(8,128)(2,1)S(1)}, u32[]{:S(2)}, u32[]{:S(2)}) collective-permute-start(bf16[64,256]{1,0:T(8,128)(2,1)} %bitcast.6), channel_id=1, source_target_pairs={{0,1},{1,0},{2,3},{3,2},{4,5},{5,4},{6,7},{7,6},{8,17},{9,16},{10,... | collective-permute-start | bytes 98312 | tf_op jit(solution)/shard_map/ppermute | solution.py:354
  4.0 8.2 %collective-permute-start.2 = (bf16[64,256]{1,0:T(8,128)(2,1)}, bf16[64,256]{1,0:T(8,128)(2,1)S(1)}, u32[]{:S(2)}, u32[]{:S(2)}) collective-permute-start(bf16[64,256]{1,0:T(8,128)(2,1)} %bitcast.7), channel_id=1, source_target_pairs={{0,8},{1,10},{2,9},{3,12},{4,11},{5,14},{6,13},{7,15},{8,0},{9,2},... | collective-permute-start | bytes 98312 | tf_op jit(solution)/shard_map/ppermute | solution.py:354
  7.1 5.0 %collective-permute-start = (bf16[16,64]{1,0:T(8,128)(2,1)}, bf16[16,64]{1,0:T(8,128)(2,1)S(1)}, u32[]{:S(2)}, u32[]{:S(2)}) collective-permute-start(bf16[16,64]{1,0:T(8,128)(2,1)} %refs_3_.1), channel_id=1, source_target_pairs={{0,8},{1,10},{2,9},{3,12},{4,11},{5,14},{6,13},{7,15},{8,0},{9,2},... | collective-permute-start | bytes 6152 | tf_op jit(solution)/shard_map/ppermute | solution.py:354
  7.5 4.7 %collective-permute-start.1 = (bf16[16,64]{1,0:T(8,128)(2,1)}, bf16[16,64]{1,0:T(8,128)(2,1)S(1)}, u32[]{:S(2)}, u32[]{:S(2)}) collective-permute-start(bf16[16,64]{1,0:T(8,128)(2,1)} %refs_3_.1), channel_id=1, source_target_pairs={{0,1},{1,0},{2,3},{3,2},{4,5},{5,4},{6,7},{7,6},{8,17},{9,16},{10,... | collective-permute-start | bytes 6152 | tf_op jit(solution)/shard_map/ppermute | solution.py:354

commit v12 on v10

--- a/solution.py
+++ b/solution.py
@@ -188,9 +188,9 @@
     on_map = jnp.where(side_lane % 16 < 8, left, right)
     col_part = jnp.concatenate(col_part, axis=0)
     main_sum = jnp.zeros((4 * CH, cols), F32)
-    full = jnp.zeros((6 * CH, 4 * CH), F32)
+    two = jnp.zeros((3 * CH, 3 * CH), F32)
     row_of = jnp.zeros((24, 4 * CH), F32)
-    x_all = x_ref[...].reshape(6 * CH, x_ref.shape[2])
+    x_half = [jnp.concatenate([x_ref[b, CH * gb : CH * (gb + 1), :] for b in range(3)], axis=0) for gb in range(2)]
     for k in range(9):
         span = slice(k * cols, (k + 1) * cols) if k < 8 else slice(8 * cols, 8 * cols + LANES)
         if k < 8:
@@ -206,7 +206,9 @@
         held = jnp.concatenate([sig[:CH] * top, sig[CH : 3 * CH], sig[3 * CH :] * bottom], axis=0)
         if k == 8:
             held = held * on_map
-        full = full + dot(x_all[:, span], (pre * held).astype(BF16), NT)
+        act = (pre * held).astype(BF16)
+        joined = jnp.concatenate([x_half[0][:, span], x_half[1][:, span]], axis=1)
+        two = two + dot(joined, jnp.concatenate([act[: 3 * CH], act[CH:]], axis=1), NT)
         inner = (back_ref[:, span] * (held * (1.0 + pre * (1.0 - sig)))).astype(BF16)
         row_of = row_of + dot(ind_ref[:, span], inner, NT)
         if k < 8:
@@ -256,10 +258,8 @@
     for a in range(3):
         for b in range(3):
             one = one_row[a][CH * b : CH * (b + 1)] + one_col[b][CH * a : CH * (a + 1)]
-            two = [
-                full[CH * (2 * b + gb) : CH * (2 * b + gb + 1), CH * (a + gb) : CH * (a + gb + 1)] for gb in range(2)
-            ]
-            w_scr[CH * (3 * a + b) : CH * (3 * a + b + 1), :] = jnp.concatenate([one, two[0] + two[1]], axis=1)
+            pair = jnp.concatenate([one, two[CH * b : CH * (b + 1), CH * a : CH * (a + 1)]], axis=1)
+            w_scr[CH * (3 * a + b) : CH * (3 * a + b + 1), :] = pair
 
     weights, chans, sums_end = chunk_rows(n_row)
     tail = total[:, :LANES] + total[:, cols + LANES :] + bias_row[:1, :]
@@ -404,7 +404,7 @@
         compiler_params=PARAMS,
     )(got, own)
     got = lax.all_to_all(copies, "col", 0, 0)
-    end = -(-(weights + 2 * chans) // 16) * 16
+    end = -(-(weights + 2 * chans) // 8) * 8
     kept, copies = pl.pallas_call(
         lambda *refs: col_sum_kernel(n_row, n_col, cols, *refs),
         out_shape=(sds((16, LANES)), sds((n_row, end, LANES), BF16)),

time: 58.1 us -> 57.6 us (level)
  no operation moved by 1% of the time
where the time goes in v12:
time: 57.6 us; the launch traced here: 57.4 us
  blocking collectives  43 us (75%)
  Pallas kernels  7.22 us (13%)
  starting transfers between devices  6.5 us (11%)
  between operations  0.67 us (1%)
    all_to_all x1, blocking collectives, shards(): got = lax.all_to_all(chunks, 'row', 0, 0)  16.4 us
    all_to_all x1, blocking collectives, shards(): got = lax.all_to_all(copies, 'col', 0, 0)  15.5 us
    all_to_all x1, blocking collectives, shards(): got = lax.all_to_all(copies, 'row', 0, 0)  11.1 us
    ppermute x2, starting transfers between devices, swap(): return lax.ppermute(strip, ('row', 'col'), pairs)  6.5 us
    pallas_call x1, Pallas kernels, shards(): pl.pallas_call(lambda *refs: main_kernel(n_row, n_col, *refs), out_shape=...  2.82 us
    pallas_call x1, Pallas kernels, shards(): pl.pallas_call(lambda *refs: own_kernel(n_col, *refs), out_shape=(sds((3,...  2.63 us
  transfers between devices with their start and end apart: 2, of which 0 were waited for; matrix products, arithmetic and copies ran while one was open for 0% of the time, Pallas kernels for 5%

profile of v12, /device:TPU:1, one launch (start us, length us, event | category | flops | bytes accessed | tf_op | source)
XLA Modules:
  0.0 57.4 jit_solution(5866323144588121596)
XLA Ops:
  0.6 0.8 %shard_map.101 = (bf16[80,128]{1,0:T(8,128)(2,1)S(1)}, bf16[16,64]{1,0:T(8,128)(2,1)S(1)}, bf16[64,256]{1,0:T(8,128)(2,1)S(1)}) custom-call(bf16[16,64]{1,0:T(8,128)(2,1)} %row_hbm.1, bf16[64,256]{1,0:T(8,128)(2,1)} %bitcast.6), custom_call_target="tpu_custom_call" | custom-call | tf_op jit(solution)/shard_map/pallas_call | solution.py:348
  1.4 3.3 %collective-permute-start.1 = (bf16[80,128]{1,0:T(8,128)(2,1)S(1)}, bf16[80,128]{1,0:T(8,128)(2,1)S(1)}, u32[]{:S(2)}, u32[]{:S(2)}) collective-permute-start(bf16[80,128]{1,0:T(8,128)(2,1)S(1)} %get-tuple-element.26), channel_id=1, source_target_pairs={{0,1},{1,0},{2,3},{3,2},{4,5},{5,4},{6,7},{7,6},{8,17},{9,16},{10,... | collective-permute-start | bytes 61448 | tf_op jit(solution)/shard_map/ppermute | solution.py:368
  4.8 3.2 %collective-permute-start = (bf16[80,128]{1,0:T(8,128)(2,1)S(1)}, bf16[80,128]{1,0:T(8,128)(2,1)S(1)}, u32[]{:S(2)}, u32[]{:S(2)}) collective-permute-start(bf16[80,128]{1,0:T(8,128)(2,1)S(1)} %get-tuple-element.26), channel_id=1, source_target_pairs={{0,8},{1,10},{2,9},{3,12},{4,11},{5,14},{6,13},{7,15},{8,0},{9,2},... | collective-permute-start | bytes 61448 | tf_op jit(solution)/shard_map/ppermute | solution.py:368
  7.9 2.6 %shard_map.102 = (bf16[3,128,2176]{2,1,0:T(8,128)(2,1)S(1)}, f32[256,2176]{1,0:T(8,128)S(1)}, f32[8,128]{1,0:T(8,128)S(1)}, f32[64,256]{1,0:T(8,128)S(1)}, bf16[...) custom-call(bf16[3,3,64,64]{3,2,1,0:T(8,128)(2,1)} %refs_0_.1, ...), custom_call_target="tpu_custom_call" | custom-call | tf_op jit(solution)/shard_map/pallas_call | solution.py:374
  10.6 0.0 collective-permute-done.1.refs_1_
  10.6 0.0 collective-permute-done.refs_0_
  10.6 2.8 %shard_map.103 = (bf16[32,32,128]{2,1,0:T(8,128)(2,1)S(1)}, f32[8,128]{1,0:T(8,128)S(1)}) custom-call(bf16[80,128]{1,0:T(8,128)(2,1)S(1)} %collective-permute-done.refs_0_, bf16[80,128]{1,0:T(8,128)(2,1)S(1)} %collective-permute-done.1.refs_1_, bf16[16,64]{1,0:T(8,128)(2,1)S(1)} %get-tuple-element.27.refs_2_, bf16[64,256]{1,0:T(8,128)(2,1)S(1)} %get-tuple-element.28.refs_3_, ...), custom_call_target="tpu_custom_call" | custom-call | tf_op jit(solution)/shard_map/pallas_call | solution.py:391
  13.4 16.4 %all_to_all.15.refs_0_ = bf16[32,32,128]{2,1,0:T(8,128)(2,1)S(1)} all-to-all(bf16[32,32,128]{2,1,0:T(8,128)(2,1)S(1)} %get-tuple-element.38), channel_id=1, replica_groups=mesh['row'=32,'col'=8] {'row'}, dimensions={0} | all-to-all | bytes 524288 | tf_op jit(solution)/shard_map/all_to_all | solution.py:400
  29.9 15.5 %all_to_all.16.refs_0_ = bf16[8,32,128]{2,1,0:T(8,128)(2,1)S(1)} all-to-all(bf16[8,32,128]{2,1,0:T(8,128)(2,1)S(1)} %shard_map.104), channel_id=1, replica_groups=mesh['row'=32,'col'=8] {'col'}, dimensions={0} | all-to-all | bytes 131072 | tf_op jit(solution)/shard_map/all_to_all | solution.py:406
  45.4 11.1 %all_to_all.17.refs_0_ = bf16[32,24,128]{2,1,0:T(8,128)(2,1)S(1)} all-to-all(bf16[32,24,128]{2,1,0:T(8,128)(2,1)S(1)} %get-tuple-element.40), channel_id=1, replica_groups=mesh['row'=32,'col'=8] {'row'}, dimensions={0} | all-to-all | bytes 393216 | tf_op jit(solution)/shard_map/all_to_all | solution.py:414
  56.5 0.9 %shard_map.106 = (f32[16,64]{1,0:T(8,128)}, f32[64,256]{1,0:T(8,128)}, f32[576,64]{1,0:T(8,128)}, f32[1,64]{1,0:T(1,128)}, f32[576,64]{1,0:T(8,128)}) custom-call(bf16[32,24,128]{2,1,0:T(8,128)(2,1)S(1)} %all_to_all.17.refs_0_, f32[16,128]{1,0:T(8,128)S(1)} %get-tuple-element.41.refs_1_), custom_call_target="tpu_custom_call" | custom-call | tf_op jit(solution)/shard_map/pallas_call | solution.py:415
  (2 shorter events, 0.1 us)
Async XLA Ops:
  1.4 9.1 %collective-permute-start.1 = (bf16[80,128]{1,0:T(8,128)(2,1)S(1)}, bf16[80,128]{1,0:T(8,128)(2,1)S(1)}, u32[]{:S(2)}, u32[]{:S(2)}) collective-permute-start(bf16[80,128]{1,0:T(8,128)(2,1)S(1)} %get-tuple-element.26), channel_id=1, source_target_pairs={{0,1},{1,0},{2,3},{3,2},{4,5},{5,4},{6,7},{7,6},{8,17},{9,16},{10,... | collective-permute-start | bytes 61448 | tf_op jit(solution)/shard_map/ppermute | solution.py:368
  4.8 5.8 %collective-permute-start = (bf16[80,128]{1,0:T(8,128)(2,1)S(1)}, bf16[80,128]{1,0:T(8,128)(2,1)S(1)}, u32[]{:S(2)}, u32[]{:S(2)}) collective-permute-start(bf16[80,128]{1,0:T(8,128)(2,1)S(1)} %get-tuple-element.26), channel_id=1, source_target_pairs={{0,8},{1,10},{2,9},{3,12},{4,11},{5,14},{6,13},{7,15},{8,0},{9,2},... | collective-permute-start | bytes 61448 | tf_op jit(solution)/shard_map/ppermute | solution.py:368

commit v13 on v12

--- a/solution.py
+++ b/solution.py
@@ -74,6 +74,7 @@
         on_map = jnp.logical_not(off_map[tap])
         main = [jnp.where(on_map & (row == k), 1.0, 0.0) for k in range(8)]
         taps.append(jnp.concatenate(main + [edge], axis=1))
+    taps.append(jnp.zeros(taps[0].shape, F32))
     return jnp.concatenate(taps, axis=0).astype(BF16)
 
 
@@ -110,7 +111,7 @@
     edge_lane = lax.broadcasted_iota(jnp.int32, (CH, LANES), 1)
     for piece in range(cols // LANES):
         wide = grad_ref[:, :, LANES * piece : LANES * (piece + 1)]
-        rows_scr[piece] = wide.astype(F32).reshape(CH * 16, LANES)
+        rows_scr[piece, : CH * 16, :] = wide.astype(F32).reshape(CH * 16, LANES)
     col_sum = jnp.zeros((CH, cols), F32)
     for half in range(2):
         rows = slice(half * CH, (half + 1) * CH)
@@ -189,7 +190,7 @@
     col_part = jnp.concatenate(col_part, axis=0)
     main_sum = jnp.zeros((4 * CH, cols), F32)
     two = jnp.zeros((3 * CH, 3 * CH), F32)
-    row_of = jnp.zeros((24, 4 * CH), F32)
+    row_of = jnp.zeros((32, 4 * CH), F32)
     x_half = [jnp.concatenate([x_ref[b, CH * gb : CH * (gb + 1), :] for b in range(3)], axis=0) for gb in range(2)]
     for k in range(9):
         span = slice(k * cols, (k + 1) * cols) if k < 8 else slice(8 * cols, 8 * cols + LANES)
@@ -375,11 +376,11 @@
         lambda *refs: own_kernel(n_col, *refs),
         out_shape=(
             sds((3, 2 * CH, places), BF16), sds((4 * CH, places)), sds((8, 2 * CH)), sds((CH, cols)),
-            sds((24, places), BF16), square, square, square, sds((CH, 8)),
+            sds((32, places), BF16), square, square, square, sds((CH, 8)),
         ),
         in_specs=[pl.BlockSpec(memory_space=pltpu.HBM)] * 4,
         scratch_shapes=[
-            pltpu.VMEM((cols // LANES, CH * 16, LANES), F32),
+            pltpu.VMEM((cols // LANES, CH * 16 + 16, LANES), F32),
             pltpu.VMEM(conv_one.shape, BF16),
             pltpu.VMEM(conv_two.shape, BF16),
             pltpu.VMEM((1, CH), F32),
@@ -404,7 +405,7 @@
         compiler_params=PARAMS,
     )(got, own)
     got = lax.all_to_all(copies, "col", 0, 0)
-    end = -(-(weights + 2 * chans) // 8) * 8
+    end = -(-(weights + 2 * chans) // 16) * 16
     kept, copies = pl.pallas_call(
         lambda *refs: col_sum_kernel(n_row, n_col, cols, *refs),
         out_shape=(sds((16, LANES)), sds((n_row, end, LANES), BF16)),

time: 57.6 us -> 58 us (level)
  no operation moved by 1% of the time
where the time goes in v13:
time: 58 us; the launch traced here: 57.7 us
  blocking collectives  43.3 us (75%)
  Pallas kernels  7.24 us (12%)
  starting transfers between devices  6.5 us (11%)
  between operations  0.67 us (1%)
    all_to_all x1, blocking collectives, shards(): got = lax.all_to_all(chunks, 'row', 0, 0)  16.4 us
    all_to_all x1, blocking collectives, shards(): got = lax.all_to_all(copies, 'col', 0, 0)  15.5 us
    all_to_all x1, blocking collectives, shards(): got = lax.all_to_all(copies, 'row', 0, 0)  11.4 us
    ppermute x2, starting transfers between devices, swap(): return lax.ppermute(strip, ('row', 'col'), pairs)  6.5 us
    pallas_call x1, Pallas kernels, shards(): pl.pallas_call(lambda *refs: main_kernel(n_row, n_col, *refs), out_shape=...  2.84 us
    pallas_call x1, Pallas kernels, shards(): pl.pallas_call(lambda *refs: own_kernel(n_col, *refs), out_shape=(sds((3,...  2.64 us
  transfers between devices with their start and end apart: 2, of which 0 were waited for; matrix products, arithmetic and copies ran while one was open for 0% of the time, Pallas kernels for 5%

profile of v13, /device:TPU:1, one launch (start us, length us, event | category | flops | bytes accessed | tf_op | source)
XLA Modules:
  0.0 57.7 jit_solution(17358333432357858246)
XLA Ops:
  0.6 0.8 %shard_map.101 = (bf16[80,128]{1,0:T(8,128)(2,1)S(1)}, bf16[16,64]{1,0:T(8,128)(2,1)S(1)}, bf16[64,256]{1,0:T(8,128)(2,1)S(1)}) custom-call(bf16[16,64]{1,0:T(8,128)(2,1)} %row_hbm.1, bf16[64,256]{1,0:T(8,128)(2,1)} %bitcast.6), custom_call_target="tpu_custom_call" | custom-call | tf_op jit(solution)/shard_map/pallas_call | solution.py:349
  1.4 3.3 %collective-permute-start.1 = (bf16[80,128]{1,0:T(8,128)(2,1)S(1)}, bf16[80,128]{1,0:T(8,128)(2,1)S(1)}, u32[]{:S(2)}, u32[]{:S(2)}) collective-permute-start(bf16[80,128]{1,0:T(8,128)(2,1)S(1)} %get-tuple-element.26), channel_id=1, source_target_pairs={{0,1},{1,0},{2,3},{3,2},{4,5},{5,4},{6,7},{7,6},{8,17},{9,16},{10,... | collective-permute-start | bytes 61448 | tf_op jit(solution)/shard_map/ppermute | solution.py:369
  4.8 3.2 %collective-permute-start = (bf16[80,128]{1,0:T(8,128)(2,1)S(1)}, bf16[80,128]{1,0:T(8,128)(2,1)S(1)}, u32[]{:S(2)}, u32[]{:S(2)}) collective-permute-start(bf16[80,128]{1,0:T(8,128)(2,1)S(1)} %get-tuple-element.26), channel_id=1, source_target_pairs={{0,8},{1,10},{2,9},{3,12},{4,11},{5,14},{6,13},{7,15},{8,0},{9,2},... | collective-permute-start | bytes 61448 | tf_op jit(solution)/shard_map/ppermute | solution.py:369
  7.9 2.6 %shard_map.102 = (bf16[3,128,2176]{2,1,0:T(8,128)(2,1)S(1)}, f32[256,2176]{1,0:T(8,128)S(1)}, f32[8,128]{1,0:T(8,128)S(1)}, f32[64,256]{1,0:T(8,128)S(1)}, bf16[...) custom-call(bf16[3,3,64,64]{3,2,1,0:T(8,128)(2,1)} %refs_0_.1, ...), custom_call_target="tpu_custom_call" | custom-call | tf_op jit(solution)/shard_map/pallas_call | solution.py:375
  10.6 0.0 collective-permute-done.1.refs_1_
  10.6 0.0 collective-permute-done.refs_0_
  10.6 2.8 %shard_map.103 = (bf16[32,32,128]{2,1,0:T(8,128)(2,1)S(1)}, f32[8,128]{1,0:T(8,128)S(1)}) custom-call(bf16[80,128]{1,0:T(8,128)(2,1)S(1)} %collective-permute-done.refs_0_, bf16[80,128]{1,0:T(8,128)(2,1)S(1)} %collective-permute-done.1.refs_1_, bf16[16,64]{1,0:T(8,128)(2,1)S(1)} %get-tuple-element.27.refs_2_, bf16[64,256]{1,0:T(8,128)(2,1)S(1)} %get-tuple-element.28.refs_3_, ...), custom_call_target="tpu_custom_call" | custom-call | tf_op jit(solution)/shard_map/pallas_call | solution.py:392
  13.4 16.4 %all_to_all.15.refs_0_ = bf16[32,32,128]{2,1,0:T(8,128)(2,1)S(1)} all-to-all(bf16[32,32,128]{2,1,0:T(8,128)(2,1)S(1)} %get-tuple-element.38), channel_id=1, replica_groups=mesh['row'=32,'col'=8] {'row'}, dimensions={0} | all-to-all | bytes 524288 | tf_op jit(solution)/shard_map/all_to_all | solution.py:401
  29.9 15.5 %all_to_all.16.refs_0_ = bf16[8,32,128]{2,1,0:T(8,128)(2,1)S(1)} all-to-all(bf16[8,32,128]{2,1,0:T(8,128)(2,1)S(1)} %shard_map.104), channel_id=1, replica_groups=mesh['row'=32,'col'=8] {'col'}, dimensions={0} | all-to-all | bytes 131072 | tf_op jit(solution)/shard_map/all_to_all | solution.py:407
  45.4 11.4 %all_to_all.17.refs_0_ = bf16[32,32,128]{2,1,0:T(8,128)(2,1)S(1)} all-to-all(bf16[32,32,128]{2,1,0:T(8,128)(2,1)S(1)} %get-tuple-element.40), channel_id=1, replica_groups=mesh['row'=32,'col'=8] {'row'}, dimensions={0} | all-to-all | bytes 524288 | tf_op jit(solution)/shard_map/all_to_all | solution.py:415
  56.8 0.9 %shard_map.106 = (f32[16,64]{1,0:T(8,128)}, f32[64,256]{1,0:T(8,128)}, f32[576,64]{1,0:T(8,128)}, f32[1,64]{1,0:T(1,128)}, f32[576,64]{1,0:T(8,128)}) custom-call(bf16[32,32,128]{2,1,0:T(8,128)(2,1)S(1)} %all_to_all.17.refs_0_, f32[16,128]{1,0:T(8,128)S(1)} %get-tuple-element.41.refs_1_), custom_call_target="tpu_custom_call" | custom-call | tf_op jit(solution)/shard_map/pallas_call | solution.py:416
  (2 shorter events, 0.1 us)
Async XLA Ops:
  1.4 9.1 %collective-permute-start.1 = (bf16[80,128]{1,0:T(8,128)(2,1)S(1)}, bf16[80,128]{1,0:T(8,128)(2,1)S(1)}, u32[]{:S(2)}, u32[]{:S(2)}) collective-permute-start(bf16[80,128]{1,0:T(8,128)(2,1)S(1)} %get-tuple-element.26), channel_id=1, source_target_pairs={{0,1},{1,0},{2,3},{3,2},{4,5},{5,4},{6,7},{7,6},{8,17},{9,16},{10,... | collective-permute-start | bytes 61448 | tf_op jit(solution)/shard_map/ppermute | solution.py:369
  4.8 5.8 %collective-permute-start = (bf16[80,128]{1,0:T(8,128)(2,1)S(1)}, bf16[80,128]{1,0:T(8,128)(2,1)S(1)}, u32[]{:S(2)}, u32[]{:S(2)}) collective-permute-start(bf16[80,128]{1,0:T(8,128)(2,1)S(1)} %get-tuple-element.26), channel_id=1, source_target_pairs={{0,8},{1,10},{2,9},{3,12},{4,11},{5,14},{6,13},{7,15},{8,0},{9,2},... | collective-permute-start | bytes 61448 | tf_op jit(solution)/shard_map/ppermute | solution.py:369

commit v14 on v13

--- a/solution.py
+++ b/solution.py
@@ -276,7 +276,7 @@
     out_ref[...] = chunk_scr[...].astype(BF16)
 
 
-def row_sum_kernel(n_row, n_col, got_ref, own_ref, out_ref):
+def row_sum_kernel(n_row, got_ref, own_ref, out_ref):
     sums_end = chunk_rows(n_row)[2]
     me = lax.axis_index("row")
     total = got_ref[0].astype(F32)
@@ -286,23 +286,34 @@
     before = got_ref[jnp.maximum(me - 1, 0)].astype(F32)[sums_end:]
     after = got_ref[jnp.minimum(me + 1, n_row - 1)].astype(F32)[sums_end:]
     rows = own_ref[...] + off_edge("row", 0) * before + off_edge("row", n_row - 1) * after
-    whole = jnp.concatenate([total, rows], axis=0).astype(BF16)
-    for k in range(n_col):
-        out_ref[k] = whole
-
-
-def col_sum_kernel(n_row, n_col, cols, got_ref, kept_ref, out_ref, scr):
+    out_ref[...] = jnp.concatenate([total, rows], axis=0)
+
+
+def pair_kernel(n_row, mine_ref, twin_ref, out_ref):
     weights, chans, sums_end = chunk_rows(n_row)
-    me = lax.axis_index("col")
+    edge = slice(weights + 2 * chans, sums_end)
+    out_ref[...] = mine_ref[...] + twin_ref[...]
+    lane = lax.broadcasted_iota(jnp.int32, (chans, LANES), 1)
+    summed = (lane >= 32) & (lane < 32 + CH)
+    out_ref[edge, :] = mine_ref[edge, :] + jnp.where(summed, twin_ref[edge, :], 0.0)
+
+
+def four_kernel(left_ref, right_ref, out_ref):
+    out_ref[...] = left_ref[...] + right_ref[...]
+
+
+def col_sum_kernel(
+    n_row, n_col, cols, mine_ref, twin_ref, other_ref, four_ref, last_ref, kept_ref, out_ref, scr
+):
+    weights, chans, sums_end = chunk_rows(n_row)
+    odd = lax.axis_index("col") % 2 == 1
     whole = math.sqrt(16 * n_row * cols * n_col)
-    total = got_ref[0].astype(F32)
-    for k in range(1, n_col):
-        total = total + got_ref[k].astype(F32)
+    total = four_ref[...] + last_ref[...]
     kept_ref[:8, :] = total[sums_end:, :] * (1.0 / math.sqrt(cols * n_col))
     kept_ref[8:, :] = total[sums_end - 8 : sums_end, :] * (1.0 / whole)
-    before = got_ref[jnp.maximum(me - 1, 0)].astype(F32) * off_edge("col", 0)
-    after = got_ref[jnp.minimum(me + 1, n_col - 1)].astype(F32) * off_edge("col", n_col - 1)
-    mine = got_ref[me].astype(F32)
+    mine, twin, other = mine_ref[...], twin_ref[...], other_ref[...]
+    before = jnp.where(odd, twin, other) * off_edge("col", 0)
+    after = jnp.where(odd, other, twin) * off_edge("col", n_col - 1)
     edge = slice(weights + 2 * chans, sums_end)
     lane = lax.broadcasted_iota(jnp.int32, (chans, LANES), 1)
     low = mine[weights : weights + chans] + jnp.where(lane < 16, before[edge], 0.0)
@@ -399,19 +410,27 @@
         compiler_params=PARAMS,
     )(row_twin, col_twin, *feats, *held)
     got = lax.all_to_all(chunks, "row", 0, 0)
-    copies = pl.pallas_call(
-        lambda *refs: row_sum_kernel(n_row, n_col, *refs),
-        out_shape=sds((n_col, sums_end + 8, LANES), BF16),
-        compiler_params=PARAMS,
+    part = sds((sums_end + 8, LANES))
+    mine = pl.pallas_call(
+        lambda *refs: row_sum_kernel(n_row, *refs), out_shape=part, compiler_params=PARAMS
     )(got, own)
-    got = lax.all_to_all(copies, "col", 0, 0)
+    beside = [(c, c ^ 1) for c in range(n_col)]
+    outside = [(c, (c + (1 if c % 2 else -1)) % n_col) for c in range(n_col)]
+    across = [(c, (c + (-3 if c % 2 else 3)) % n_col) for c in range(n_col)]
+    paired = lax.ppermute(mine, "col", beside)
+    two_sum = pl.pallas_call(
+        lambda *refs: pair_kernel(n_row, *refs), out_shape=part, compiler_params=PARAMS
+    )(mine, paired)
+    side = lax.ppermute(two_sum, "col", outside)
+    four = pl.pallas_call(four_kernel, out_shape=part, compiler_params=PARAMS)(two_sum, side)
+    last = lax.ppermute(four, "col", across)
     end = -(-(weights + 2 * chans) // 16) * 16
     kept, copies = pl.pallas_call(
         lambda *refs: col_sum_kernel(n_row, n_col, cols, *refs),
         out_shape=(sds((16, LANES)), sds((n_row, end, LANES), BF16)),
         scratch_shapes=[pltpu.VMEM((end, LANES), F32)],
         compiler_params=PARAMS,
-    )(got)
+    )(mine, paired, side, four, last)
     got = lax.all_to_all(copies, "row", 0, 0)
     row_grad, col_grad, one, bias_grad, two = pl.pallas_call(
         lambda *refs: spread_kernel(n_row, *refs),

time: 58 us -> 54.8 us (0.945)
  blocking collectives: 43.3 us -> 27.7 us
  starting transfers between devices: 6.5 us -> 15.2 us
  waiting for transfers between devices: 0.01 us -> 3.69 us
    all_to_all x1 -> x0, blocking collectives: 15.5 us -> none  [shards(): got = lax.all_to_all(copies, 'col', 0, 0)]
    ppermute x0 -> x3, starting transfers between devices: none -> 8.7 us  [the longest x1 5.19 us: shards(): last = lax.ppermute(four, 'col', across)]
    ppermute x0 -> x3, waiting for transfers between devices: none -> 3.68 us  [the longest x1 1.42 us: shards(): last = lax.ppermute(four, 'col', across)]
  transfers between devices with their start and end apart: 2 -> 5, of which waited for: 0 -> 3; matrix products, arithmetic and copies ran while one was open for 0% -> 0% of each run, Pallas kernels for 5% -> 5%
where the time goes in v14:
time: 54.8 us; the launch traced here: 54.5 us
  blocking collectives  27.7 us (51%)
  starting transfers between devices  15.2 us (28%)
  Pallas kernels  7.24 us (13%)
  waiting for transfers between devices  3.69 us (7%)
  between operations  0.68 us (1%)
    all_to_all x1, blocking collectives, shards(): got = lax.all_to_all(chunks, 'row', 0, 0)  16.4 us
    all_to_all x1, blocking collectives, shards(): got = lax.all_to_all(copies, 'row', 0, 0)  11.3 us
    ppermute x2, starting transfers between devices, swap(): return lax.ppermute(strip, ('row', 'col'), pairs)  6.5 us
    ppermute x1, starting transfers between devices, shards(): last = lax.ppermute(four, 'col', across)  5.19 us
    ppermute x1, starting transfers between devices, shards(): side = lax.ppermute(two_sum, 'col', outside)  3.01 us
    pallas_call x1, Pallas kernels, shards(): pl.pallas_call(lambda *refs: main_kernel(n_row, n_col, *refs), out_shape=...  2.84 us
    pallas_call x1, Pallas kernels, shards(): pl.pallas_call(lambda *refs: own_kernel(n_col, *refs), out_shape=(sds((3,...  2.64 us
    ppermute x1, waiting for transfers between devices, shards(): last = lax.ppermute(four, 'col', across)  1.42 us
  transfers between devices with their start and end apart: 5, of which 3 were waited for; matrix products, arithmetic and copies ran while one was open for 0% of the time, Pallas kernels for 5%

profile of v14, /device:TPU:1, one launch (start us, length us, event | category | flops | bytes accessed | tf_op | source)
XLA Modules:
  0.0 54.5 jit_solution(10662349661839755469)
XLA Ops:
  0.6 0.8 %shard_map.101 = (bf16[80,128]{1,0:T(8,128)(2,1)S(1)}, bf16[16,64]{1,0:T(8,128)(2,1)S(1)}, bf16[64,256]{1,0:T(8,128)(2,1)S(1)}) custom-call(bf16[16,64]{1,0:T(8,128)(2,1)} %row_hbm.1, bf16[64,256]{1,0:T(8,128)(2,1)} %bitcast.6), custom_call_target="tpu_custom_call" | custom-call | tf_op jit(solution)/shard_map/pallas_call | solution.py:360
  1.4 3.3 %collective-permute-start.1 = (bf16[80,128]{1,0:T(8,128)(2,1)S(1)}, bf16[80,128]{1,0:T(8,128)(2,1)S(1)}, u32[]{:S(2)}, u32[]{:S(2)}) collective-permute-start(bf16[80,128]{1,0:T(8,128)(2,1)S(1)} %get-tuple-element.26), channel_id=1, source_target_pairs={{0,1},{1,0},{2,3},{3,2},{4,5},{5,4},{6,7},{7,6},{8,17},{9,16},{10,... | collective-permute-start | bytes 61448 | tf_op jit(solution)/shard_map/ppermute | solution.py:380
  4.8 3.2 %collective-permute-start = (bf16[80,128]{1,0:T(8,128)(2,1)S(1)}, bf16[80,128]{1,0:T(8,128)(2,1)S(1)}, u32[]{:S(2)}, u32[]{:S(2)}) collective-permute-start(bf16[80,128]{1,0:T(8,128)(2,1)S(1)} %get-tuple-element.26), channel_id=1, source_target_pairs={{0,8},{1,10},{2,9},{3,12},{4,11},{5,14},{6,13},{7,15},{8,0},{9,2},... | collective-permute-start | bytes 61448 | tf_op jit(solution)/shard_map/ppermute | solution.py:380
  7.9 2.6 %shard_map.102 = (bf16[3,128,2176]{2,1,0:T(8,128)(2,1)S(1)}, f32[256,2176]{1,0:T(8,128)S(1)}, f32[8,128]{1,0:T(8,128)S(1)}, f32[64,256]{1,0:T(8,128)S(1)}, bf16[...) custom-call(bf16[3,3,64,64]{3,2,1,0:T(8,128)(2,1)} %refs_0_.1, ...), custom_call_target="tpu_custom_call" | custom-call | tf_op jit(solution)/shard_map/pallas_call | solution.py:386
  10.6 0.0 collective-permute-done.1.refs_1_
  10.6 0.0 collective-permute-done.refs_0_
  10.6 2.8 %shard_map.103 = (bf16[32,32,128]{2,1,0:T(8,128)(2,1)S(1)}, f32[8,128]{1,0:T(8,128)S(1)}) custom-call(bf16[80,128]{1,0:T(8,128)(2,1)S(1)} %collective-permute-done.refs_0_, bf16[80,128]{1,0:T(8,128)(2,1)S(1)} %collective-permute-done.1.refs_1_, bf16[16,64]{1,0:T(8,128)(2,1)S(1)} %get-tuple-element.27.refs_2_, bf16[64,256]{1,0:T(8,128)(2,1)S(1)} %get-tuple-element.28.refs_3_, ...), custom_call_target="tpu_custom_call" | custom-call | tf_op jit(solution)/shard_map/pallas_call | solution.py:403
  13.4 16.4 %all_to_all.10.refs_0_ = bf16[32,32,128]{2,1,0:T(8,128)(2,1)S(1)} all-to-all(bf16[32,32,128]{2,1,0:T(8,128)(2,1)S(1)} %get-tuple-element.38), channel_id=1, replica_groups=mesh['row'=32,'col'=8] {'row'}, dimensions={0} | all-to-all | bytes 524288 | tf_op jit(solution)/shard_map/all_to_all | solution.py:412
  29.9 0.5 collective-permute-start.2
  30.4 0.8 %collective-permute-done.2.refs_1_ = f32[32,128]{1,0:T(8,128)S(1)} collective-permute-done((f32[32,128]{1,0:T(8,128)S(1)}, f32[32,128]{1,0:T(8,128)S(1)}, u32[]{:S(2)}, u32[]{:S(2)}) %collective-permute-start.2) | collective-permute-done | bytes 16416 | tf_op jit(solution)/shard_map/ppermute | solution.py:420
  31.3 3.0 %collective-permute-start.3 = (f32[32,128]{1,0:T(8,128)S(1)}, f32[32,128]{1,0:T(8,128)S(1)}, u32[]{:S(2)}, u32[]{:S(2)}) collective-permute-start(f32[32,128]{1,0:T(8,128)S(1)} %shard_map.105.left_ref), channel_id=1, source_target_pairs={{0,7},{1,2},{2,1},{3,4},{4,3},{5,6},{6,5},{7,0},{8,15},{9,10},{10,... | collective-permute-start | bytes 49160 | tf_op jit(solution)/shard_map/ppermute | solution.py:424
  34.3 1.4 %collective-permute-done.3.right_ref.refs_2_ = f32[32,128]{1,0:T(8,128)S(1)} collective-permute-done((f32[32,128]{1,0:T(8,128)S(1)}, f32[32,128]{1,0:T(8,128)S(1)}, u32[]{:S(2)}, u32[]{:S(2)}) %collective-permute-start.3) | collective-permute-done | bytes 16416 | tf_op jit(solution)/shard_map/ppermute | solution.py:424
  35.7 5.2 %collective-permute-start.4 = (f32[32,128]{1,0:T(8,128)S(1)}, f32[32,128]{1,0:T(8,128)S(1)}, u32[]{:S(2)}, u32[]{:S(2)}) collective-permute-start(f32[32,128]{1,0:T(8,128)S(1)} %shard_map.106.refs_3_), channel_id=1, source_target_pairs={{0,3},{1,6},{2,5},{3,0},{4,7},{5,2},{6,1},{7,4},{8,11},{9,14},{10,... | collective-permute-start | bytes 49160 | tf_op jit(solution)/shard_map/ppermute | solution.py:426
  40.9 1.4 %collective-permute-done.4.refs_4_ = f32[32,128]{1,0:T(8,128)S(1)} collective-permute-done((f32[32,128]{1,0:T(8,128)S(1)}, f32[32,128]{1,0:T(8,128)S(1)}, u32[]{:S(2)}, u32[]{:S(2)}) %collective-permute-start.4) | collective-permute-done | bytes 16416 | tf_op jit(solution)/shard_map/ppermute | solution.py:426
  42.3 11.3 %all_to_all.11.refs_0_ = bf16[32,32,128]{2,1,0:T(8,128)(2,1)S(1)} all-to-all(bf16[32,32,128]{2,1,0:T(8,128)(2,1)S(1)} %get-tuple-element.40), channel_id=1, replica_groups=mesh['row'=32,'col'=8] {'row'}, dimensions={0} | all-to-all | bytes 524288 | tf_op jit(solution)/shard_map/all_to_all | solution.py:434
  53.7 0.9 %shard_map.108 = (f32[16,64]{1,0:T(8,128)}, f32[64,256]{1,0:T(8,128)}, f32[576,64]{1,0:T(8,128)}, f32[1,64]{1,0:T(1,128)}, f32[576,64]{1,0:T(8,128)}) custom-call(bf16[32,32,128]{2,1,0:T(8,128)(2,1)S(1)} %all_to_all.11.refs_0_, f32[16,128]{1,0:T(8,128)S(1)} %get-tuple-element.41.refs_1_), custom_call_target="tpu_custom_call" | custom-call | tf_op jit(solution)/shard_map/pallas_call | solution.py:435
  (4 shorter events, 0.1 us)
Async XLA Ops:
  1.4 9.1 %collective-permute-start.1 = (bf16[80,128]{1,0:T(8,128)(2,1)S(1)}, bf16[80,128]{1,0:T(8,128)(2,1)S(1)}, u32[]{:S(2)}, u32[]{:S(2)}) collective-permute-start(bf16[80,128]{1,0:T(8,128)(2,1)S(1)} %get-tuple-element.26), channel_id=1, source_target_pairs={{0,1},{1,0},{2,3},{3,2},{4,5},{5,4},{6,7},{7,6},{8,17},{9,16},{10,... | collective-permute-start | bytes 61448 | tf_op jit(solution)/shard_map/ppermute | solution.py:380
  4.8 5.8 %collective-permute-start = (bf16[80,128]{1,0:T(8,128)(2,1)S(1)}, bf16[80,128]{1,0:T(8,128)(2,1)S(1)}, u32[]{:S(2)}, u32[]{:S(2)}) collective-permute-start(bf16[80,128]{1,0:T(8,128)(2,1)S(1)} %get-tuple-element.26), channel_id=1, source_target_pairs={{0,8},{1,10},{2,9},{3,12},{4,11},{5,14},{6,13},{7,15},{8,0},{9,2},... | collective-permute-start | bytes 61448 | tf_op jit(solution)/shard_map/ppermute | solution.py:380
  29.9 1.3 %collective-permute-start.2 = (f32[32,128]{1,0:T(8,128)S(1)}, f32[32,128]{1,0:T(8,128)S(1)}, u32[]{:S(2)}, u32[]{:S(2)}) collective-permute-start(f32[32,128]{1,0:T(8,128)S(1)} %shard_map.104.refs_0_), channel_id=1, source_target_pairs={{0,1},{1,0},{2,3},{3,2},{4,5},{5,4},{6,7},{7,6},{8,9},{9,8},{10,11... | collective-permute-start | bytes 49160 | tf_op jit(solution)/shard_map/ppermute | solution.py:420
  31.3 4.4 %collective-permute-start.3 = (f32[32,128]{1,0:T(8,128)S(1)}, f32[32,128]{1,0:T(8,128)S(1)}, u32[]{:S(2)}, u32[]{:S(2)}) collective-permute-start(f32[32,128]{1,0:T(8,128)S(1)} %shard_map.105.left_ref), channel_id=1, source_target_pairs={{0,7},{1,2},{2,1},{3,4},{4,3},{5,6},{6,5},{7,0},{8,15},{9,10},{10,... | collective-permute-start | bytes 49160 | tf_op jit(solution)/shard_map/ppermute | solution.py:424
  35.7 6.6 %collective-permute-start.4 = (f32[32,128]{1,0:T(8,128)S(1)}, f32[32,128]{1,0:T(8,128)S(1)}, u32[]{:S(2)}, u32[]{:S(2)}) collective-permute-start(f32[32,128]{1,0:T(8,128)S(1)} %shard_map.106.refs_3_), channel_id=1, source_target_pairs={{0,3},{1,6},{2,5},{3,0},{4,7},{5,2},{6,1},{7,4},{8,11},{9,14},{10,... | collective-permute-start | bytes 49160 | tf_op jit(solution)/shard_map/ppermute | solution.py:426

commit v15 on v14

--- a/solution.py
+++ b/solution.py
@@ -46,8 +46,10 @@
     return copies
 
 
-def pack_kernel(row_hbm, col_hbm, out_ref, row_ref, col_ref, sems):
-    for copy in start_copies((row_hbm, col_hbm), (row_ref, col_ref), sems):
+def pack_kernel(*refs):
+    out_ref, row_ref, col_ref = refs[6:9]
+    copies = start_copies(refs[:6], refs[7:13], refs[13])
+    for copy in copies[:2]:
         copy.wait()
     rows = row_ref[...].astype(F32)
     out_ref[:16, :] = jnp.concatenate([rows, jnp.zeros_like(rows)], axis=1).astype(BF16)
@@ -55,6 +57,8 @@
     lane = lax.broadcasted_iota(jnp.int32, (CH, LANES), 1)
     first, last = col_ref[:, :LANES].astype(F32), col_ref[:, cols - LANES :].astype(F32)
     out_ref[16:, :] = jnp.where(lane < LANES // 2, first, last).astype(BF16)
+    for copy in copies[2:]:
+        copy.wait()
 
 
 def off_edge(axis, index):
@@ -79,15 +83,12 @@
 
 
 def own_kernel(
-    n_col, one_hbm, two_hbm, bias_hbm, grad_hbm,
+    n_col, one_ref, two_ref, bias_ref, grad_ref,
     x_ref, back_ref, grad_rows_ref, grad_cols_ref, ind_ref, k1c_ref, k1ct_ref, k1f_ref, bias_col_ref,
-    rows_scr, one_ref, two_ref, bias_ref, grad_ref, sems,
+    rows_scr,
 ):
-    copies = start_copies((one_hbm, two_hbm, bias_hbm, grad_hbm), (one_ref, two_ref, bias_ref, grad_ref), sems)
     cols = grad_ref.shape[2]
     ind_ref[...] = indicator(cols, n_col)
-    for copy in copies[:3]:
-        copy.wait()
     one = [[one_ref[a, b].astype(F32) for b in range(3)] for a in range(3)]
     for k in range(3):
         rows = slice(CH * k, CH * (k + 1))
@@ -106,7 +107,6 @@
     ).astype(BF16)
     bias = jnp.concatenate([bias_ref[...], jnp.zeros((1, LANES - CH), F32)], axis=1)
     bias_col_ref[...] = jnp.broadcast_to(bias, (8, LANES)).T[:CH, :]
-    copies[3].wait()
     lane = lax.broadcasted_iota(jnp.int32, (CH, cols), 1)
     edge_lane = lax.broadcasted_iota(jnp.int32, (CH, LANES), 1)
     for piece in range(cols // LANES):
@@ -141,7 +141,7 @@
 
 
 def main_kernel(
-    n_row, n_col, row_twin_ref, col_twin_ref, row_ref, col_ref,
+    n_row, n_col, col_twin_ref, row_twin_ref, row_ref, col_ref,
     x_ref, back_ref, grad_rows_ref, grad_cols_ref, ind_ref, k1c_ref, k1ct_ref, k1f_ref, bias_ref,
     out_ref, own_ref, w_scr, chunk_scr,
 ):
@@ -357,13 +357,15 @@
         pltpu.with_memory_space_constraint(x, pltpu.HBM)
         for x in (grad_out, row_feat, col_feat.T, conv_one, conv_two, bias_one.reshape(1, CH))
     )
-    strip, *feats = pl.pallas_call(
+    given = (row_feat, col_turned, conv_one, conv_two, bias_row, grad_out)
+    strip, *feats, conv_one, conv_two, bias_row, grad_out = pl.pallas_call(
         pack_kernel,
-        out_shape=(sds((16 + CH, LANES), BF16), sds(row_feat.shape, BF16), sds(col_turned.shape, BF16)),
-        in_specs=[pl.BlockSpec(memory_space=pltpu.HBM)] * 2,
-        scratch_shapes=[pltpu.SemaphoreType.DMA((2,))],
+        out_shape=(sds((16 + CH, LANES), BF16), *(sds(x.shape, x.dtype) for x in given)),
+        in_specs=[pl.BlockSpec(memory_space=pltpu.HBM)] * 6,
+        scratch_shapes=[pltpu.SemaphoreType.DMA((6,))],
         compiler_params=PARAMS,
-    )(row_feat, col_turned)
+    )(*given)
+
 
     def twin(index, count):
         return index ^ 1
@@ -389,15 +391,7 @@
             sds((3, 2 * CH, places), BF16), sds((4 * CH, places)), sds((8, 2 * CH)), sds((CH, cols)),
             sds((32, places), BF16), square, square, square, sds((CH, 8)),
         ),
-        in_specs=[pl.BlockSpec(memory_space=pltpu.HBM)] * 4,
-        scratch_shapes=[
-            pltpu.VMEM((cols // LANES, CH * 16 + 16, LANES), F32),
-            pltpu.VMEM(conv_one.shape, BF16),
-            pltpu.VMEM(conv_two.shape, BF16),
-            pltpu.VMEM((1, CH), F32),
-            pltpu.VMEM(grad_out.shape, BF16),
-            pltpu.SemaphoreType.DMA((4,)),
-        ],
+        scratch_shapes=[pltpu.VMEM((cols // LANES, CH * 16 + 16, LANES), F32)],
         compiler_params=PARAMS,
     )(conv_one, conv_two, bias_row, grad_out)
     chunks, own = pl.pallas_call(
@@ -408,7 +402,7 @@
             pltpu.VMEM((n_row, sums_end + 8, LANES), F32),
         ],
         compiler_params=PARAMS,
-    )(row_twin, col_twin, *feats, *held)
+    )(col_twin, row_twin, *feats, *held)
     got = lax.all_to_all(chunks, "row", 0, 0)
     part = sds((sums_end + 8, LANES))
     mine = pl.pallas_call(

time: 54.8 us -> 55.2 us (level)
  starting transfers between devices: 15.2 us -> 17.6 us
  blocking collectives: 27.7 us -> 26.2 us
  Pallas kernels: 7.24 us -> 6.54 us
    ppermute x1, starting transfers between devices: 0.5 us -> 2.21 us  [shards(): paired = lax.ppermute(mine, 'col', beside)]
    all_to_all x1, blocking collectives: 16.4 us -> 14.9 us  [shards(): got = lax.all_to_all(chunks, 'row', 0, 0)]
    pallas_call x1, Pallas kernels: 2.64 us -> 1.54 us  [shards(): pl.pallas_call(lambda *refs: own_kernel(n_col, *refs), out_shape=(sds((3,...]
    ppermute x1, starting transfers between devices: 3.01 us -> 3.91 us  [shards(): side = lax.ppermute(two_sum, 'col', outside)]
  transfers between devices with their start and end apart: 5 -> 5, of which waited for: 3 -> 4; matrix products, arithmetic and copies ran while one was open for 0% -> 0% of each run, Pallas kernels for 5% -> 3%
where the time goes in v15:
time: 55.2 us; the launch traced here: 55 us
  blocking collectives  26.2 us (47%)
  starting transfers between devices  17.6 us (32%)
  Pallas kernels  6.54 us (12%)
  waiting for transfers between devices  3.96 us (7%)
  between operations  0.67 us (1%)
    all_to_all x1, blocking collectives, shards(): got = lax.all_to_all(chunks, 'row', 0, 0)  14.9 us
    all_to_all x1, blocking collectives, shards(): got = lax.all_to_all(copies, 'row', 0, 0)  11.3 us
    ppermute x2, starting transfers between devices, swap(): return lax.ppermute(strip, ('row', 'col'), pairs)  6.5 us
    ppermute x1, starting transfers between devices, shards(): last = lax.ppermute(four, 'col', across)  4.96 us
    ppermute x1, starting transfers between devices, shards(): side = lax.ppermute(two_sum, 'col', outside)  3.91 us
    pallas_call x1, Pallas kernels, shards(): pl.pallas_call(lambda *refs: main_kernel(n_row, n_col, *refs), out_shape=...  2.74 us
    ppermute x1, starting transfers between devices, shards(): paired = lax.ppermute(mine, 'col', beside)  2.21 us
    pallas_call x1, Pallas kernels, shards(): pl.pallas_call(lambda *refs: own_kernel(n_col, *refs), out_shape=(sds((3,...  1.54 us
  transfers between devices with their start and end apart: 5, of which 4 were waited for; matrix products, arithmetic and copies ran while one was open for 0% of the time, Pallas kernels for 3%

profile of v15, /device:TPU:1, one launch (start us, length us, event | category | flops | bytes accessed | tf_op | source)
XLA Modules:
  0.0 55.0 jit_solution(3599179378664712968)
XLA Ops:
  0.6 1.3 %shard_map.101 = (bf16[80,128]{1,0:T(8,128)(2,1)S(1)}, bf16[16,64]{1,0:T(8,128)(2,1)S(1)}, bf16[64,256]{1,0:T(8,128)(2,1)S(1)}, bf16[3,3,64,64]{3,2,1,0:T(8,128)...) custom-call(bf16[16,64]{1,0:T(8,128)(2,1)} %refs_0_.1, ...), custom_call_target="tpu_custom_call" | custom-call | tf_op jit(solution)/shard_map/pallas_call | solution.py:361
  1.9 3.3 %collective-permute-start = (bf16[80,128]{1,0:T(8,128)(2,1)S(1)}, bf16[80,128]{1,0:T(8,128)(2,1)S(1)}, u32[]{:S(2)}, u32[]{:S(2)}) collective-permute-start(bf16[80,128]{1,0:T(8,128)(2,1)S(1)} %get-tuple-element.30), channel_id=1, source_target_pairs={{0,1},{1,0},{2,3},{3,2},{4,5},{5,4},{6,7},{7,6},{8,17},{9,16},{10,... | collective-permute-start | bytes 61448 | tf_op jit(solution)/shard_map/ppermute | solution.py:382
  5.3 3.2 %collective-permute-start.1 = (bf16[80,128]{1,0:T(8,128)(2,1)S(1)}, bf16[80,128]{1,0:T(8,128)(2,1)S(1)}, u32[]{:S(2)}, u32[]{:S(2)}) collective-permute-start(bf16[80,128]{1,0:T(8,128)(2,1)S(1)} %get-tuple-element.30), channel_id=1, source_target_pairs={{0,8},{1,10},{2,9},{3,12},{4,11},{5,14},{6,13},{7,15},{8,0},{9,2},... | collective-permute-start | bytes 61448 | tf_op jit(solution)/shard_map/ppermute | solution.py:382
  8.4 1.5 %shard_map.102 = (bf16[3,128,2176]{2,1,0:T(8,128)(2,1)S(1)}, f32[256,2176]{1,0:T(8,128)S(1)}, f32[8,128]{1,0:T(8,128)S(1)}, f32[64,256]{1,0:T(8,128)S(1)}, bf16[...) custom-call(bf16[3,3,64,64]{3,2,1,0:T(8,128)(2,1)S(1)} %get-tuple-el, ...), custom_call_target="tpu_custom_call" | custom-call | tf_op jit(solution)/shard_map/pallas_call | solution.py:388
  10.0 0.0 collective-permute-done.refs_0_
  10.0 0.3 collective-permute-done.1.refs_1_
  10.3 2.7 %shard_map.103 = (bf16[32,32,128]{2,1,0:T(8,128)(2,1)S(1)}, f32[8,128]{1,0:T(8,128)S(1)}) custom-call(bf16[80,128]{1,0:T(8,128)(2,1)S(1)} %collective-permute-done.refs_0_, bf16[80,128]{1,0:T(8,128)(2,1)S(1)} %collective-permute-done.1.refs_1_, bf16[16,64]{1,0:T(8,128)(2,1)S(1)} %get-tuple-element.31.refs_2_, bf16[64,256]{1,0:T(8,128)(2,1)S(1)} %get-tuple-element.32.refs_3_, ...), custom_call_target="tpu_custom_call" | custom-call | tf_op jit(solution)/shard_map/pallas_call | solution.py:397
  13.0 14.9 %all_to_all.10.refs_0_ = bf16[32,32,128]{2,1,0:T(8,128)(2,1)S(1)} all-to-all(bf16[32,32,128]{2,1,0:T(8,128)(2,1)S(1)} %get-tuple-element.46), channel_id=1, replica_groups=mesh['row'=32,'col'=8] {'row'}, dimensions={0} | all-to-all | bytes 524288 | tf_op jit(solution)/shard_map/all_to_all | solution.py:406
  27.9 2.2 %collective-permute-start.2 = (f32[32,128]{1,0:T(8,128)S(1)}, f32[32,128]{1,0:T(8,128)S(1)}, u32[]{:S(2)}, u32[]{:S(2)}) collective-permute-start(f32[32,128]{1,0:T(8,128)S(1)} %shard_map.104.refs_0_), channel_id=1, source_target_pairs={{0,1},{1,0},{2,3},{3,2},{4,5},{5,4},{6,7},{7,6},{8,9},{9,8},{10,11... | collective-permute-start | bytes 49160 | tf_op jit(solution)/shard_map/ppermute | solution.py:414
  30.1 0.8 %collective-permute-done.2.refs_1_ = f32[32,128]{1,0:T(8,128)S(1)} collective-permute-done((f32[32,128]{1,0:T(8,128)S(1)}, f32[32,128]{1,0:T(8,128)S(1)}, u32[]{:S(2)}, u32[]{:S(2)}) %collective-permute-start.2) | collective-permute-done | bytes 16416 | tf_op jit(solution)/shard_map/ppermute | solution.py:414
  31.0 3.9 %collective-permute-start.3 = (f32[32,128]{1,0:T(8,128)S(1)}, f32[32,128]{1,0:T(8,128)S(1)}, u32[]{:S(2)}, u32[]{:S(2)}) collective-permute-start(f32[32,128]{1,0:T(8,128)S(1)} %shard_map.105.left_ref), channel_id=1, source_target_pairs={{0,7},{1,2},{2,1},{3,4},{4,3},{5,6},{6,5},{7,0},{8,15},{9,10},{10,... | collective-permute-start | bytes 49160 | tf_op jit(solution)/shard_map/ppermute | solution.py:418
  34.9 1.4 %collective-permute-done.3.right_ref.refs_2_ = f32[32,128]{1,0:T(8,128)S(1)} collective-permute-done((f32[32,128]{1,0:T(8,128)S(1)}, f32[32,128]{1,0:T(8,128)S(1)}, u32[]{:S(2)}, u32[]{:S(2)}) %collective-permute-start.3) | collective-permute-done | bytes 16416 | tf_op jit(solution)/shard_map/ppermute | solution.py:418
  36.3 5.0 %collective-permute-start.4 = (f32[32,128]{1,0:T(8,128)S(1)}, f32[32,128]{1,0:T(8,128)S(1)}, u32[]{:S(2)}, u32[]{:S(2)}) collective-permute-start(f32[32,128]{1,0:T(8,128)S(1)} %shard_map.106.refs_3_), channel_id=1, source_target_pairs={{0,3},{1,6},{2,5},{3,0},{4,7},{5,2},{6,1},{7,4},{8,11},{9,14},{10,... | collective-permute-start | bytes 49160 | tf_op jit(solution)/shard_map/ppermute | solution.py:420
  41.3 1.4 %collective-permute-done.4.refs_4_ = f32[32,128]{1,0:T(8,128)S(1)} collective-permute-done((f32[32,128]{1,0:T(8,128)S(1)}, f32[32,128]{1,0:T(8,128)S(1)}, u32[]{:S(2)}, u32[]{:S(2)}) %collective-permute-start.4) | collective-permute-done | bytes 16416 | tf_op jit(solution)/shard_map/ppermute | solution.py:420
  42.7 11.3 %all_to_all.11.refs_0_ = bf16[32,32,128]{2,1,0:T(8,128)(2,1)S(1)} all-to-all(bf16[32,32,128]{2,1,0:T(8,128)(2,1)S(1)} %get-tuple-element.48), channel_id=1, replica_groups=mesh['row'=32,'col'=8] {'row'}, dimensions={0} | all-to-all | bytes 524288 | tf_op jit(solution)/shard_map/all_to_all | solution.py:428
  54.1 0.9 %shard_map.108 = (f32[16,64]{1,0:T(8,128)}, f32[64,256]{1,0:T(8,128)}, f32[576,64]{1,0:T(8,128)}, f32[1,64]{1,0:T(1,128)}, f32[576,64]{1,0:T(8,128)}) custom-call(bf16[32,32,128]{2,1,0:T(8,128)(2,1)S(1)} %all_to_all.11.refs_0_, f32[16,128]{1,0:T(8,128)S(1)} %get-tuple-element.49.refs_1_), custom_call_target="tpu_custom_call" | custom-call | tf_op jit(solution)/shard_map/pallas_call | solution.py:429
  (4 shorter events, 0.1 us)
Async XLA Ops:
  1.9 8.0 %collective-permute-start = (bf16[80,128]{1,0:T(8,128)(2,1)S(1)}, bf16[80,128]{1,0:T(8,128)(2,1)S(1)}, u32[]{:S(2)}, u32[]{:S(2)}) collective-permute-start(bf16[80,128]{1,0:T(8,128)(2,1)S(1)} %get-tuple-element.30), channel_id=1, source_target_pairs={{0,1},{1,0},{2,3},{3,2},{4,5},{5,4},{6,7},{7,6},{8,17},{9,16},{10,... | collective-permute-start | bytes 61448 | tf_op jit(solution)/shard_map/ppermute | solution.py:382
  5.3 5.0 %collective-permute-start.1 = (bf16[80,128]{1,0:T(8,128)(2,1)S(1)}, bf16[80,128]{1,0:T(8,128)(2,1)S(1)}, u32[]{:S(2)}, u32[]{:S(2)}) collective-permute-start(bf16[80,128]{1,0:T(8,128)(2,1)S(1)} %get-tuple-element.30), channel_id=1, source_target_pairs={{0,8},{1,10},{2,9},{3,12},{4,11},{5,14},{6,13},{7,15},{8,0},{9,2},... | collective-permute-start | bytes 61448 | tf_op jit(solution)/shard_map/ppermute | solution.py:382
  27.9 3.0 %collective-permute-start.2 = (f32[32,128]{1,0:T(8,128)S(1)}, f32[32,128]{1,0:T(8,128)S(1)}, u32[]{:S(2)}, u32[]{:S(2)}) collective-permute-start(f32[32,128]{1,0:T(8,128)S(1)} %shard_map.104.refs_0_), channel_id=1, source_target_pairs={{0,1},{1,0},{2,3},{3,2},{4,5},{5,4},{6,7},{7,6},{8,9},{9,8},{10,11... | collective-permute-start | bytes 49160 | tf_op jit(solution)/shard_map/ppermute | solution.py:414
  31.0 5.3 %collective-permute-start.3 = (f32[32,128]{1,0:T(8,128)S(1)}, f32[32,128]{1,0:T(8,128)S(1)}, u32[]{:S(2)}, u32[]{:S(2)}) collective-permute-start(f32[32,128]{1,0:T(8,128)S(1)} %shard_map.105.left_ref), channel_id=1, source_target_pairs={{0,7},{1,2},{2,1},{3,4},{4,3},{5,6},{6,5},{7,0},{8,15},{9,10},{10,... | collective-permute-start | bytes 49160 | tf_op jit(solution)/shard_map/ppermute | solution.py:418
  36.3 6.4 %collective-permute-start.4 = (f32[32,128]{1,0:T(8,128)S(1)}, f32[32,128]{1,0:T(8,128)S(1)}, u32[]{:S(2)}, u32[]{:S(2)}) collective-permute-start(f32[32,128]{1,0:T(8,128)S(1)} %shard_map.106.refs_3_), channel_id=1, source_target_pairs={{0,3},{1,6},{2,5},{3,0},{4,7},{5,2},{6,1},{7,4},{8,11},{9,14},{10,... | collective-permute-start | bytes 49160 | tf_op jit(solution)/shard_map/ppermute | solution.py:420

commit v16 on v14

--- a/solution.py
+++ b/solution.py
@@ -141,7 +141,7 @@
 
 
 def main_kernel(
-    n_row, n_col, row_twin_ref, col_twin_ref, row_ref, col_ref,
+    n_row, n_col, col_twin_ref, row_twin_ref, row_ref, col_ref,
     x_ref, back_ref, grad_rows_ref, grad_cols_ref, ind_ref, k1c_ref, k1ct_ref, k1f_ref, bias_ref,
     out_ref, own_ref, w_scr, chunk_scr,
 ):
@@ -408,7 +408,7 @@
             pltpu.VMEM((n_row, sums_end + 8, LANES), F32),
         ],
         compiler_params=PARAMS,
-    )(row_twin, col_twin, *feats, *held)
+    )(col_twin, row_twin, *feats, *held)
     got = lax.all_to_all(chunks, "row", 0, 0)
     part = sds((sums_end + 8, LANES))
     mine = pl.pallas_call(

time: 54.8 us -> 55.9 us (1.020)
  blocking collectives: 27.7 us -> 30.6 us
  starting transfers between devices: 15.2 us -> 12.5 us
  waiting for transfers between devices: 3.69 us -> 4.72 us
    all_to_all x1, blocking collectives: 16.4 us -> 19.1 us  [shards(): got = lax.all_to_all(chunks, 'row', 0, 0)]
    ppermute x1, starting transfers between devices: 5.19 us -> 3.45 us  [shards(): last = lax.ppermute(four, 'col', across)]
    ppermute x2, starting transfers between devices: 6.5 us -> 5.48 us  [swap(): return lax.ppermute(strip, ('row', 'col'), pairs)]
where the time goes in v16:
time: 55.9 us; the launch traced here: 55.7 us
  blocking collectives  30.6 us (55%)
  starting transfers between devices  12.5 us (22%)
  Pallas kernels  7.24 us (13%)
  waiting for transfers between devices  4.72 us (8%)
  between operations  0.69 us (1%)
    all_to_all x1, blocking collectives, shards(): got = lax.all_to_all(chunks, 'row', 0, 0)  19.1 us
    all_to_all x1, blocking collectives, shards(): got = lax.all_to_all(copies, 'row', 0, 0)  11.4 us
    ppermute x2, starting transfers between devices, swap(): return lax.ppermute(strip, ('row', 'col'), pairs)  5.48 us
    ppermute x1, starting transfers between devices, shards(): last = lax.ppermute(four, 'col', across)  3.45 us
    ppermute x1, starting transfers between devices, shards(): side = lax.ppermute(two_sum, 'col', outside)  3.44 us
    pallas_call x1, Pallas kernels, shards(): pl.pallas_call(lambda *refs: main_kernel(n_row, n_col, *refs), out_shape=...  2.83 us
    pallas_call x1, Pallas kernels, shards(): pl.pallas_call(lambda *refs: own_kernel(n_col, *refs), out_shape=(sds((3,...  2.64 us
    ppermute x1, waiting for transfers between devices, shards(): last = lax.ppermute(four, 'col', across)  1.83 us
  transfers between devices with their start and end apart: 5, of which 3 were waited for; matrix products, arithmetic and copies ran while one was open for 0% of the time, Pallas kernels for 5%

profile of v16, /device:TPU:1, one launch (start us, length us, event | category | flops | bytes accessed | tf_op | source)
XLA Modules:
  0.0 55.7 jit_solution(6441234416434790687)
XLA Ops:
  0.6 0.8 %shard_map.101 = (bf16[80,128]{1,0:T(8,128)(2,1)S(1)}, bf16[16,64]{1,0:T(8,128)(2,1)S(1)}, bf16[64,256]{1,0:T(8,128)(2,1)S(1)}) custom-call(bf16[16,64]{1,0:T(8,128)(2,1)} %row_hbm.1, bf16[64,256]{1,0:T(8,128)(2,1)} %bitcast.6), custom_call_target="tpu_custom_call" | custom-call | tf_op jit(solution)/shard_map/pallas_call | solution.py:360
  1.4 5.5 %collective-permute-start.1 = (bf16[80,128]{1,0:T(8,128)(2,1)S(1)}, bf16[80,128]{1,0:T(8,128)(2,1)S(1)}, u32[]{:S(2)}, u32[]{:S(2)}) collective-permute-start(bf16[80,128]{1,0:T(8,128)(2,1)S(1)} %get-tuple-element.26), channel_id=1, source_target_pairs={{0,8},{1,10},{2,9},{3,12},{4,11},{5,14},{6,13},{7,15},{8,0},{9,2},... | collective-permute-start | bytes 61448 | tf_op jit(solution)/shard_map/ppermute | solution.py:380
  6.9 0.0 collective-permute-start
  6.9 2.6 %shard_map.102 = (bf16[3,128,2176]{2,1,0:T(8,128)(2,1)S(1)}, f32[256,2176]{1,0:T(8,128)S(1)}, f32[8,128]{1,0:T(8,128)S(1)}, f32[64,256]{1,0:T(8,128)S(1)}, bf16[...) custom-call(bf16[3,3,64,64]{3,2,1,0:T(8,128)(2,1)} %refs_0_.1, ...), custom_call_target="tpu_custom_call" | custom-call | tf_op jit(solution)/shard_map/pallas_call | solution.py:386
  9.6 0.0 collective-permute-done.1.refs_1_
  9.6 0.0 collective-permute-done.refs_0_
  9.6 2.8 %shard_map.103 = (bf16[32,32,128]{2,1,0:T(8,128)(2,1)S(1)}, f32[8,128]{1,0:T(8,128)S(1)}) custom-call(bf16[80,128]{1,0:T(8,128)(2,1)S(1)} %collective-permute-done.refs_0_, bf16[80,128]{1,0:T(8,128)(2,1)S(1)} %collective-permute-done.1.refs_1_, bf16[16,64]{1,0:T(8,128)(2,1)S(1)} %get-tuple-element.27.refs_2_, bf16[64,256]{1,0:T(8,128)(2,1)S(1)} %get-tuple-element.28.refs_3_, ...), custom_call_target="tpu_custom_call" | custom-call | tf_op jit(solution)/shard_map/pallas_call | solution.py:403
  12.4 19.1 %all_to_all.10.refs_0_ = bf16[32,32,128]{2,1,0:T(8,128)(2,1)S(1)} all-to-all(bf16[32,32,128]{2,1,0:T(8,128)(2,1)S(1)} %get-tuple-element.38), channel_id=1, replica_groups=mesh['row'=32,'col'=8] {'row'}, dimensions={0} | all-to-all | bytes 524288 | tf_op jit(solution)/shard_map/all_to_all | solution.py:412
  31.6 0.1 collective-permute-start.2
  31.7 1.2 %collective-permute-done.2.refs_1_ = f32[32,128]{1,0:T(8,128)S(1)} collective-permute-done((f32[32,128]{1,0:T(8,128)S(1)}, f32[32,128]{1,0:T(8,128)S(1)}, u32[]{:S(2)}, u32[]{:S(2)}) %collective-permute-start.2) | collective-permute-done | bytes 16416 | tf_op jit(solution)/shard_map/ppermute | solution.py:420
  32.9 3.4 %collective-permute-start.3 = (f32[32,128]{1,0:T(8,128)S(1)}, f32[32,128]{1,0:T(8,128)S(1)}, u32[]{:S(2)}, u32[]{:S(2)}) collective-permute-start(f32[32,128]{1,0:T(8,128)S(1)} %shard_map.105.left_ref), channel_id=1, source_target_pairs={{0,7},{1,2},{2,1},{3,4},{4,3},{5,6},{6,5},{7,0},{8,15},{9,10},{10,... | collective-permute-start | bytes 49160 | tf_op jit(solution)/shard_map/ppermute | solution.py:424
  36.3 1.7 %collective-permute-done.3.right_ref.refs_2_ = f32[32,128]{1,0:T(8,128)S(1)} collective-permute-done((f32[32,128]{1,0:T(8,128)S(1)}, f32[32,128]{1,0:T(8,128)S(1)}, u32[]{:S(2)}, u32[]{:S(2)}) %collective-permute-start.3) | collective-permute-done | bytes 16416 | tf_op jit(solution)/shard_map/ppermute | solution.py:424
  38.0 3.4 %collective-permute-start.4 = (f32[32,128]{1,0:T(8,128)S(1)}, f32[32,128]{1,0:T(8,128)S(1)}, u32[]{:S(2)}, u32[]{:S(2)}) collective-permute-start(f32[32,128]{1,0:T(8,128)S(1)} %shard_map.106.refs_3_), channel_id=1, source_target_pairs={{0,3},{1,6},{2,5},{3,0},{4,7},{5,2},{6,1},{7,4},{8,11},{9,14},{10,... | collective-permute-start | bytes 49160 | tf_op jit(solution)/shard_map/ppermute | solution.py:426
  41.5 1.8 %collective-permute-done.4.refs_4_ = f32[32,128]{1,0:T(8,128)S(1)} collective-permute-done((f32[32,128]{1,0:T(8,128)S(1)}, f32[32,128]{1,0:T(8,128)S(1)}, u32[]{:S(2)}, u32[]{:S(2)}) %collective-permute-start.4) | collective-permute-done | bytes 16416 | tf_op jit(solution)/shard_map/ppermute | solution.py:426
  43.3 11.4 %all_to_all.11.refs_0_ = bf16[32,32,128]{2,1,0:T(8,128)(2,1)S(1)} all-to-all(bf16[32,32,128]{2,1,0:T(8,128)(2,1)S(1)} %get-tuple-element.40), channel_id=1, replica_groups=mesh['row'=32,'col'=8] {'row'}, dimensions={0} | all-to-all | bytes 524288 | tf_op jit(solution)/shard_map/all_to_all | solution.py:434
  54.8 0.9 %shard_map.108 = (f32[16,64]{1,0:T(8,128)}, f32[64,256]{1,0:T(8,128)}, f32[576,64]{1,0:T(8,128)}, f32[1,64]{1,0:T(1,128)}, f32[576,64]{1,0:T(8,128)}) custom-call(bf16[32,32,128]{2,1,0:T(8,128)(2,1)S(1)} %all_to_all.11.refs_0_, f32[16,128]{1,0:T(8,128)S(1)} %get-tuple-element.41.refs_1_), custom_call_target="tpu_custom_call" | custom-call | tf_op jit(solution)/shard_map/pallas_call | solution.py:435
  (4 shorter events, 0.1 us)
Async XLA Ops:
  1.4 8.1 %collective-permute-start.1 = (bf16[80,128]{1,0:T(8,128)(2,1)S(1)}, bf16[80,128]{1,0:T(8,128)(2,1)S(1)}, u32[]{:S(2)}, u32[]{:S(2)}) collective-permute-start(bf16[80,128]{1,0:T(8,128)(2,1)S(1)} %get-tuple-element.26), channel_id=1, source_target_pairs={{0,8},{1,10},{2,9},{3,12},{4,11},{5,14},{6,13},{7,15},{8,0},{9,2},... | collective-permute-start | bytes 61448 | tf_op jit(solution)/shard_map/ppermute | solution.py:380
  6.9 2.7 %collective-permute-start = (bf16[80,128]{1,0:T(8,128)(2,1)S(1)}, bf16[80,128]{1,0:T(8,128)(2,1)S(1)}, u32[]{:S(2)}, u32[]{:S(2)}) collective-permute-start(bf16[80,128]{1,0:T(8,128)(2,1)S(1)} %get-tuple-element.26), channel_id=1, source_target_pairs={{0,1},{1,0},{2,3},{3,2},{4,5},{5,4},{6,7},{7,6},{8,17},{9,16},{10,... | collective-permute-start | bytes 61448 | tf_op jit(solution)/shard_map/ppermute | solution.py:380
  31.6 1.3 %collective-permute-start.2 = (f32[32,128]{1,0:T(8,128)S(1)}, f32[32,128]{1,0:T(8,128)S(1)}, u32[]{:S(2)}, u32[]{:S(2)}) collective-permute-start(f32[32,128]{1,0:T(8,128)S(1)} %shard_map.104.refs_0_), channel_id=1, source_target_pairs={{0,1},{1,0},{2,3},{3,2},{4,5},{5,4},{6,7},{7,6},{8,9},{9,8},{10,11... | collective-permute-start | bytes 49160 | tf_op jit(solution)/shard_map/ppermute | solution.py:420
  32.9 5.2 %collective-permute-start.3 = (f32[32,128]{1,0:T(8,128)S(1)}, f32[32,128]{1,0:T(8,128)S(1)}, u32[]{:S(2)}, u32[]{:S(2)}) collective-permute-start(f32[32,128]{1,0:T(8,128)S(1)} %shard_map.105.left_ref), channel_id=1, source_target_pairs={{0,7},{1,2},{2,1},{3,4},{4,3},{5,6},{6,5},{7,0},{8,15},{9,10},{10,... | collective-permute-start | bytes 49160 | tf_op jit(solution)/shard_map/ppermute | solution.py:424
  38.0 5.3 %collective-permute-start.4 = (f32[32,128]{1,0:T(8,128)S(1)}, f32[32,128]{1,0:T(8,128)S(1)}, u32[]{:S(2)}, u32[]{:S(2)}) collective-permute-start(f32[32,128]{1,0:T(8,128)S(1)} %shard_map.106.refs_3_), channel_id=1, source_target_pairs={{0,3},{1,6},{2,5},{3,0},{4,7},{5,2},{6,1},{7,4},{8,11},{9,14},{10,... | collective-permute-start | bytes 49160 | tf_op jit(solution)/shard_map/ppermute | solution.py:426
